TPU v7x, 32 devices: a whole 2x2x4 slice. The times are simulated.
32 devices in a mesh: batch: 8 (over y, x, core), seq: 4 (over z).
Axes of the slice: x: 2, y: 2, z: 4, core: 2. Of those that a mesh axis runs over, the one named last changes fastest.
Arguments:
- layer_input: bfloat16 [8, 2048, 768], P('batch', 'seq'), may hold values from -6 to 6
- segment_ids: int32 [8, 2048], P('batch', 'seq'), may hold values from 0 to 16, as said below
- w_qkv: bfloat16 [768, 2304], replicated, may hold values from -0.21875 to 0.21875
- b_query: float32 [768], replicated, may hold values from -1.8 to 1.8
- b_value: float32 [768], replicated, may hold values from -1.8 to 1.8
- w_out: bfloat16 [768, 768], replicated, may hold values from -0.875 to 0.875
- b_out: float32 [768], replicated, may hold values from -1.8 to 1.8
- ln1_gain: float32 [768], replicated, may hold values from 0.5 to 1.5
- ln1_bias: float32 [768], replicated, may hold values from -1.8 to 1.8
- w_up: bfloat16 [768, 3072], replicated, may hold values from -0.21875 to 0.21875
- b_up: float32 [3072], replicated, may hold values from -1.8 to 1.8
- w_down: bfloat16 [3072, 768], replicated, may hold values from -0.109375 to 0.109375
- b_down: float32 [768], replicated, may hold values from -1.8 to 1.8
- ln2_gain: float32 [768], replicated, may hold values from 0.5 to 1.5
- ln2_bias: float32 [768], replicated, may hold values from -1.8 to 1.8
- cotangent: bfloat16 [8, 2048, 768], P('batch', 'seq'), may hold values from -6 to 6
Outputs:
- out: bfloat16 [8, 2048, 768], P('batch', 'seq')
- d_x: float32 [8, 2048, 768], P('batch', 'seq')
- d_w_qkv: float32 [768, 2304], replicated
- d_b_query: float32 [768], replicated
- d_b_value: float32 [768], replicated
- d_w_out: float32 [768, 768], replicated
- d_b_out: float32 [768], replicated
- d_ln1_gain: float32 [768], replicated
- d_ln1_bias: float32 [768], replicated
- d_w_up: float32 [768, 3072], replicated
- d_b_up: float32 [3072], replicated
- d_w_down: float32 [3072, 768], replicated
- d_b_down: float32 [768], replicated
- d_ln2_gain: float32 [768], replicated
- d_ln2_bias: float32 [768], replicated
Inputs may be any that keep to these rules, and one draw needn't show every extreme that they name: `segment_ids`: along each stream the segment ids never fall; a document is a run of equal ids and attends only within itself. In each batch index one of its 1 streams, which one drawn, holds a document from a position below 512 to one at or past 2048 - 512.
All inputs are finite; a program needn't handle non-finite values.
Results may differ from a plain program's by a relative error of at most 0.035.
Values may be sent and summed in bfloat16 or wider, within the bound.
No kernel may reach another device: no remote copies, remote signals or barrier semaphores. Data moves between devices by JAX's collectives and lax.ppermute only.
A program may use at most 256 MiB of HBM per device.

v0:
```python
import math

import jax
import jax.numpy as jnp
from jax import lax
from jax.sharding import PartitionSpec as P

HEADS = 12


masked_score = -1e30


def layer_norm(hidden, gain, shift):
    centred = hidden - jnp.mean(hidden, axis=-1, keepdims=True)
    rstd = lax.rsqrt(jnp.mean(centred * centred, axis=-1, keepdims=True) + 1e-05)
    normed = centred * rstd
    return (normed * gain + shift, normed, rstd)


def norm_back(grad, normed, rstd, gain):
    d_gain = jnp.sum(grad * normed, axis=0)
    d_shift = jnp.sum(grad, axis=0)
    scaled = grad * gain
    d_input = rstd * (
        scaled
        - jnp.mean(scaled, axis=-1, keepdims=True)
        - normed * jnp.mean(scaled * normed, axis=-1, keepdims=True)
    )
    return (d_input, d_gain, d_shift)


def gelu_tanh(value):
    return jax.nn.gelu(value, approximate=True)


def fold_block(carry, queries, query_ids, keys, values, key_ids, scale):
    peak, total, accum = carry
    raw = jnp.einsum("bqhd,bkhd->bhqk", queries, keys, preferred_element_type=jnp.float32)
    allowed = (query_ids[:, :, None] == key_ids[:, None, :])[:, None]
    scores = jnp.where(allowed, raw * scale, masked_score)
    new_peak = jnp.maximum(peak, jnp.max(scores, axis=-1))
    weights = jnp.where(allowed, jnp.exp(scores - new_peak[..., None]), 0.0)
    factor = jnp.exp(peak - new_peak)
    total = total * factor + jnp.sum(weights, axis=-1)
    accum = accum * factor[..., None] + jnp.einsum(
        "bhqk,bkhd->bhqd", weights.astype(jnp.bfloat16), values, preferred_element_type=jnp.float32
    )
    return (new_peak, total, accum)


def fold_piece(carry, piece, queries, query_ids, scale):
    keys, values, key_ids = piece
    streams, count, width = keys.shape
    heads = queries.shape[2]
    head_dim = queries.shape[3]
    size = math.gcd(count, 512)

    def one_block(inner, index):
        begin = index * size
        key_block = lax.dynamic_slice_in_dim(keys, begin, size, 1).reshape(
            streams, size, heads, head_dim
        )
        value_block = lax.dynamic_slice_in_dim(values, begin, size, 1).reshape(
            streams, size, heads, head_dim
        )
        id_block = lax.dynamic_slice_in_dim(key_ids, begin, size, 1)
        return (
            fold_block(inner, queries, query_ids, key_block, value_block, id_block, scale),
            None,
        )

    carry, _ = lax.scan(one_block, carry, jnp.arange(count // size, dtype=jnp.int32))
    return carry


def grad_block(queries, grads_out, logsum, delta, query_ids, keys, values, key_ids, scale):
    raw = jnp.einsum("bqhd,bkhd->bhqk", queries, keys, preferred_element_type=jnp.float32)
    allowed = (query_ids[:, :, None] == key_ids[:, None, :])[:, None]
    probs = jnp.where(allowed, jnp.exp(raw * scale - logsum[..., None]), 0.0)
    d_values = jnp.einsum(
        "bhqk,bqhd->bkhd", probs.astype(jnp.bfloat16), grads_out, preferred_element_type=jnp.float32
    )
    d_probs = jnp.einsum("bqhd,bkhd->bhqk", grads_out, values, preferred_element_type=jnp.float32)
    d_scores = (probs * (d_probs - delta[..., None]) * scale).astype(jnp.bfloat16)
    d_queries = jnp.einsum("bhqk,bkhd->bqhd", d_scores, keys, preferred_element_type=jnp.float32)
    d_keys = jnp.einsum("bhqk,bqhd->bkhd", d_scores, queries, preferred_element_type=jnp.float32)
    return (d_queries, d_keys, d_values)


def per_device(
    layer_input,
    segment_ids,
    w_qkv,
    b_query,
    b_value,
    w_out,
    b_out,
    ln1_gain,
    ln1_bias,
    w_up,
    b_up,
    w_down,
    b_down,
    ln2_gain,
    ln2_bias,
    cotangent,
):
    streams, shard, width = layer_input.shape
    heads = HEADS
    head_dim = width // heads
    scale = head_dim ** (-0.5)
    rows = streams * shard
    flat_input = layer_input.reshape(rows, width)
    mixed = jnp.dot(flat_input, w_qkv, preferred_element_type=jnp.float32)
    queries = (mixed[:, :width] + b_query).astype(jnp.bfloat16)
    keys = mixed[:, width : 2 * width].astype(jnp.bfloat16)
    values = (mixed[:, 2 * width :] + b_value).astype(jnp.bfloat16)
    queries4 = queries.reshape(streams, shard, heads, head_dim)
    keys3 = keys.reshape(streams, shard, width)
    values3 = values.reshape(streams, shard, width)
    start_carry = (
        jnp.full((streams, heads, shard), masked_score, jnp.float32),
        jnp.zeros((streams, heads, shard), jnp.float32),
        jnp.zeros((streams, heads, shard, head_dim), jnp.float32),
    )
    peak, total, accum = fold_piece(
        start_carry,
        (
            lax.all_gather(keys3, "seq", axis=1, tiled=True),
            lax.all_gather(values3, "seq", axis=1, tiled=True),
            lax.all_gather(segment_ids, "seq", axis=1, tiled=True),
        ),
        queries4,
        segment_ids,
        scale,
    )
    attended = accum / total[..., None]
    logsum = peak + jnp.log(total)
    attended_low = attended.transpose(0, 2, 1, 3).reshape(rows, width).astype(jnp.bfloat16)
    first = (
        layer_input.astype(jnp.float32).reshape(rows, width)
        + jnp.dot(attended_low, w_out, preferred_element_type=jnp.float32)
        + b_out
    )
    normed_out, normed_one, rstd_one = layer_norm(first, ln1_gain, ln1_bias)
    normed_low = normed_out.astype(jnp.bfloat16)
    hidden = jnp.dot(normed_low, w_up, preferred_element_type=jnp.float32) + b_up
    activated, gelu_back = jax.vjp(gelu_tanh, hidden)
    activated_low = activated.astype(jnp.bfloat16)
    second = (
        normed_out + jnp.dot(activated_low, w_down, preferred_element_type=jnp.float32) + b_down
    )
    result, normed_two, rstd_two = layer_norm(second, ln2_gain, ln2_bias)
    grad = cotangent.astype(jnp.float32).reshape(rows, width)
    d_second, d_ln2_gain, d_ln2_bias = norm_back(grad, normed_two, rstd_two, ln2_gain)
    d_b_down = jnp.sum(d_second, axis=0)
    d_second_low = d_second.astype(jnp.bfloat16)
    d_w_down = jnp.einsum(
        "rf,rd->fd", activated_low, d_second_low, preferred_element_type=jnp.float32
    )
    (d_hidden,) = gelu_back(jnp.dot(d_second_low, w_down.T, preferred_element_type=jnp.float32))
    d_b_up = jnp.sum(d_hidden, axis=0)
    d_hidden_low = d_hidden.astype(jnp.bfloat16)
    d_w_up = jnp.einsum("rd,rf->df", normed_low, d_hidden_low, preferred_element_type=jnp.float32)
    d_normed = d_second + jnp.dot(d_hidden_low, w_up.T, preferred_element_type=jnp.float32)
    d_first, d_ln1_gain, d_ln1_bias = norm_back(d_normed, normed_one, rstd_one, ln1_gain)
    d_b_out = jnp.sum(d_first, axis=0)
    d_first_low = d_first.astype(jnp.bfloat16)
    d_w_out = jnp.einsum("rd,re->de", attended_low, d_first_low, preferred_element_type=jnp.float32)
    d_attended = jnp.dot(d_first_low, w_out.T, preferred_element_type=jnp.float32).astype(
        jnp.bfloat16
    )
    grads_out4 = d_attended.reshape(streams, shard, heads, head_dim)
    delta = jnp.sum(grads_out4.astype(jnp.float32).transpose(0, 2, 1, 3) * attended, axis=-1)
    whole_keys, whole_values, whole_ids = (
        lax.all_gather(keys3, "seq", axis=1, tiled=True),
        lax.all_gather(values3, "seq", axis=1, tiled=True),
        lax.all_gather(segment_ids, "seq", axis=1, tiled=True),
    )
    length = whole_keys.shape[1]
    size = math.gcd(length, 512)

    def key_step(carry, index):
        d_query_sum, d_key_all, d_value_all = carry
        begin = index * size
        key_block = lax.dynamic_slice_in_dim(whole_keys, begin, size, 1).reshape(
            streams, size, heads, head_dim
        )
        value_block = lax.dynamic_slice_in_dim(whole_values, begin, size, 1).reshape(
            streams, size, heads, head_dim
        )
        id_block = lax.dynamic_slice_in_dim(whole_ids, begin, size, 1)
        query_part, key_part, value_part = grad_block(
            queries4,
            grads_out4,
            logsum,
            delta,
            segment_ids,
            key_block,
            value_block,
            id_block,
            scale,
        )
        d_key_all = lax.dynamic_update_slice_in_dim(
            d_key_all, key_part.reshape(streams, size, width), begin, 1
        )
        d_value_all = lax.dynamic_update_slice_in_dim(
            d_value_all, value_part.reshape(streams, size, width), begin, 1
        )
        return ((d_query_sum + query_part, d_key_all, d_value_all), None)

    init = (
        jnp.zeros((streams, shard, heads, head_dim), jnp.float32),
        jnp.zeros((streams, length, width), jnp.float32),
        jnp.zeros((streams, length, width), jnp.float32),
    )
    (d_query4, d_key_all, d_value_all), _ = lax.scan(
        key_step, init, jnp.arange(length // size, dtype=jnp.int32)
    )
    d_keys, d_values = (
        lax.psum_scatter(
            d_key_all.astype(jnp.bfloat16), "seq", scatter_dimension=1, tiled=True
        ).astype(jnp.float32),
        lax.psum_scatter(
            d_value_all.astype(jnp.bfloat16), "seq", scatter_dimension=1, tiled=True
        ).astype(jnp.float32),
    )
    d_queries = d_query4.reshape(rows, width)
    d_keys = d_keys.reshape(rows, width)
    d_values = d_values.reshape(rows, width)
    d_b_query = jnp.sum(d_queries, axis=0)
    d_b_value = jnp.sum(d_values, axis=0)
    d_mixed_low = jnp.concatenate(
        [
            d_queries.astype(jnp.bfloat16),
            d_keys.astype(jnp.bfloat16),
            d_values.astype(jnp.bfloat16),
        ],
        axis=1,
    )
    d_w_qkv = jnp.einsum("rd,re->de", flat_input, d_mixed_low, preferred_element_type=jnp.float32)
    d_input = d_first + jnp.dot(d_mixed_low, w_qkv.T, preferred_element_type=jnp.float32)
    pieces = (
        d_w_qkv,
        d_b_query,
        d_b_value,
        d_w_out,
        d_b_out,
        d_ln1_gain,
        d_ln1_bias,
        d_w_up,
        d_b_up,
        d_w_down,
        d_b_down,
        d_ln2_gain,
        d_ln2_bias,
    )
    flat = jnp.concatenate([piece.reshape(-1) for piece in pieces])
    devices = lax.axis_size("batch") * lax.axis_size("seq")
    entries = flat.shape[0]
    share = -(-entries // devices)
    lanes = -(-share // 128) * 128
    flat = flat.reshape(devices, share)
    flat = jnp.pad(flat, ((0, 0), (0, lanes - share))).reshape(devices * lanes // 128, 128)
    shares = lax.psum_scatter(flat, ("batch", "seq"), scatter_dimension=0, tiled=True)
    gathered = lax.all_gather(
        shares.astype(jnp.bfloat16), ("batch", "seq"), axis=0, tiled=True
    ).astype(shares.dtype)
    summed = gathered.reshape(devices, lanes)[:, :share].reshape(-1)
    results = []
    offset = 0
    for piece in pieces:
        results.append(summed[offset : offset + piece.size].reshape(piece.shape))
        offset = offset + piece.size
    return (
        result.astype(jnp.bfloat16).reshape(streams, shard, width),
        d_input.reshape(streams, shard, width),
    ) + tuple(results)


def solution(mesh):
    return jax.shard_map(
        per_device,
        mesh=mesh,
        in_specs=(
            P("batch", "seq", None),
            P("batch", "seq"),
            P(),
            P(),
            P(),
            P(),
            P(),
            P(),
            P(),
            P(),
            P(),
            P(),
            P(),
            P(),
            P(),
            P("batch", "seq", None),
        ),
        out_specs=(
            P("batch", "seq", None),
            P("batch", "seq", None),
            P(),
            P(),
            P(),
            P(),
            P(),
            P(),
            P(),
            P(),
            P(),
            P(),
            P(),
            P(),
            P(),
        ),
        check_vma=False,
    )
```

profile of v0, /device:TPU:0, one launch (start us, length us, event | category | flops | bytes accessed | tf_op | source)
XLA Modules:
  0.0 1758.1 jit_solution(8090221197547360769)
XLA Ops:
  21.3 13.7 all_gather.15
  35.0 46.9 %all-gather.7.cloned.1.call-done = bf16[2048,768]{1,0:T(8,128)(2,1)} async-done(((bf16[512,768]{1,0:T(8,128)(2,1)}), bf16[2048,768]{1,0:T(8,128)(2,1)}) %all-gather.7.cloned.1.call-update) | async-done | bytes 3145744 | tf_op jit(solution)/shard_map/all_gather | solution.py:130
  86.6 59.7 %all-gather.9.cloned.1.call-done = bf16[2048,768]{1,0:T(8,128)(2,1)} async-done(((bf16[512,768]{1,0:T(8,128)(2,1)}), bf16[2048,768]{1,0:T(8,128)(2,1)}) %all-gather.9.cloned.1.call-update) | async-done | bytes 3145744 | tf_op jit(solution)/shard_map/all_gather | solution.py:131
  151.6 108.5 %while.30 = (s32[]{:T(128)}, f32[1,12,512]{2,1,0:T(8,128)}, f32[1,12,512]{2,1,0:T(8,128)}, f32[1,12,512,64]{2,3,1,0:T(8,128)}, s32[1,512]{1,0:T(1,128)S(1)}, /*i...) while((s32[]{:T(128)}, f32[1,12,512]{2,1,0:T(8,128)}, ...), condition=%wide.region_3.4_spmd.clone, body=%wide.region_0.3_spmd.clone.sunk | while | flops 847679488 | bytes 103719328 | solution.py:73
  164.2 8.0 fusion.126
  191.1 8.0 fusion.126
  218.1 8.0 fusion.126
  237.2 7.2 fusion.124
  245.2 8.0 fusion.126
  301.8 130.2 %while.31 = (s32[]{:T(128)}, f32[1,512,12,64]{1,3,2,0:T(8,128)}, bf16[1,2048,768]{1,2,0:T(8,128)(2,1)}, bf16[1,2048,768]{1,2,0:T(8,128)(2,1)}, s32[4]{0:T(128)},...) while((s32[]{:T(128)}, f32[1,512,12,64]{1,3,2,0:T(8,128)}, ...), condition=%wide.region_14.15_spmd.clone, body=%wide.region_13.14_spmd.clone.sunk | while | flops 2048917504 | bytes 158188112 | solution.py:218
  456.4 10.4 fusion.63
  466.8 10.8 reshape.356
  477.7 13.4 reduce-scatter.7.cloned.1.call-done
  491.1 62.5 %reduce-scatter.5.cloned.1.call-done = bf16[1,512,768]{1,2,0:T(8,128)(2,1)} async-done(((bf16[1,2048,768]{1,2,0:T(8,128)(2,1)}), bf16[1,512,768]{1,2,0:T(8,128)(2,1)}) %reduce-scatter.5.cloned.1.call-update) | async-done | bytes 786448 | tf_op jit(solution)/shard_map/reduce_scatter | solution.py:222
  560.4 8.0 copy.67
  568.3 7.9 reshape.353
  584.2 21.3 %dynamic-update-slice.3 = f32[7087104]{0:T(1024)} dynamic-update-slice(f32[7087104]{0:T(1024)} %constant_dynamic-update-slice_fusion.7, f32[589824]{0:T(1024)} %reshape.354, s32[]{} %constant.80) | dynamic-update-slice | bytes 4718596
  609.4 80.3 %dynamic-update-slice.7 = f32[7087104]{0:T(1024)} dynamic-update-slice(f32[7087104]{0:T(1024)} %constant_dynamic-update-slice_fusion.4, f32[2359296]{0:T(1024)} %bitcast.241, s32[]{} %constant.84) | dynamic-update-slice | bytes 18874372
  691.1 80.5 %dynamic-update-slice.9 = f32[7087104]{0:T(1024)} dynamic-update-slice(f32[7087104]{0:T(1024)} %constant_dynamic-update-slice_fusion.3, f32[2359296]{0:T(1024)} %reshape.356, s32[]{} %constant.86) | dynamic-update-slice | bytes 18874372
  775.5 37.8 %reshape.357 = f32[32,221472]{1,0:T(8,128)} reshape(f32[7087104]{0:T(1024)} %constant_dynamic-update-slice_fusion) | data formatting | bytes 56696832 | tf_op jit(solution)/shard_map/reshape | solution.py:264
  813.3 20.9 %pad.4 = f32[32,221568]{1,0:T(8,128)} pad(f32[32,221472]{1,0:T(8,128)} %reshape.357, f32[]{:T(128)} %constant.60.clone.1), padding=0_0x0_96 | pad | bytes 56709124 | tf_op jit(solution)/shard_map/jit(_pad)/pad | solution.py:265
  834.2 25.4 %reshape.358 = f32[55392,128]{1,0:T(8,128)} reshape(f32[32,221568]{1,0:T(8,128)} %pad.4) | data formatting | bytes 56721408 | tf_op jit(solution)/shard_map/reshape | solution.py:265
  859.6 606.0 %fusion = f32[1744,128]{1,0:T(8,128)} fusion(f32[55392,128]{1,0:T(8,128)} %reshape.358), kind=kCustom, calls=%all-reduce-scatter | all-reduce-scatter fusion | flops 7143425 | bytes 29253632
  1483.1 108.1 %all-gather.11.cloned.1.call-done = bf16[32,1731,128]{2,1,0:T(8,128)(2,1)} async-done(((bf16[1,1731,128]{2,1,0:T(8,128)(2,1)}), bf16[32,1731,128]{2,1,0:T(8,128)(2,1)}) %all-gather.11.cloned.1.call-update) | async-done | bytes 14180368 | tf_op jit(solution)/shard_map/all_gather | solution.py:267
  1591.2 12.8 copy.75
  1604.0 10.0 slice_convert_fusion
  1613.9 36.6 %reshape.377 = f32[7087104]{0:T(1024)} reshape(f32[32,221472]{1,0:T(8,128)} %slice_convert_fusion) | data formatting | bytes 56696832
  1650.5 30.0 %slice.67 = f32[3076,2304]{1,0:T(8,128)} reshape(f32[7087104]{0:T(1024)} %reshape.377) | data formatting | bytes 56696832 | tf_op jit(solution)/shard_map/slice | solution.py:274
  1681.9 31.3 %slice.71 = f32[9228,768]{1,0:T(8,128)} reshape(f32[7087104]{0:T(1024)} %reshape.377) | data formatting | bytes 56696832 | tf_op jit(solution)/shard_map/slice | solution.py:274
  1713.2 8.3 slice.93
  1726.1 8.0 slice.95
  1740.5 10.9 reshape.361
  (383 shorter events, 336.2 us)
Async XLA Ops:
  7.2 8.4 copy-start.36
  7.2 8.4 copy-start.37
  7.2 74.7 %all-gather.7.cloned.1.call-start = ((), (), s32[]{:S(2)}) async-start(), calls=%async_computation.4 | async-start | bytes 3932160 | tf_op jit(solution)/shard_map/all_gather | solution.py:130
  15.5 130.8 %all-gather.9.cloned.1.call-start = ((), (), s32[]{:S(2)}) async-start(), calls=%async_computation.5 | async-start | bytes 3932160 | tf_op jit(solution)/shard_map/all_gather | solution.py:131
  18.9 472.2 %reduce-scatter.7.cloned.1.call-start = ((), (), s32[]{:S(2)}) async-start(), calls=%async_computation.3 | async-start | bytes 3932160 | tf_op jit(solution)/shard_map/reduce_scatter | solution.py:225
  151.6 111.0 %copy-start.46 = (f32[768]{0:T(1024)S(1)}, f32[768]{0:T(1024)}, u32[]{:S(2)}) copy-start(f32[768]{0:T(1024)} %param.26) | copy-start | bytes 9220
  153.7 9.7 copy-start.6
  164.2 8.1 copy-start.13
  164.2 8.7 copy-start.1
  164.2 8.7 copy-start.7
  180.6 9.7 copy-start.6
  191.0 8.7 copy-start.1
  191.0 8.7 copy-start.7
  207.6 9.7 copy-start.6
  218.1 8.7 copy-start.1
  218.1 8.7 copy-start.7
  234.7 9.7 copy-start.6
  245.2 8.7 copy-start.1
  245.2 8.7 copy-start.7
  265.7 22.6 %copy-start.11 = (f32[512,768]{1,0:T(8,128)}, f32[512,768]{1,0:T(8,128)S(1)}, u32[]{:S(2)}) copy-start(f32[512,768]{1,0:T(8,128)S(1)} %get-tuple-element.367) | copy-start | bytes 4718596
  266.1 22.2 %copy-start.34 = (f32[512]{0:T(512)}, f32[512]{0:T(512)S(1)}, u32[]{:S(2)}) copy-start(f32[512]{0:T(512)S(1)} %add_rsqrt_fusion.1) | copy-start | bytes 6148
  319.0 11.7 slice-start
  351.2 12.1 slice-start
  383.9 12.1 slice-start
  416.4 12.1 slice-start
  432.0 121.5 %reduce-scatter.5.cloned.1.call-start = ((), (), s32[]{:S(2)}) async-start(), calls=%async_computation.2 | async-start | bytes 3932160 | tf_op jit(solution)/shard_map/reduce_scatter | solution.py:222
  432.6 1158.6 %all-gather.11.cloned.1.call-start = ((), (), s32[]{:S(2)}) async-start(), calls=%async_computation.6 | async-start | bytes 14665728 | tf_op jit(solution)/shard_map/all_gather | solution.py:267
  581.4 24.1 %copy-start.30 = (f32[768]{0:T(1024)S(1)}, f32[768]{0:T(1024)}, u32[]{:S(2)}) copy-start(f32[768]{0:T(1024)} %get-tuple-element.345) | copy-start | bytes 9220
  581.4 26.7 %copy-start.40 = (f32[768]{0:T(1024)S(1)}, f32[768]{0:T(1024)}, u32[]{:S(2)}) copy-start(f32[768]{0:T(1024)} %get-tuple-element.293) | copy-start | bytes 9220
  691.1 80.5 %copy-start.33 = (f32[768]{0:T(1024)S(1)}, f32[768]{0:T(1024)}, u32[]{:S(2)}) copy-start(f32[768]{0:T(1024)} %get-tuple-element.343) | copy-start | bytes 9220
  691.1 81.8 %copy-start.29 = (f32[768]{0:T(1024)S(1)}, f32[768]{0:T(1024)}, u32[]{:S(2)}) copy-start(f32[768]{0:T(1024)} %get-tuple-element.290) | copy-start | bytes 9220
  1467.2 3.9 collective-permute-start
  (86 other events, 472.8 us)
Sparse Core Ops, SparseCore 0:
  15.6 66.2 all-gather.6
  84.1 62.1 all-gather.8
  432.1 58.8 reduce-scatter.6
  493.3 60.2 reduce-scatter.4
  1477.9 113.1 all-gather.10
where the time goes:
time: 1780 us; the launch traced here: 1760 us
  blocking collectives  620 us (35%)
  local copies, waits for them, and re-layouts  555 us (31%)
  waiting for transfers between devices  293 us (16%)
  matrix products  202 us (11%)
  other arithmetic  64.6 us (4%)
    unnamed x1, blocking collectives  606 us
    unnamed x92, local copies, waits for them, and re-layouts  277 us
    all_gather x1, waiting for transfers between devices, per_device(): lax.all_gather(shares.astype(jnp.bfloat16), ('batch', 'seq'), axis=0, til...  108 us
    slice x8, local copies, waits for them, and re-layouts, per_device(): results.append(summed[offset:offset + piece.size].reshape(piece.shape))  90 us
    reduce_scatter x1, waiting for transfers between devices, per_device(): lax.psum_scatter(d_key_all.astype(jnp.bfloat16), 'seq', scatter_dimension...  62.5 us
    all_gather x1, waiting for transfers between devices, per_device(): lax.all_gather(values3, 'seq', axis=1, tiled=True)  59.7 us
    all_gather x1, waiting for transfers between devices, per_device(): lax.all_gather(keys3, 'seq', axis=1, tiled=True)  46.9 us
    reshape x1, local copies, waits for them, and re-layouts, per_device(): flat = flat.reshape(devices, share)  37.8 us
  transfers between devices with their start and end apart: 6, of which 6 were waited for; matrix products, arithmetic and copies ran while one was open for 3% of the time, Pallas kernels for 0%

commit v1 on v0

v1 whole, which is shorter than its diff:
```python
import functools
import math

import jax
import jax.numpy as jnp
from jax import lax
from jax.experimental import pallas as pl
from jax.experimental.pallas import tpu as pltpu
from jax.sharding import PartitionSpec as P

HEADS = 12
LANES = 128
MASK = 1e30
BF = jnp.bfloat16
F32 = jnp.float32
VMEM = 56 * 2**20
EXTRA = 128


def dot(left, right, contract=((1,), (0,))):
    return lax.dot_general(left, right, (contract, ((), ())), preferred_element_type=F32)


def stages_of(axis):
    return [(axis, bit) for bit in range(int(math.log2(lax.axis_size(axis))))]


def bit_of(stage):
    index = lax.axis_index(stage[0])
    if len(stage) == 2:
        return (index >> stage[1]) & 1
    return jnp.where(index % 2 == 0, index >> stage[1], index >> stage[2]) & 1


def swap(value, stage):
    count = lax.axis_size(stage[0])
    bits = stage[1:] * 2
    return lax.ppermute(value, stage[0], [(i, i ^ (1 << bits[i % 2])) for i in range(count)])


ANYWHERE = pl.BlockSpec(memory_space=pl.ANY)


def together(values, late=()):
    if len(values) + len(late) < 2:
        return list(values)
    return pl.pallas_call(
        lambda *refs: None,
        in_specs=[ANYWHERE] * (len(values) + len(late)),
        out_specs=[ANYWHERE] * len(values),
        out_shape=[jax.ShapeDtypeStruct(v.shape, v.dtype) for v in values],
        input_output_aliases={i: i for i in range(len(values))},
        name="together",
    )(*values, *late)


def part_of(terms, index, parts):
    rows = terms[0].shape[0] // parts
    total = lax.dynamic_slice_in_dim(terms[0], index * rows, rows, 0)
    if len(terms) == 1:
        return total
    total = total.astype(F32)
    for term in terms[1:]:
        total = total + lax.dynamic_slice_in_dim(term, index * rows, rows, 0).astype(F32)
    return total.astype(BF)


def rest_of(terms, stage, came):
    mine = bit_of(stage)
    rows = terms[0].shape[0] // 2
    return [lax.dynamic_slice_in_dim(t, mine * rows, rows, 0) for t in terms] + [came]


def split(value):
    half = value.shape[0] // 2
    return value[:half], value[half:]


def total_of(terms):
    total = terms[0].astype(F32)
    for term in terms[1:]:
        total = total + term.astype(F32)
    return total.astype(BF)


def joined(mine, other, stage):
    return jnp.where(
        bit_of(stage) == 0,
        jnp.concatenate([mine, other], axis=0),
        jnp.concatenate([other, mine], axis=0),
    )


def sum_everywhere(terms):
    core, chips = stages_of("batch")[0], stages_of("batch")[1:]
    plane = [(axis, one, two) for (axis, one), (_, two) in zip(chips, chips[::-1])]
    order = plane + stages_of("seq")
    for stage in order:
        came, _ = yield part_of(terms, 1 - bit_of(stage), 2), stage
        terms = rest_of(terms, stage, came)
    value = total_of(terms)
    for stage in order[::-1]:
        came, value = yield value, stage
        value = joined(value, came, stage)
    came, value = yield value, core
    return value, came


def line_scatter(sent):
    stages = stages_of("seq")
    came, kept = yield sent, stages[0]
    for axis, bit in stages[1:]:
        value = kept + came.astype(F32)
        mine = (lax.axis_index(axis) >> bit) & 1
        pairs = value.reshape(value.shape[0] // 2, 2, *value.shape[1:])
        sent = lax.dynamic_index_in_dim(pairs, 1 - mine, 1, keepdims=False).astype(BF)
        kept = lax.dynamic_index_in_dim(pairs, mine, 1, keepdims=False)
        if bit + 1 < len(stages):
            came, _ = yield sent, (axis, bit)
    parts = []
    for part in split(sent[0]):
        parts.append((yield part, stages[-1])[0])
    return kept[0] + jnp.concatenate(parts, axis=0).astype(F32)


class Exchanges:
    def __init__(self):
        self.chains, self.came, self.sent, self.results = {}, {}, {}, {}

    def add(self, name, chain):
        self.chains[name] = chain

    def go(self, names, late=(), kept=None, land=()):
        names = [n for n in names if n not in self.results]
        waiting = [n for n in names if n in self.came]
        landing = waiting + list(land)
        if landing:
            self.came.update(zip(landing, together([self.came[n] for n in landing], late)))
        next_sent, stages = {}, {}
        for name in names:
            try:
                if name not in waiting:
                    next_sent[name], stages[name] = next(self.chains[name])
                    continue
                back = self.sent[name]
                if name == "input" and kept is not None:
                    back = kept
                next_sent[name], stages[name] = self.chains[name].send((self.came[name], back))
            except StopIteration as stop:
                self.results[name] = stop.value
        next_sent = dict(zip(next_sent, together(list(next_sent.values()))))
        for name, value in next_sent.items():
            self.sent[name], self.came[name] = value, swap(value, stages[name])
        return list(next_sent.values())


def line_steps(block):
    count = lax.axis_size("seq")
    pairs = [
        [(i, i ^ 1) for i in range(count)],
        [(i, ((i + 1) ^ 1) - 1) for i in range(1, count - 1)],
    ]
    one = two = block
    for k in range(1, count):
        one, two = lax.ppermute(two, "seq", pairs[0]), lax.ppermute(one, "seq", pairs[1])
        late = yield
        one, two = together([one, two], late)
        yield one, two


def whole_spec(shape):
    return pl.BlockSpec(shape, lambda *_: (0,) * len(shape))


def params(flops, nbytes):
    return dict(
        compiler_params=pltpu.CompilerParams(vmem_limit_bytes=VMEM),
        cost_estimate=pl.CostEstimate(flops=flops, bytes_accessed=nbytes, transcendentals=0),
    )


def hot(ids_row, same, other):
    spread = jnp.broadcast_to(ids_row.astype(F32), (LANES, ids_row.shape[1]))
    lanes = lax.broadcasted_iota(jnp.int32, spread.shape, 0).astype(F32)
    return jnp.transpose(jnp.where(spread == lanes, same, other)).astype(BF)


def project_kernel(first, rows, place_ref, *refs):
    refs = list(refs)
    blocks = [refs.pop(0) for _ in range(1 if first else 2)]
    w_refs = [refs.pop(0) for _ in range(3 if first else 2)]
    b_refs = [refs.pop(0) for _ in range(3 if first else 2)]
    refs = refs if first else refs[2:]
    whole_ref, kv_ref = refs.pop(0), refs.pop(0)
    if first:
        q_ref, qh_ref = refs.pop(0), refs.pop(0)
    token_ref, key_hot, mixed, sems = refs
    token_ref[...] = jnp.zeros_like(token_ref)
    width = blocks[0].shape[1]
    step = pl.program_id(0)
    last = pl.num_programs(0) - 1
    lanes = mixed.shape[-1]

    def valid(b):
        return place_ref[2 + b] == 1

    def block_copies(b):
        at = pl.ds(place_ref[b] * rows, rows)
        return [
            pltpu.make_async_copy(blocks[b].at[pl.ds(0, rows)], whole_ref.at[at], sems.at[b, 0]),
            pltpu.make_async_copy(
                key_hot.at[b], kv_ref.at[at, pl.ds(2 * width, LANES)], sems.at[b, 1]
            ),
        ]

    def step_copies(b, at_step):
        at = pl.ds(place_ref[b] * rows, rows)
        begin = pl.multiple_of(at_step * lanes, LANES)
        return [
            pltpu.make_async_copy(
                mixed.at[b, i, at_step], kv_ref.at[at, pl.ds(i * width + begin, lanes)],
                sems.at[b, 2 + i],
            )
            for i in range(2)
        ]

    for b in range(len(blocks)):

        @pl.when(jnp.logical_and(step == 0, valid(b)))
        def _():
            ids = blocks[b][rows : rows + 16, :rows][0:1]
            key_hot[b] = hot(ids, 0.0, 1.0)
            if first:
                qh_ref[...] = hot(ids, -MASK, 0.0)
            for copy in block_copies(b):
                copy.start()

        @pl.when(valid(b))
        def _():
            block = blocks[b][:rows]
            for i in range(2):
                mixed[b, i, step] = (dot(block, w_refs[i][...]) + b_refs[i][...]).astype(BF)
            if first:
                q_ref[...] = (dot(block, w_refs[2][...]) + b_refs[2][...]).astype(BF)

        @pl.when(jnp.logical_and(step > 0, valid(b)))
        def _():
            for copy in step_copies(b, step - 1):
                copy.wait()

        @pl.when(valid(b))
        def _():
            for copy in step_copies(b, step):
                copy.start()

        @pl.when(jnp.logical_and(step == last, valid(b)))
        def _():
            for copy in step_copies(b, step) + block_copies(b):
                copy.wait()


def project(first, place, blocks, w_qkv, bias, state, length):
    width = w_qkv.shape[0]
    rows = blocks[0].shape[0] - 16
    lanes = 2 * LANES
    steps = width // lanes
    full = whole_spec

    def columns(count, which):
        return pl.BlockSpec((count, lanes), lambda p, *_: (0, which * steps + p))

    parts = (1, 2, 0) if first else (1, 2)
    in_specs = [full(blocks[0].shape)] * len(blocks)
    in_specs += [columns(width, i) for i in parts] + [columns(1, i) for i in parts]
    operands = [*blocks] + [w_qkv] * len(parts) + [bias] * len(parts)
    out_specs = [ANYWHERE, ANYWHERE]
    out_shape = [
        jax.ShapeDtypeStruct((length, width), BF),
        jax.ShapeDtypeStruct((length, 2 * width + LANES), BF),
    ]
    aliases = {}
    if first:
        out_specs += [pl.BlockSpec((rows, lanes), lambda p, *_: (0, p)), full((rows, LANES))]
        out_shape += [
            jax.ShapeDtypeStruct((rows, width), BF),
            jax.ShapeDtypeStruct((rows, LANES), BF),
        ]
    else:
        in_specs += [ANYWHERE, ANYWHERE]
        operands += state
        aliases = {len(operands) - 1: 0, len(operands): 1}
    out_specs.append(full((8, LANES)))
    out_shape.append(jax.ShapeDtypeStruct((8, LANES), F32))
    return pl.pallas_call(
        functools.partial(project_kernel, first, rows),
        grid_spec=pltpu.PrefetchScalarGridSpec(
            num_scalar_prefetch=1,
            grid=(steps,),
            in_specs=in_specs,
            out_specs=out_specs,
            scratch_shapes=[
                pltpu.VMEM((len(blocks), rows, LANES), BF),
                pltpu.VMEM((len(blocks), 2, steps, rows, lanes), BF),
                pltpu.SemaphoreType.DMA((len(blocks), 4)),
            ],
        ),
        out_shape=out_shape,
        input_output_aliases=aliases,
        name="project",
        **params(2 * len(blocks) * rows * width * width, 8 * rows * width),
    )(place, *operands)


def attend_kernel(scale, tile, q_ref, k_ref, v_ref, qh_ref, kh_ref, o_ref, low_ref, lse_ref):
    half = LANES // 2
    lane = lax.broadcasted_iota(jnp.int32, (1, LANES), 1)
    lower = lane < half
    factor = scale * math.log2(math.e)
    jobs = [(t, h) for t in range(q_ref.shape[0] // tile) for h in range(2)]

    def scores_of(t, h):
        at = slice(t * tile, (t + 1) * tile)
        query = q_ref[at]
        query = jnp.where(lane // half == h, query, jnp.zeros_like(query))
        query = jnp.concatenate([query, qh_ref[at]], axis=1)
        return dot(query, jnp.concatenate([k_ref[...], kh_ref[...]], axis=1), ((1,), (1,)))

    ready = scores_of(*jobs[0])
    before = None
    for i, (t, h) in enumerate(jobs):
        scores = ready
        if i + 1 < len(jobs):
            ready = scores_of(*jobs[i + 1])
        peak = jnp.max(scores, axis=1, keepdims=True)
        weights = jnp.exp2((scores - peak) * factor).astype(BF)
        value = v_ref[...]
        both = dot(weights, jnp.concatenate([value, jnp.ones_like(value)], axis=1))
        total = both[:, LANES:]
        now = both[:, :LANES] / total, peak * factor + jnp.log2(total)
        if h == 0:
            before = now
            continue
        at = slice(t * tile, (t + 1) * tile)
        out = jnp.where(lower, before[0], now[0])
        o_ref[at] = out
        low_ref[at] = out.astype(BF)
        turned = jnp.transpose(jnp.where(lower, before[1], now[1]))
        lse_ref[0, :, at] = jnp.concatenate([turned[0:4], turned[half : half + 4]], axis=0)


def attend(queries, keys_values, query_hot, scale):
    rows, width = queries.shape
    length = keys_values.shape[0]
    pairs = width // LANES
    by_pair = pl.BlockSpec((rows, LANES), lambda p: (0, p))
    return pl.pallas_call(
        functools.partial(attend_kernel, scale, 256),
        grid=(pairs,),
        in_specs=[
            by_pair,
            pl.BlockSpec((length, LANES), lambda p: (0, p)),
            pl.BlockSpec((length, LANES), lambda p: (0, pairs + p)),
            pl.BlockSpec((rows, LANES), lambda p: (0, 0)),
            pl.BlockSpec((length, LANES), lambda p: (0, 2 * pairs)),
        ],
        out_specs=[by_pair, by_pair, pl.BlockSpec((1, 8, rows), lambda p: (p, 0, 0))],
        out_shape=[
            jax.ShapeDtypeStruct((rows, width), F32),
            jax.ShapeDtypeStruct((rows, width), BF),
            jax.ShapeDtypeStruct((pairs, 8, rows), F32),
        ],
        name="attend",
        **params(4 * rows * length * width, 8 * length * width),
    )(queries, keys_values, keys_values, query_hot, keys_values)


def attend_back_kernel(
    final, scale, pairs, skip, at_ref, q_ref, k_ref, v_ref, qh_ref, kh_ref, do_ref, o_ref,
    lse_ref, *refs,
):
    refs = list(refs)
    if final:
        dq_in, sums_in = refs.pop(0), refs.pop(0)
    dq_ref, sums_ref, dk_ref, dv_ref, token_ref, dq_acc, delta_acc, sv_acc = refs[skip:]
    step = pl.program_id(1)
    half = LANES // 2
    lane = lax.broadcasted_iota(jnp.int32, (1, LANES), 1)
    factor = scale * math.log2(math.e)
    token_ref[...] = jnp.zeros_like(token_ref)

    @pl.when(step == 0)
    def _():
        if final:
            dq_acc[...] = dq_in[...]
            sv_acc[...] = sums_in[...]
        else:
            dq_acc[...] = jnp.zeros_like(dq_acc)
            sv_acc[...] = jnp.zeros_like(sv_acc)
        for p in range(pairs):
            at = slice(p * LANES, (p + 1) * LANES)
            both = jnp.transpose(do_ref[:, at].astype(F32) * o_ref[:, at])
            delta_acc[p, 0:1] = jnp.sum(both[:half], axis=0, keepdims=True)
            delta_acc[p, 1:2] = jnp.sum(both[half:], axis=0, keepdims=True)

    jobs = [(p, h) for p in range(pairs) for h in range(2)]

    def products(p, h):
        at = slice(p * LANES, (p + 1) * LANES)
        own = lane // half == h
        query, d_out = q_ref[:, at], do_ref[:, at]
        query = jnp.where(own, query, jnp.zeros_like(query))
        d_out = jnp.where(own, d_out, jnp.zeros_like(d_out))
        keys = jnp.concatenate([k_ref[:, at], kh_ref[...]], axis=1)
        scores = dot(keys, jnp.concatenate([query, qh_ref[...]], axis=1), ((1,), (1,)))
        return scores, dot(v_ref[:, at], d_out, ((1,), (1,))), query, d_out

    ready = products(*jobs[0])
    d_key = d_value = d_query = None
    for i, (p, h) in enumerate(jobs):
        scores, d_probs, query, d_out = ready
        if i + 1 < len(jobs):
            ready = products(*jobs[i + 1])
        at = slice(p * LANES, (p + 1) * LANES)
        probs = jnp.exp2(scores * factor - lse_ref[p, 4 * h : 4 * h + 1, :])
        d_scores = (probs * (d_probs - delta_acc[p, h : h + 1, :])).astype(BF)
        key = k_ref[:, at]
        key = jnp.where(lane // half == h, key, jnp.zeros_like(key))
        terms = (
            dot(probs.astype(BF), d_out),
            dot(d_scores, query),
            dot(d_scores, key, ((0,), (0,))),
        )
        if h == 0:
            d_value, d_key, d_query = terms
            continue
        d_value, d_key, d_query = d_value + terms[0], d_key + terms[1], d_query + terms[2]
        dk_ref[:, at] = (d_key * scale).astype(BF)
        dv_ref[:, at] = d_value.astype(BF)
        sv_acc[1:2, at] += jnp.sum(d_value, axis=0, keepdims=True)
        dq_acc[:, at] += d_query

    @pl.when(step == pl.num_programs(1) - 1)
    def _():
        if final:
            whole = dq_acc[...] * scale
            dq_ref[...] = whole.astype(BF)
            sv_acc[0:1] = jnp.sum(whole, axis=0, keepdims=True)
        else:
            dq_ref[...] = dq_acc[...]
        sums_ref[...] = sv_acc[...]


def parity_block(final, i, at):
    return 2 * i + (at[0] if final else 1 - at[0])


def attend_back(
    final, parts, at, deps, before, partial, queries, keys_values, query_hot, d_out, out,
    logsum, scale,
):
    rows, width = queries.shape
    length = keys_values.shape[0]
    lanes = width // parts
    pairs = lanes // LANES
    per_query = pl.BlockSpec((rows, lanes), lambda part, t, at: (0, part))
    per_key = pl.BlockSpec((rows, lanes), lambda part, t, at: (parity_block(final, t, at), part))
    sums = pl.BlockSpec((8, lanes), lambda part, t, at: (0, part))
    operands = [queries, keys_values, keys_values, query_hot, keys_values, d_out, out, logsum]
    operands += partial
    return pl.pallas_call(
        functools.partial(attend_back_kernel, final, scale, pairs, len(deps) + len(before)),
        grid_spec=pltpu.PrefetchScalarGridSpec(
            num_scalar_prefetch=1,
            grid=(parts, length // rows // 2),
            in_specs=[
                per_query,
                per_key,
                pl.BlockSpec(
                    (rows, lanes), lambda part, t, at: (parity_block(final, t, at), parts + part)
                ),
                pl.BlockSpec((rows, LANES), lambda part, t, at: (0, 0)),
                pl.BlockSpec(
                    (rows, LANES),
                    lambda part, t, at: (parity_block(final, t, at), 2 * width // LANES),
                ),
                per_query,
                per_query,
                pl.BlockSpec((pairs, 8, rows), lambda part, t, at: (part, 0, 0)),
            ]
            + [per_query, sums][: len(partial)]
            + [ANYWHERE] * (len(before) + len(deps)),
            out_specs=[per_query, sums, per_key, per_key, whole_spec((8, LANES))],
            scratch_shapes=[
                pltpu.VMEM((rows, lanes), F32),
                pltpu.VMEM((pairs, 8, rows), F32),
                pltpu.VMEM((8, lanes), F32),
            ],
        ),
        out_shape=[
            jax.ShapeDtypeStruct((rows, width), BF if final else F32),
            jax.ShapeDtypeStruct((8, width), F32),
            jax.ShapeDtypeStruct((length, width), BF),
            jax.ShapeDtypeStruct((length, width), BF),
            jax.ShapeDtypeStruct((8, LANES), F32),
        ],
        input_output_aliases={
            1 + len(operands) + i: 4 - len(before) + i for i in range(len(before))
        },
        name="attend_back",
        **params(10 * rows * length * width, 8 * length * width),
    )(at, *operands, *before, *deps)


def projection_kernel(
    skip, core_ref, x_ref, whole_ref, dq_ref, dk_ref, dv_ref, dwo_ref, one_ref, attn_ref, *refs
):
    keep_ref, give_ref = refs[skip:]
    width = x_ref.shape[1]
    half = width // 2

    def write(first_ref, second_ref):
        first_ref[:width] = dot(whole_ref[...], dk_ref[...], ((0,), (0,))).astype(BF)
        second_ref[:width] = dot(whole_ref[...], dv_ref[...], ((0,), (0,))).astype(BF)
        d_w_q = dot(x_ref[...], dq_ref[...], ((0,), (0,))).astype(BF)
        first_ref[width : width + half] = d_w_q[:half]
        second_ref[width : width + half] = d_w_q[half:]
        first_ref[width + half : 2 * width] = dwo_ref[:half]
        second_ref[width + half : 2 * width] = dwo_ref[half:]
        zeros = jnp.zeros((EXTRA - 32, one_ref.shape[1]), F32)
        sums = [one_ref[...], attn_ref[...], zeros]
        first_ref[2 * width :] = jnp.concatenate(sums, axis=0).astype(BF)
        second_ref[2 * width :] = jnp.zeros((EXTRA, one_ref.shape[1]), BF)

    @pl.when(core_ref[0] == 0)
    def _():
        write(keep_ref, give_ref)

    @pl.when(core_ref[0] == 1)
    def _():
        write(give_ref, keep_ref)


def projection(core, inputs, whole, d_query, d_key, d_value, d_w_out, sums_one, sums_attn, deps):
    rows, width = inputs.shape
    length = whole.shape[0]
    tile = 256

    def columns(count):
        return pl.BlockSpec((count, tile), lambda j, _: (0, j))

    shape = jax.ShapeDtypeStruct((2 * width + EXTRA, width), BF)
    return pl.pallas_call(
        functools.partial(projection_kernel, len(deps)),
        grid_spec=pltpu.PrefetchScalarGridSpec(
            num_scalar_prefetch=1,
            grid=(width // tile,),
            in_specs=[
                whole_spec((rows, width)),
                whole_spec((length, width)),
                columns(rows),
                columns(length),
                columns(length),
                columns(width),
                columns(24),
                columns(8),
            ]
            + [ANYWHERE] * len(deps),
            out_specs=[columns(2 * width + EXTRA)] * 2,
        ),
        out_shape=[shape, shape],
        name="projection",
        **params(4 * length * width * width, 8 * length * width),
    )(core, inputs, whole, d_query, d_key, d_value, d_w_out, sums_one, sums_attn, *deps)


def input_kernel(final, skip, at_ref, dk_ref, dv_ref, w_ref, *refs):
    refs = list(refs)
    if final:
        dq_ref, dh1_ref = refs.pop(0), refs.pop(0)
    out_ref = refs[skip]
    width = dk_ref.shape[1]
    step = pl.program_id(0)
    product = dot(dk_ref[...], w_ref[:, width : 2 * width], ((1,), (1,)))
    product = product + dot(dv_ref[...], w_ref[:, 2 * width :], ((1,), (1,)))
    out_ref[0] = product.astype(out_ref.dtype)
    if final:

        @pl.when(parity_block(True, step, at_ref) == at_ref[1])
        def _():
            out_ref[0] += dh1_ref[...] + dot(dq_ref[...], w_ref[:, :width], ((1,), (1,)))


def input_grad(final, at, d_key, d_value, w_qkv, own, deps):
    width = w_qkv.shape[0]
    count = lax.axis_size("seq")
    rows = d_key.shape[0] // count
    half = count // 2
    per_block = pl.BlockSpec((rows, width), lambda i, at: (parity_block(final, i, at), 0))
    return pl.pallas_call(
        functools.partial(input_kernel, final, len(deps)),
        grid_spec=pltpu.PrefetchScalarGridSpec(
            num_scalar_prefetch=1,
            grid=(half,),
            in_specs=[per_block, per_block, whole_spec(w_qkv.shape)]
            + [whole_spec((rows, width))] * len(own)
            + [ANYWHERE] * len(deps),
            out_specs=pl.BlockSpec((1, rows, width), lambda i, _: (i, 0, 0)),
        ),
        out_shape=jax.ShapeDtypeStruct((half, rows, width), F32 if final else BF),
        name="input_grad",
        **params(2 * count * rows * width * width, 4 * count * rows * width),
    )(at, d_key, d_value, w_qkv, *own, *deps)


def normalise(hidden):
    centred = hidden - jnp.mean(hidden, axis=-1, keepdims=True)
    rstd = lax.rsqrt(jnp.mean(centred * centred, axis=-1, keepdims=True) + 1e-05)
    return centred * rstd, rstd


def norm_back(scaled, normed, rstd):
    return rstd * (
        scaled
        - jnp.mean(scaled, axis=-1, keepdims=True)
        - normed * jnp.mean(scaled * normed, axis=-1, keepdims=True)
    )


def column_sum(value):
    return jnp.sum(value, axis=0, keepdims=True)


def gelu_both(value):
    slope = math.sqrt(2.0 / math.pi)
    square = value * value
    bent = jnp.tanh(slope * (value + 0.044715 * (value * square)))
    rise = 0.5 * (1.0 + bent)
    inner = slope * (1.0 + (3.0 * 0.044715) * square)
    return value * rise, rise + (0.5 * value) * (1.0 - bent * bent) * inner


def ffn_kernel(
    chunks, core_ref, o_ref, x_ref, g_ref, wo_ref, up_ref, down_ref, bup_ref, vec_ref,
    out_ref, keep_ref, give_ref, dh2_ref, du_ref, n1_ref, r1_ref, sums_ref,
    y1, low, act, slope, h2, dh2_low,
):
    step = pl.program_id(0)
    b_out, gain1, bias1, b_down, gain2, bias2 = (vec_ref[i : i + 1] for i in range(6))

    @pl.when(step == 0)
    def _():
        hidden = x_ref[...].astype(F32) + dot(o_ref[...], wo_ref[...]) + b_out
        normed, rstd = normalise(hidden)
        n1_ref[...] = normed
        r1_ref[...] = jnp.broadcast_to(rstd, r1_ref.shape)
        value = normed * gain1 + bias1
        y1[...] = value
        low[...] = value.astype(BF)

    @pl.when(step < chunks)
    def _():
        value, rate = gelu_both(dot(low[...], up_ref[...]) + bup_ref[0])
        act[step] = value.astype(BF)
        slope[step] = rate
        product = dot(act[step], down_ref[...])

        @pl.when(step == 0)
        def _():
            h2[...] = y1[...] + b_down + product

        @pl.when(step > 0)
        def _():
            h2[...] += product

    @pl.when(step == chunks - 1)
    def _():
        normed, rstd = normalise(h2[...])
        out_ref[...] = (normed * gain2 + bias2).astype(BF)
        grad = g_ref[...].astype(F32)
        d_hidden = norm_back(grad * gain2, normed, rstd)
        dh2_ref[...] = d_hidden
        dh2_low[...] = d_hidden.astype(BF)
        sums_ref[...] = jnp.zeros_like(sums_ref)
        sums_ref[0:1] = column_sum(d_hidden)
        sums_ref[1:2] = column_sum(grad * normed)
        sums_ref[2:3] = column_sum(grad)

    @pl.when(step >= chunks)
    def _():
        chunk = 2 * chunks - 1 - step
        d_u = dot(dh2_low[...], down_ref[...], ((1,), (1,))) * slope[chunk]
        sums_ref[pl.ds(8 + chunk, 1)] = column_sum(d_u)
        d_u = d_u.astype(BF)
        du_ref[...] = d_u

        @pl.when(core_ref[0] == 0)
        def _():
            keep_ref[...] = dot(act[chunk], dh2_low[...], ((0,), (0,))).astype(BF)
            give_ref[...] = dot(low[...], d_u, ((0,), (0,))).astype(BF)

        @pl.when(core_ref[0] == 1)
        def _():
            give_ref[...] = dot(act[chunk], dh2_low[...], ((0,), (0,))).astype(BF)
            keep_ref[...] = dot(low[...], d_u, ((0,), (0,))).astype(BF)


def ffn(core, o_low, inputs, grad, w_out, w_up, w_down, b_up, vectors):
    rows, width = inputs.shape
    wide = w_up.shape[1]
    chunks = wide // width
    full = whole_spec

    def fore(i):
        return jnp.minimum(i, chunks - 1)

    def both(i):
        return jnp.where(i < chunks, i, 2 * chunks - 1 - i)

    def back(i):
        return jnp.minimum(2 * chunks - 1 - i, chunks - 1)

    rows_spec = full((rows, width))
    share = pl.BlockSpec((width, width), lambda i, _: (back(i), 0))
    f32_rows = jax.ShapeDtypeStruct((rows, width), F32)
    return pl.pallas_call(
        functools.partial(ffn_kernel, chunks),
        grid_spec=pltpu.PrefetchScalarGridSpec(
            num_scalar_prefetch=1,
            grid=(2 * chunks,),
            in_specs=[
                rows_spec,
                rows_spec,
                rows_spec,
                full((width, width)),
                pl.BlockSpec((width, width), lambda i, _: (0, fore(i))),
                pl.BlockSpec((width, width), lambda i, _: (both(i), 0)),
                pl.BlockSpec((1, 1, width), lambda i, _: (fore(i), 0, 0)),
                full(vectors.shape),
            ],
            out_specs=[
                rows_spec,
                share,
                share,
                rows_spec,
                pl.BlockSpec((rows, width), lambda i, _: (0, back(i))),
                rows_spec,
                full((rows, LANES)),
                full((16, width)),
            ],
            scratch_shapes=[
                pltpu.VMEM((rows, width), F32),
                pltpu.VMEM((rows, width), BF),
                pltpu.VMEM((chunks, rows, width), BF),
                pltpu.VMEM((chunks, rows, width), F32),
                pltpu.VMEM((rows, width), F32),
                pltpu.VMEM((rows, width), BF),
            ],
        ),
        out_shape=[
            jax.ShapeDtypeStruct((rows, width), BF),
            jax.ShapeDtypeStruct((wide, width), BF),
            jax.ShapeDtypeStruct((wide, width), BF),
            f32_rows,
            jax.ShapeDtypeStruct((rows, wide), BF),
            f32_rows,
            jax.ShapeDtypeStruct((rows, LANES), F32),
            jax.ShapeDtypeStruct((16, width), F32),
        ],
        name="ffn",
        **params(11 * rows * width * wide, 12 * width * wide),
    )(core, o_low, inputs, grad, w_out, w_up, w_down, b_up.reshape(chunks, 1, width), vectors)


def norm_one_kernel(
    o_ref, dh2_ref, du_ref, n1_ref, r1_ref, up_ref, wo_ref, gain_ref, two_ref,
    dh1_ref, do_ref, dwo_ref, sums_ref, acc,
):
    step = pl.program_id(0)
    product = dot(du_ref[...], up_ref[...], ((1,), (1,)))

    @pl.when(step == 0)
    def _():
        acc[...] = dh2_ref[...] + product

    @pl.when(step > 0)
    def _():
        acc[...] += product

    @pl.when(step == pl.num_programs(0) - 1)
    def _():
        grad = acc[...]
        normed = n1_ref[...]
        d_hidden = norm_back(grad * gain_ref[0:1], normed, r1_ref[:, 0:1])
        dh1_ref[...] = d_hidden
        low = d_hidden.astype(BF)
        dwo_ref[...] = dot(o_ref[...], low, ((0,), (0,))).astype(BF)
        sums_ref[:16] = two_ref[...]
        sums_ref[16:] = jnp.zeros((8, low.shape[1]), F32)
        sums_ref[16:17] = column_sum(d_hidden)
        sums_ref[17:18] = column_sum(grad * normed)
        sums_ref[18:19] = column_sum(grad)
        do_ref[...] = dot(low, wo_ref[...], ((1,), (1,))).astype(BF)


def norm_one(o_low, dh2, du, n1, r1, w_up, w_out, gain, sums_two):
    rows, width = n1.shape
    wide = w_up.shape[1]
    full = whole_spec
    rows_spec = full((rows, width))
    return pl.pallas_call(
        norm_one_kernel,
        grid=(wide // width,),
        in_specs=[
            rows_spec,
            rows_spec,
            pl.BlockSpec((rows, width), lambda i: (0, i)),
            rows_spec,
            full((rows, LANES)),
            pl.BlockSpec((width, width), lambda i: (0, i)),
            full((width, width)),
            full((1, width)),
            full(sums_two.shape),
        ],
        out_specs=[rows_spec, rows_spec, full((width, width)), full((24, width))],
        out_shape=[
            jax.ShapeDtypeStruct((rows, width), F32),
            jax.ShapeDtypeStruct((rows, width), BF),
            jax.ShapeDtypeStruct((width, width), BF),
            jax.ShapeDtypeStruct((24, width), F32),
        ],
        scratch_shapes=[pltpu.VMEM((rows, width), F32)],
        name="norm_one",
        **params(3 * rows * width * wide, 2 * width * wide),
    )(o_low, dh2, du, n1, r1, w_up, w_out, gain, sums_two)


def place_ffn_kernel(core_ref, mine_ref, other_ref, down_ref, up_ref):
    for core in range(2):

        @pl.when(core_ref[0] == core)
        def _():
            down_ref[...] = (mine_ref, other_ref)[core][...].astype(F32)
            up_ref[...] = (other_ref, mine_ref)[core][...].astype(F32)


def place_ffn(core, wide, mine, other):
    width = mine.shape[1]
    block = pl.BlockSpec((width, width), lambda i, _: (i, 0))
    return pl.pallas_call(
        place_ffn_kernel,
        grid_spec=pltpu.PrefetchScalarGridSpec(
            num_scalar_prefetch=1,
            grid=(wide // width,),
            in_specs=[block, block],
            out_specs=[block, pl.BlockSpec((width, width), lambda i, _: (0, i))],
        ),
        out_shape=[
            jax.ShapeDtypeStruct((wide, width), F32),
            jax.ShapeDtypeStruct((width, wide), F32),
        ],
        name="place_ffn",
        **params(0, 16 * wide * width),
    )(core, mine, other)


def place_attn_kernel(
    core_ref, mine_ref, other_ref, half_mine, half_other, low_mine, low_other,
    out_ref, dwo_ref, small_ref,
):
    half = half_mine.shape[0]
    step = pl.program_id(0)
    for core in range(2):
        mine = core_ref[0] == core

        for at, ref in ((0, out_ref), (1, dwo_ref)):

            @pl.when(jnp.logical_and(mine, step == at))
            def _():
                ref[:half] = (half_mine, half_other)[core][...].astype(F32)
                ref[half:] = (half_other, half_mine)[core][...].astype(F32)

        @pl.when(jnp.logical_and(mine, step == 0))
        def _():
            small_ref[...] = (low_mine, low_other)[core][...].astype(F32)

        for which in range(2):

            @pl.when(jnp.logical_and(mine, step == 1 + which))
            def _():
                out_ref[...] = (mine_ref, other_ref)[(core + which) % 2][...].astype(F32)


def place_attn(core, mine, other):
    width = mine.shape[1]
    half = width // 2
    block = whole_spec((width, width))
    halves = pl.BlockSpec((half, width), lambda i, _: (2 + jnp.minimum(i, 1), 0))
    low = pl.BlockSpec((EXTRA, width), lambda i, _: (2 * width // EXTRA, 0))
    return pl.pallas_call(
        place_attn_kernel,
        grid_spec=pltpu.PrefetchScalarGridSpec(
            num_scalar_prefetch=1,
            grid=(3,),
            in_specs=[block, block, halves, halves, low, low],
            out_specs=[
                pl.BlockSpec((width, width), lambda i, _: (0, i)),
                whole_spec((width, width)),
                whole_spec((EXTRA, width)),
            ],
        ),
        out_shape=[
            jax.ShapeDtypeStruct((width, 3 * width), F32),
            jax.ShapeDtypeStruct((width, width), F32),
            jax.ShapeDtypeStruct((EXTRA, width), F32),
        ],
        name="place_attn",
        **params(0, 24 * width * width),
    )(core, mine, other, mine, other, mine, other)


def per_device(
    layer_input,
    segment_ids,
    w_qkv,
    b_query,
    b_value,
    w_out,
    b_out,
    ln1_gain,
    ln1_bias,
    w_up,
    b_up,
    w_down,
    b_down,
    ln2_gain,
    ln2_bias,
    cotangent,
):
    _, rows, width = layer_input.shape
    scale = (width // HEADS) ** (-0.5)
    inputs = layer_input.reshape(rows, width)
    ids = segment_ids.reshape(rows)

    id_rows = -(-rows // width)
    id_block = jnp.pad(ids.astype(BF), (0, id_rows * width - rows)).reshape(id_rows, width)
    block = jnp.concatenate([inputs, jnp.pad(id_block, ((0, 16 - id_rows), (0, 0)))], axis=0)
    count = lax.axis_size("seq")
    here = lax.axis_index("seq")
    bias = jnp.concatenate([b_query, jnp.zeros_like(b_value), b_value]).reshape(1, -1)
    length = rows * count

    def place(first, second):
        inside = [jnp.logical_and(at >= 0, at < count) for at in (first, second)]
        return jnp.stack(
            [jnp.clip(at, 0, count - 1) for at in (first, second)]
            + [flag.astype(jnp.int32) for flag in inside]
        ).astype(jnp.int32)

    whole, keys_values, queries, query_hot, token = project(
        True, place(here, here), [block], w_qkv, bias, [], length
    )
    ring = line_steps(block)
    way = 1 - 2 * (here & 1)

    def near(k):
        return here + way * k, here - way * k

    for k in range(1, count):
        next(ring)
        pair = ring.send([token])
        whole, keys_values, token = project(
            False, place(*near(k)), pair, w_qkv, bias, [whole, keys_values], length
        )
    attended, attended_low, logsum = attend(queries, keys_values, query_hot, scale)

    core = stages_of("batch")[0]
    core_bit = bit_of(core).reshape(1)
    vectors = jnp.stack([b_out, ln1_gain, ln1_bias, b_down, ln2_gain, ln2_bias] + [b_down] * 2)
    result, kept, give, dh2, du, normed_one, rstd_one, sums_two = ffn(
        core_bit, attended_low, inputs, cotangent.reshape(rows, width),
        w_out, w_up, w_down, b_up, vectors,
    )
    came = swap(give, core)
    d_first, d_attended, d_w_out, sums_one = norm_one(
        attended_low, dh2, du, normed_one, rstd_one, w_up, w_out, ln1_gain.reshape(1, width),
        sums_two,
    )
    came = together([came], [d_first])
    exchanges = Exchanges()
    exchanges.add("ffn", sum_everywhere([kept, *came]))
    here_at = jnp.stack([here & 1, here]).astype(jnp.int32)
    parts = 2

    def back(final, deps, before, partial):
        return attend_back(
            final, parts, here_at, deps, before, partial, queries, keys_values, query_hot,
            d_attended, attended, logsum, scale,
        )

    sent = exchanges.go(["ffn"])
    got = back(False, sent, [], [])
    partial = list(got[:2])
    d_x_sent = input_grad(False, here_at, *got[2:4], w_qkv, [], got[4:])
    exchanges.add("input", line_scatter(d_x_sent))
    sent = exchanges.go(["ffn", "input"], [d_x_sent])
    got = back(True, sent, got[2:4], partial)
    d_query, sums_attn, d_key, d_value, token = got
    sent = exchanges.go(["ffn"], [token])
    attn_kept, attn_give = projection(
        core_bit, inputs, whole, d_query, d_key, d_value, d_w_out, sums_one, sums_attn, sent
    )
    sent = exchanges.go(["ffn"], [attn_kept], land=["input"])
    attn_came = swap(*together([attn_give], sent), core)
    d_x_kept = input_grad(True, here_at, d_key, d_value, w_qkv, [d_query, d_first], sent)
    attn_came = together([attn_came], [d_x_kept])
    exchanges.add("attn", sum_everywhere([attn_kept, *attn_came]))
    both = ["ffn", "attn"]
    exchanges.go(both, [d_x_kept])
    exchanges.go(both)
    exchanges.go(both + ["input"], kept=d_x_kept)
    exchanges.go(both + ["input"])
    exchanges.go(["attn"])
    exchanges.go(["attn"], land=["input"])
    exchanges.go(["attn"], land=["ffn"])
    exchanges.go(["ffn", "input"])
    exchanges.go(["attn"])
    while "ffn" not in exchanges.results:
        exchanges.go(["ffn"])
    d_w_down, d_w_up = place_ffn(core_bit, w_up.shape[1], *exchanges.results["ffn"])
    exchanges.go(["attn"], [d_w_down])
    while len(exchanges.results) < 3:
        exchanges.go(["attn", "input"])
    d_input = exchanges.results["input"]
    d_w_qkv, d_w_out, small = place_attn(core_bit, *exchanges.results["attn"])
    chunks = w_up.shape[1] // width
    d_b_down, d_ln2_gain, d_ln2_bias = (small[i] for i in range(3))
    d_b_up = small[8 : 8 + chunks].reshape(-1)
    d_b_out, d_ln1_gain, d_ln1_bias = (small[16 + i] for i in range(3))
    d_b_query, d_b_value = (small[24 + i] for i in range(2))

    return (
        result.reshape(layer_input.shape),
        d_input.reshape(layer_input.shape),
        d_w_qkv,
        d_b_query,
        d_b_value,
        d_w_out,
        d_b_out,
        d_ln1_gain,
        d_ln1_bias,
        d_w_up,
        d_b_up,
        d_w_down,
        d_b_down,
        d_ln2_gain,
        d_ln2_bias,
    )


def solution(mesh):
    rows = P("batch", "seq", None)
    return jax.shard_map(
        per_device,
        mesh=mesh,
        in_specs=(rows, P("batch", "seq")) + (P(),) * 13 + (rows,),
        out_specs=(rows, rows) + (P(),) * 13,
        check_vma=False,
    )
```

time: 1780 us -> 435 us (0.24)
  blocking collectives: 620 us -> 0 us
  local copies, waits for them, and re-layouts: 555 us -> 25.1 us
  matrix products: 202 us -> 0 us
  Pallas kernels: 0 us -> 176 us
  waiting for transfers between devices: 293 us -> 143 us
  starting transfers between devices: 2.12 us -> 29.6 us
    unnamed x1 -> x0, blocking collectives: 606 us -> none
    unnamed x92 -> x90, local copies, waits for them, and re-layouts: 277 us -> 19.9 us
    all_gather x3 -> x0, waiting for transfers between devices: 215 us -> none  [the longest x1 108 us: per_device(): lax.all_gather(shares.astype(jnp.bfloat16), ('batch', 'seq'), axis=0, til...]
    dot_general x40 -> x0, matrix products: 202 us -> none  [the longest x4 28.7 us: fold_block(): jnp.einsum('bqhd,bkhd->bhqk', queries, keys, preferred_element_type=jnp.f...]
    pallas_call x0 -> x36, Pallas kernels: none -> 176 us  [the longest x2 46.3 us: attend_back(): pl.pallas_call(functools.partial(attend_back_kernel, final, scale, pairs,...]
    ppermute x0 -> x29, waiting for transfers between devices: none -> 143 us  [the longest x23 118 us: swap(): lax.ppermute(value, stage[0], [(i, i ^ 1 << bits[i % 2]) for i in range(c...]
    reshape x6 -> x3, local copies, waits for them, and re-layouts: 96.5 us -> 1.23 us  [the longest x1 0.61 us: per_device(): d_b_up = small[8:8 + chunks].reshape(-1)]
    slice x9 -> x3, local copies, waits for them, and re-layouts: 91 us -> 3.23 us  [the longest x1 1.56 us: per_device(): d_b_down, d_ln2_gain, d_ln2_bias = (small[i] for i in range(3))]
  transfers between devices with their start and end apart: 6 -> 29, of which waited for: 6 -> 16; matrix products, arithmetic and copies ran while one was open for 3% -> 4% of each run, Pallas kernels for 0% -> 27%
where the time goes in v1:
time: 435 us; the launch traced here: 428 us
  Pallas kernels  176 us (40%)
  waiting for transfers between devices  143 us (33%)
  other arithmetic  52.9 us (12%)
  starting transfers between devices  29.6 us (7%)
  local copies, waits for them, and re-layouts  25.1 us (6%)
    ppermute x23, waiting for transfers between devices, swap(): lax.ppermute(value, stage[0], [(i, i ^ 1 << bits[i % 2]) for i in range(c...  118 us
    pallas_call x2, Pallas kernels, attend_back(): pl.pallas_call(functools.partial(attend_back_kernel, final, scale, pairs,...  46.3 us
    pallas_call x1, Pallas kernels, ffn(): pl.pallas_call(functools.partial(ffn_kernel, chunks), grid_spec=pltpu.Pre...  28 us
    pallas_call x4, Pallas kernels, project(): pl.pallas_call(functools.partial(project_kernel, first, rows), grid_spec=...  27.3 us
    ppermute x3, waiting for transfers between devices, line_steps(): lax.ppermute(two, 'seq', pairs[0])  24.5 us
    convert_element_type x8, other arithmetic, part_of(): return total.astype(BF)  22 us
    unnamed x90, local copies, waits for them, and re-layouts  19.9 us
    pallas_call x1, Pallas kernels, attend(): pl.pallas_call(functools.partial(attend_kernel, scale, 256), grid=(pairs,...  19.3 us
  transfers between devices with their start and end apart: 29, of which 16 were waited for; matrix products, arithmetic and copies ran while one was open for 4% of the time, Pallas kernels for 27%

profile of v1, /device:TPU:0, one launch (start us, length us, event | category | flops | bytes accessed | tf_op | source)
XLA Modules:
  0.0 427.7 jit_solution(8900578248036285563)
XLA Ops:
  8.3 7.4 %project.4 = (bf16[2048,768]{1,0:T(8,128)(2,1)}, bf16[2048,1664]{1,0:T(8,128)(2,1)}, bf16[512,768]{1,0:T(8,128)(2,1)}, bf16[512,128]{1,0:T(8,128)(2,1)}, f32[8,128]{1,0:T(8,128)}) custom-call(s32[4]{0:T(128)} %pad_add_fusion.place_ref, bf16[528,768]{1,0:T(8,128)(2,1)} %copy-done.18, bf16[768,2304]{1,0:T(8,128)(2,1)} %w_ref.3, bf16[768,2304]{1,0:T(8,128)(2,1)} %w_ref.3, ...), custom_call_target="tpu_custom_call" | custom-call | flops 603979776 | bytes 3145728 | tf_op jit(solution)/shard_map/project/pallas_call | solution.py:294
  15.8 8.0 %collective-permute-done.refs_0_ = bf16[528,768]{1,0:T(8,128)(2,1)S(1)} collective-permute-done((bf16[528,768]{1,0:T(8,128)(2,1)S(1)}, bf16[528,768]{1,0:T(8,128)(2,1)S(1)}, u32[]{:S(2)}, u32[]{:S(2)}) %collective-permute-start) | collective-permute-done | bytes 811040 | tf_op jit(solution)/shard_map/ppermute | solution.py:165
  24.9 4.5 %collective-permute-start.2 = (bf16[528,768]{1,0:T(8,128)(2,1)}, bf16[528,768]{1,0:T(8,128)(2,1)S(1)}, u32[]{:S(2)}, u32[]{:S(2)}) collective-permute-start(bf16[528,768]{1,0:T(8,128)(2,1)} %get-tuple-element.96.refs_1_), channel_id=1, source_target_pairs={{0,1},{1,0},{2,3},{3,2},{4,5},{5,4},{6,7},{7,6},{8,9},{9,8},{10,11... | collective-permute-start | bytes 2433032 | tf_op jit(solution)/shard_map/ppermute | solution.py:165
  30.7 6.7 %project.5 = (bf16[2048,768]{1,0:T(8,128)(2,1)}, bf16[2048,1664]{1,0:T(8,128)(2,1)}, f32[8,128]{1,0:T(8,128)}) custom-call(s32[4]{0:T(128)} %pad_add_fusion.2.place_ref, bf16[528,768]{1,0:T(8,128)(2,1)} %get-tuple-element.97.refs_0_, bf16[528,768]{1,0:T(8,128)(2,1)} %get-tuple-element.96.refs_1_, ...), custom_call_target="tpu_custom_call", output_to_operand_aliasing={{0}: (7, {}), {1}: (8, {})} | custom-call | flops 1207959552 | bytes 3145728 | tf_op jit(solution)/shard_map/project/pallas_call | solution.py:294
  37.4 9.3 %collective-permute-done.2.refs_0_ = bf16[528,768]{1,0:T(8,128)(2,1)S(1)} collective-permute-done((bf16[528,768]{1,0:T(8,128)(2,1)}, bf16[528,768]{1,0:T(8,128)(2,1)S(1)}, u32[]{:S(2)}, u32[]{:S(2)}) %collective-permute-start.2) | collective-permute-done | bytes 811040 | tf_op jit(solution)/shard_map/ppermute | solution.py:165
  54.0 6.6 %project.6 = (bf16[2048,768]{1,0:T(8,128)(2,1)}, bf16[2048,1664]{1,0:T(8,128)(2,1)}, f32[8,128]{1,0:T(8,128)}) custom-call(s32[4]{0:T(128)} %pad_add_fusion.3.place_ref, bf16[528,768]{1,0:T(8,128)(2,1)} %get-tuple-element.102.refs_0_, bf16[528,768]{1,0:T(8,128)(2,1)} %get-tuple-element.101.refs_1_, ...), custom_call_target="tpu_custom_call", output_to_operand_aliasing={{0}: (7, {}), {1}: (8, {})} | custom-call | flops 1207959552 | bytes 3145728 | tf_op jit(solution)/shard_map/project/pallas_call | solution.py:294
  60.6 7.2 %collective-permute-done.4.refs_0_ = bf16[528,768]{1,0:T(8,128)(2,1)S(1)} collective-permute-done((bf16[528,768]{1,0:T(8,128)(2,1)}, bf16[528,768]{1,0:T(8,128)(2,1)S(1)}, u32[]{:S(2)}, u32[]{:S(2)}) %collective-permute-start.4) | collective-permute-done | bytes 811040 | tf_op jit(solution)/shard_map/ppermute | solution.py:165
  68.9 6.6 %project.7 = (bf16[2048,768]{1,0:T(8,128)(2,1)}, bf16[2048,1664]{1,0:T(8,128)(2,1)}, f32[8,128]{1,0:T(8,128)}) custom-call(s32[4]{0:T(128)} %pad_add_fusion.1.place_ref, bf16[528,768]{1,0:T(8,128)(2,1)} %get-tuple-element.106.refs_0_, bf16[528,768]{1,0:T(8,128)(2,1)} %get-tuple-element.107.refs_1_, ...), custom_call_target="tpu_custom_call", output_to_operand_aliasing={{0}: (7, {}), {1}: (8, {})} | custom-call | flops 1207959552 | bytes 3145728 | tf_op jit(solution)/shard_map/project/pallas_call | solution.py:294
  75.5 19.3 %attend.1 = (f32[512,768]{1,0:T(8,128)}, bf16[512,768]{1,0:T(8,128)(2,1)}, f32[6,8,512]{2,1,0:T(8,128)}) custom-call(bf16[512,768]{1,0:T(8,128)(2,1)} %get-tuple-element.94.q_ref, bf16[2048,1664]{1,0:T(8,128)(2,1)} %get-tuple-element.110.k_ref.v_ref.kh_ref, bf16[2048,1664]{1,0:T(8,128)(2,1)} %get-tuple-element.110.k_ref.v_ref.kh_ref, ...), custom_call_target="tpu_custom_call" | custom-call | flops 3221225472 | bytes 12582912 | tf_op jit(solution)/shard_map/attend/pallas_call | solution.py:356
  94.8 28.0 %ffn.1 = (bf16[512,768]{1,0:T(8,128)(2,1)}, bf16[3072,768]{1,0:T(8,128)(2,1)}, bf16[3072,768]{1,0:T(8,128)(2,1)}, f32[512,768]{1,0:T(8,128)}, bf16[512,3072]{1,0...) custom-call(s32[1]{0:T(128)} %bitcast.core_ref, ...), custom_call_target="tpu_custom_call" | custom-call | flops 13287555072 | bytes 28311552 | tf_op jit(solution)/shard_map/ffn/pallas_call | solution.py:725
  122.9 11.7 %norm_one.1 = (f32[512,768]{1,0:T(8,128)}, bf16[512,768]{1,0:T(8,128)(2,1)}, bf16[768,768]{1,0:T(8,128)(2,1)}, f32[24,768]{1,0:T(8,128)}) custom-call(bf16[512,768]{1,0:T(8,128)(2,1)} %get-tuple-element.112.o_ref, f32[512,768]{1,0:T(8,128)} %get-tuple-element.114.dh2_ref, bf16[512,3072]{1,0:T(8,128)(2,1)} %get-tuple-element.115.du_ref, ...), custom_call_target="tpu_custom_call" | custom-call | flops 3623878656 | bytes 4718592 | tf_op jit(solution)/shard_map/norm_one/pallas_call | solution.py:810
  134.6 4.4 %add_convert_fusion.refs_0_ = bf16[1536,768]{1,0:T(8,128)(2,1)} fusion(bf16[3072,768]{1,0:T(8,128)(2,1)} %together.25, s32[]{:T(128)S(6)} %select_n.234, bf16[3072,768]{1,0:T(8,128)(2,1)} %get-tuple-element.122), kind=kLoop, calls=%fused_computation.1 | loop fusion | flops 4718592 | bytes 7077892 | tf_op jit(solution)/shard_map/convert_element_type | solution.py:65
  141.0 22.9 %attend_back.2 = (f32[512,768]{1,0:T(8,128)}, f32[8,768]{1,0:T(8,128)}, bf16[2048,768]{1,0:T(8,128)(2,1)}, bf16[2048,768]{1,0:T(8,128)(2,1)}, f32[8,128]{1,0:T(8,128)}) custom-call(s32[2]{0:T(128)} %pad_add_fusion.4.at_ref, bf16[512,768]{1,0:T(8,128)(2,1)} %get-tuple-element.94.q_ref, bf16[2048,1664]{1,0:T(8,128)(2,1)} %get-tuple-element.110.k_ref.v_ref.kh_ref, ...), custom_call_target="tpu_custom_call" | custom-call | flops 8053063680 | bytes 12582912 | tf_op jit(solution)/shard_map/attend_back/pallas_call | solution.py:470
  164.0 6.9 %input_grad.2.refs_1_ = bf16[2,512,768]{2,1,0:T(8,128)(2,1)} custom-call(s32[2]{0:T(128)} %pad_add_fusion.4.at_ref, bf16[2048,768]{1,0:T(8,128)(2,1)} %get-tuple-element.127.dk_ref.refs_2_, bf16[2048,768]{1,0:T(8,128)(2,1)} %get-tuple-element.128.dv_ref.refs_3_, bf16[768,2304]{1,0:T(8,128)(2,1)} %w_ref.3, f32[8,128]{1,0:T(8,128)} %get-tuple-element.129.refs_0_), custom_call_target="tpu_custom_call" | custom-call | flops 2415919104 | bytes 6291456 | tf_op jit(solution)/shard_map/input_grad/pallas_call | solution.py:599
  172.3 3.7 add_convert_fusion.2.refs_0_
  178.7 23.4 %attend_back.3 = (bf16[512,768]{1,0:T(8,128)(2,1)}, f32[8,768]{1,0:T(8,128)}, bf16[2048,768]{1,0:T(8,128)(2,1)}, bf16[2048,768]{1,0:T(8,128)(2,1)}, f32[8,128]{1,0:T(8,128)}) custom-call(s32[2]{0:T(128)} %pad_add_fusion.4.at_ref, bf16[512,768]{1,0:T(8,128)(2,1)} %get-tuple-element.94.q_ref, ...), custom_call_target="tpu_custom_call", output_to_operand_aliasing={{2}: (11, {}), {3}: (12, {})} | custom-call | flops 8053063680 | bytes 12582912 | tf_op jit(solution)/shard_map/attend_back/pallas_call | solution.py:470
  206.3 11.3 %projection.1 = (bf16[1664,768]{1,0:T(8,128)(2,1)}, bf16[1664,768]{1,0:T(8,128)(2,1)}) custom-call(s32[1]{0:T(128)} %bitcast.core_ref, bf16[512,768]{1,0:T(8,128)(2,1)} %bitcast.31, bf16[2048,768]{1,0:T(8,128)(2,1)} %get-tuple-element.136.whole_ref, bf16[512,768]{1,0:T(8,128)(2,1)} %get-tuple-element.134.dq_ref.refs_0_, ...), custom_call_target="tpu_custom_call" | custom-call | flops 4831838208 | bytes 12582912 | tf_op jit(solution)/shard_map/projection/pallas_call | solution.py:552
  217.7 9.0 %collective-permute-done.9.refs_0_ = bf16[384,768]{1,0:T(8,128)(2,1)S(1)} collective-permute-done((bf16[384,768]{1,0:T(8,128)(2,1)S(1)}, bf16[384,768]{1,0:T(8,128)(2,1)S(1)}, u32[]{:S(2)}, u32[]{:S(2)}) %collective-permute-start.9) | collective-permute-done | bytes 589856 | tf_op jit(solution)/shard_map/ppermute | solution.py:38
  233.6 8.7 %input_grad.3.refs_1_ = f32[2,512,768]{2,1,0:T(8,128)} custom-call(s32[2]{0:T(128)} %pad_add_fusion.4.at_ref, bf16[2048,768]{1,0:T(8,128)(2,1)} %get-tuple-element.132.dk_ref, bf16[2048,768]{1,0:T(8,128)(2,1)} %get-tuple-element.133.dv_ref, bf16[768,2304]{1,0:T(8,128)(2,1)} %w_ref.3, bf16[512,768]{1,0:T(8,128)(2,1)} %get-tuple-element.134.dq_ref.refs_0_, ...), custom_call_target="tpu_custom_call" | custom-call | flops 2415919104 | bytes 6291456 | tf_op jit(solution)/shard_map/input_grad/pallas_call | solution.py:599
  242.4 5.3 %collective-permute-done.11.refs_0_ = bf16[192,768]{1,0:T(8,128)(2,1)S(1)} collective-permute-done((bf16[192,768]{1,0:T(8,128)(2,1)S(1)}, bf16[192,768]{1,0:T(8,128)(2,1)S(1)}, u32[]{:S(2)}, u32[]{:S(2)}) %collective-permute-start.11) | collective-permute-done | bytes 294944 | tf_op jit(solution)/shard_map/ppermute | solution.py:38
  255.6 14.7 %collective-permute-done.13.refs_0_ = bf16[192,768]{1,0:T(8,128)(2,1)S(1)} collective-permute-done((bf16[192,768]{1,0:T(8,128)(2,1)}, bf16[192,768]{1,0:T(8,128)(2,1)S(1)}, u32[]{:S(2)}, u32[]{:S(2)}) %collective-permute-start.13) | collective-permute-done | bytes 294944 | tf_op jit(solution)/shard_map/ppermute | solution.py:38
  277.9 13.9 %collective-permute-done.15.refs_0_ = bf16[384,768]{1,0:T(8,128)(2,1)} collective-permute-done((bf16[384,768]{1,0:T(8,128)(2,1)}, bf16[384,768]{1,0:T(8,128)(2,1)}, u32[]{:S(2)}, u32[]{:S(2)}) %collective-permute-start.15) | collective-permute-done | bytes 589856 | tf_op jit(solution)/shard_map/ppermute | solution.py:38
  303.9 12.3 %collective-permute-done.18.refs_1_ = bf16[208,768]{1,0:T(8,128)(2,1)S(1)} collective-permute-done((bf16[208,768]{1,0:T(8,128)(2,1)}, bf16[208,768]{1,0:T(8,128)(2,1)S(1)}, u32[]{:S(2)}, u32[]{:S(2)}) %collective-permute-start.18) | collective-permute-done | bytes 319520 | tf_op jit(solution)/shard_map/ppermute | solution.py:38
  316.1 4.0 collective-permute-done.19.refs_2_
  330.2 15.9 %collective-permute-done.20 = bf16[104,768]{1,0:T(8,128)(2,1)S(1)} collective-permute-done((bf16[104,768]{1,0:T(8,128)(2,1)}, bf16[104,768]{1,0:T(8,128)(2,1)S(1)}, u32[]{:S(2)}, u32[]{:S(2)}) %collective-permute-start.20) | collective-permute-done | bytes 159776 | tf_op jit(solution)/shard_map/ppermute | solution.py:38
  347.5 13.8 %collective-permute-done.21.refs_0_ = bf16[104,768]{1,0:T(8,128)(2,1)S(1)} collective-permute-done((bf16[104,768]{1,0:T(8,128)(2,1)S(1)}, bf16[104,768]{1,0:T(8,128)(2,1)S(1)}, u32[]{:S(2)}, u32[]{:S(2)}) %collective-permute-start.21) | collective-permute-done | bytes 159776 | tf_op jit(solution)/shard_map/ppermute | solution.py:38
  363.9 9.5 %collective-permute-done.23.refs_0_ = bf16[208,768]{1,0:T(8,128)(2,1)S(1)} collective-permute-done((bf16[208,768]{1,0:T(8,128)(2,1)S(1)}, bf16[208,768]{1,0:T(8,128)(2,1)S(1)}, u32[]{:S(2)}, u32[]{:S(2)}) %collective-permute-start.23) | collective-permute-done | bytes 319520 | tf_op jit(solution)/shard_map/ppermute | solution.py:38
  377.2 3.8 maximum_select_fusion.mine_ref
  382.1 9.7 %collective-permute-done.25 = bf16[416,768]{1,0:T(8,128)(2,1)S(1)} collective-permute-done((bf16[416,768]{1,0:T(8,128)(2,1)S(1)}, bf16[416,768]{1,0:T(8,128)(2,1)S(1)}, u32[]{:S(2)}, u32[]{:S(2)}) %collective-permute-start.25) | collective-permute-done | bytes 639008 | tf_op jit(solution)/shard_map/ppermute | solution.py:38
  392.8 10.2 %place_ffn.1 = (f32[3072,768]{1,0:T(8,128)}, f32[768,3072]{1,0:T(8,128)}) custom-call(s32[1]{0:T(128)} %bitcast.core_ref, bf16[3072,768]{1,0:T(8,128)(2,1)} %copy-done.4, bf16[3072,768]{1,0:T(8,128)(2,1)} %collective-permute-done.27.other_ref), custom_call_target="tpu_custom_call" | custom-call | bytes 37748736 | tf_op jit(solution)/shard_map/place_ffn/pallas_call | solution.py:849
  403.0 6.7 %collective-permute-done.26.refs_0_ = bf16[832,768]{1,0:T(8,128)(2,1)S(1)} collective-permute-done((bf16[832,768]{1,0:T(8,128)(2,1)S(1)}, bf16[832,768]{1,0:T(8,128)(2,1)S(1)}, u32[]{:S(2)}, u32[]{:S(2)}) %collective-permute-start.26) | collective-permute-done | bytes 1277984 | tf_op jit(solution)/shard_map/ppermute | solution.py:38
  418.5 6.1 %place_attn.1 = (f32[768,2304]{1,0:T(8,128)}, f32[768,768]{1,0:T(8,128)}, f32[128,768]{1,0:T(8,128)}) custom-call(s32[1]{0:T(128)} %bitcast.core_ref, bf16[1664,768]{1,0:T(8,128)(2,1)} %copy-done.1, bf16[1664,768]{1,0:T(8,128)(2,1)} %collective-permute-done.28.other_ref.half_other.low_other, bf16[1664,768]{1,0:T(8,128)(2,1)} %copy-done.1, ...), custom_call_target="tpu_custom_call" | custom-call | bytes 14155776 | tf_op jit(solution)/shard_map/place_attn/pallas_call | solution.py:899
  (196 shorter events, 95.0 us)
Async XLA Ops:
  2.6 21.2 %collective-permute-start = (bf16[528,768]{1,0:T(8,128)(2,1)S(1)}, bf16[528,768]{1,0:T(8,128)(2,1)S(1)}, u32[]{:S(2)}, u32[]{:S(2)}) collective-permute-start(bf16[528,768]{1,0:T(8,128)(2,1)S(1)} %fusion.1.refs_0_), channel_id=1, source_target_pairs={{0,1},{1,0},{2,3},{3,2},{4,5},{5,4},{6,7},{7,6},{8,9},{9,8},{10,11... | collective-permute-start | bytes 2433032 | tf_op jit(solution)/shard_map/ppermute | solution.py:165
  5.7 18.1 %collective-permute-start.1 = (bf16[528,768]{1,0:T(8,128)(2,1)S(1)}, bf16[528,768]{1,0:T(8,128)(2,1)S(1)}, u32[]{:S(2)}, u32[]{:S(2)}) collective-permute-start(bf16[528,768]{1,0:T(8,128)(2,1)S(1)} %fusion.1.refs_0_), channel_id=1, source_target_pairs={{1,2},{2,1},{5,6},{6,5},{9,10},{10,9},{13,14},{14,13},{17,18},{18,... | collective-permute-start | bytes 2433032 | tf_op jit(solution)/shard_map/ppermute | solution.py:165
  24.9 21.9 %collective-permute-start.2 = (bf16[528,768]{1,0:T(8,128)(2,1)}, bf16[528,768]{1,0:T(8,128)(2,1)S(1)}, u32[]{:S(2)}, u32[]{:S(2)}) collective-permute-start(bf16[528,768]{1,0:T(8,128)(2,1)} %get-tuple-element.96.refs_1_), channel_id=1, source_target_pairs={{0,1},{1,0},{2,3},{3,2},{4,5},{5,4},{6,7},{7,6},{8,9},{9,8},{10,11... | collective-permute-start | bytes 2433032 | tf_op jit(solution)/shard_map/ppermute | solution.py:165
  29.4 17.4 %collective-permute-start.3 = (bf16[528,768]{1,0:T(8,128)(2,1)}, bf16[528,768]{1,0:T(8,128)(2,1)S(1)}, u32[]{:S(2)}, u32[]{:S(2)}) collective-permute-start(bf16[528,768]{1,0:T(8,128)(2,1)} %get-tuple-element.97.refs_0_), channel_id=1, source_target_pairs={{1,2},{2,1},{5,6},{6,5},{9,10},{10,9},{13,14},{14,13},{17,18},{18,... | collective-permute-start | bytes 2433032 | tf_op jit(solution)/shard_map/ppermute | solution.py:165
  30.7 21.5 %copy-start.43 = (f32[768]{0:T(1024)S(1)}, f32[768]{0:T(1024)}, u32[]{:S(2)}) copy-start(f32[768]{0:T(1024)} %param.29) | copy-start | bytes 9220
  30.7 21.5 %copy-start.44 = (f32[768]{0:T(1024)S(1)}, f32[768]{0:T(1024)}, u32[]{:S(2)}) copy-start(f32[768]{0:T(1024)} %param.30) | copy-start | bytes 9220
  47.9 19.8 %collective-permute-start.4 = (bf16[528,768]{1,0:T(8,128)(2,1)}, bf16[528,768]{1,0:T(8,128)(2,1)S(1)}, u32[]{:S(2)}, u32[]{:S(2)}) collective-permute-start(bf16[528,768]{1,0:T(8,128)(2,1)} %get-tuple-element.101.refs_1_), channel_id=1, source_target_pairs={{0,1},{1,0},{2,3},{3,2},{4,5},{5,4},{6,7},{7,6},{8,9},{9,8},{10,11... | collective-permute-start | bytes 2433032 | tf_op jit(solution)/shard_map/ppermute | solution.py:165
  51.3 16.5 %collective-permute-start.5 = (bf16[528,768]{1,0:T(8,128)(2,1)}, bf16[528,768]{1,0:T(8,128)(2,1)S(1)}, u32[]{:S(2)}, u32[]{:S(2)}) collective-permute-start(bf16[528,768]{1,0:T(8,128)(2,1)} %get-tuple-element.102.refs_0_), channel_id=1, source_target_pairs={{1,2},{2,1},{5,6},{6,5},{9,10},{10,9},{13,14},{14,13},{17,18},{18,... | collective-permute-start | bytes 2433032 | tf_op jit(solution)/shard_map/ppermute | solution.py:165
  122.8 11.8 %collective-permute-start.6 = (bf16[3072,768]{1,0:T(8,128)(2,1)}, bf16[3072,768]{1,0:T(8,128)(2,1)}, u32[]{:S(2)}, u32[]{:S(2)}) collective-permute-start(bf16[3072,768]{1,0:T(8,128)(2,1)} %get-tuple-element.123), channel_id=1, source_target_pairs={{0,4},{4,0},{8,12},{12,8},{16,20},{20,16},{24,28},{28,24},{1,5},{5... | collective-permute-start | bytes 14155784 | tf_op jit(solution)/shard_map/ppermute | solution.py:38
  139.0 31.9 %collective-permute-start.7 = (bf16[1536,768]{1,0:T(8,128)(2,1)}, bf16[1536,768]{1,0:T(8,128)(2,1)S(1)}, u32[]{:S(2)}, u32[]{:S(2)}) collective-permute-start(bf16[1536,768]{1,0:T(8,128)(2,1)} %add_convert_fusion.refs_0_), channel_id=1, source_target_pairs={{0,8},{4,20},{8,0},{12,28},{16,24},{20,4},{24,16},{28,12},{1,9},{5... | collective-permute-start | bytes 7077896 | tf_op jit(solution)/shard_map/ppermute | solution.py:38
  176.1 26.0 %collective-permute-start.8 = (bf16[768,768]{1,0:T(8,128)(2,1)}, bf16[768,768]{1,0:T(8,128)(2,1)S(1)}, u32[]{:S(2)}, u32[]{:S(2)}) collective-permute-start(bf16[768,768]{1,0:T(8,128)(2,1)} %get-tuple-element.130.refs_4_), channel_id=1, source_target_pairs={{0,16},{4,12},{8,24},{12,4},{16,0},{20,28},{24,8},{28,20},{1,17},{... | collective-permute-start | bytes 3538952 | tf_op jit(solution)/shard_map/ppermute | solution.py:38
  177.6 40.1 %collective-permute-start.10 = (bf16[2,512,768]{2,1,0:T(8,128)(2,1)}, bf16[2,512,768]{2,1,0:T(8,128)(2,1)S(1)}, u32[]{:S(2)}, u32[]{:S(2)}) collective-permute-start(bf16[2,512,768]{2,1,0:T(8,128)(2,1)} %get-tuple-element.131.refs_5_), channel_id=1, source_target_pairs={{0,1},{1,0},{2,3},{3,2},{4,5},{5,4},{6,7},{7,6},{8,9},{9,8},{10,11... | collective-permute-start | bytes 4718600 | tf_op jit(solution)/shard_map/ppermute | solution.py:38
  205.3 21.4 %collective-permute-start.9 = (bf16[384,768]{1,0:T(8,128)(2,1)S(1)}, bf16[384,768]{1,0:T(8,128)(2,1)S(1)}, u32[]{:S(2)}, u32[]{:S(2)}) collective-permute-start(bf16[384,768]{1,0:T(8,128)(2,1)S(1)} %add_convert_fusion.4.refs_0_), channel_id=1, source_target_pairs={{0,1},{1,0},{2,3},{3,2},{4,5},{5,4},{6,7},{7,6},{8,9},{9,8},{10,11... | collective-permute-start | bytes 1769480 | tf_op jit(solution)/shard_map/ppermute | solution.py:38
  231.0 19.7 %collective-permute-start.12 = (bf16[1664,768]{1,0:T(8,128)(2,1)}, bf16[1664,768]{1,0:T(8,128)(2,1)}, u32[]{:S(2)}, u32[]{:S(2)}) collective-permute-start(bf16[1664,768]{1,0:T(8,128)(2,1)} %together.31), channel_id=1, source_target_pairs={{0,4},{4,0},{8,12},{12,8},{16,20},{20,16},{24,28},{28,24},{1,5},{5... | collective-permute-start | bytes 7667720 | tf_op jit(solution)/shard_map/ppermute | solution.py:38
  232.0 15.7 %collective-permute-start.11 = (bf16[192,768]{1,0:T(8,128)(2,1)S(1)}, bf16[192,768]{1,0:T(8,128)(2,1)S(1)}, u32[]{:S(2)}, u32[]{:S(2)}) collective-permute-start(bf16[192,768]{1,0:T(8,128)(2,1)S(1)} %copy-done.25), channel_id=1, source_target_pairs={{0,2},{1,3},{2,0},{3,1},{4,6},{5,7},{6,4},{7,5},{8,10},{9,11},{10,... | collective-permute-start | bytes 884744 | tf_op jit(solution)/shard_map/ppermute | solution.py:38
  255.1 17.6 %collective-permute-start.14 = (bf16[832,768]{1,0:T(8,128)(2,1)}, bf16[832,768]{1,0:T(8,128)(2,1)}, u32[]{:S(2)}, u32[]{:S(2)}) collective-permute-start(bf16[832,768]{1,0:T(8,128)(2,1)} %get-tuple-element.144), channel_id=1, source_target_pairs={{0,8},{4,20},{8,0},{12,28},{16,24},{20,4},{24,16},{28,12},{1,9},{5... | collective-permute-start | bytes 3833864 | tf_op jit(solution)/shard_map/ppermute | solution.py:38
  255.6 14.7 %collective-permute-start.13 = (bf16[192,768]{1,0:T(8,128)(2,1)}, bf16[192,768]{1,0:T(8,128)(2,1)S(1)}, u32[]{:S(2)}, u32[]{:S(2)}) collective-permute-start(bf16[192,768]{1,0:T(8,128)(2,1)} %get-tuple-element.143), channel_id=1, source_target_pairs={{0,2},{1,3},{2,0},{3,1},{4,6},{5,7},{6,4},{7,5},{8,10},{9,11},{10,... | collective-permute-start | bytes 884744 | tf_op jit(solution)/shard_map/ppermute | solution.py:38
  277.4 14.4 %collective-permute-start.16 = (bf16[416,768]{1,0:T(8,128)(2,1)}, bf16[416,768]{1,0:T(8,128)(2,1)}, u32[]{:S(2)}, u32[]{:S(2)}) collective-permute-start(bf16[416,768]{1,0:T(8,128)(2,1)} %get-tuple-element.148), channel_id=1, source_target_pairs={{0,16},{4,12},{8,24},{12,4},{16,0},{20,28},{24,8},{28,20},{1,17},{... | collective-permute-start | bytes 1916936 | tf_op jit(solution)/shard_map/ppermute | solution.py:38
  277.9 13.9 %collective-permute-start.15 = (bf16[384,768]{1,0:T(8,128)(2,1)}, bf16[384,768]{1,0:T(8,128)(2,1)}, u32[]{:S(2)}, u32[]{:S(2)}) collective-permute-start(bf16[384,768]{1,0:T(8,128)(2,1)} %get-tuple-element.147), channel_id=1, source_target_pairs={{0,1},{1,0},{2,3},{3,2},{4,5},{5,4},{6,7},{7,6},{8,9},{9,8},{10,11... | collective-permute-start | bytes 1769480 | tf_op jit(solution)/shard_map/ppermute | solution.py:38
  300.0 21.9 %copy-start.6 = (bf16[768,768]{1,0:T(8,128)(2,1)S(1)}, bf16[768,768]{1,0:T(8,128)(2,1)}, u32[]{:S(2)}) copy-start(bf16[768,768]{1,0:T(8,128)(2,1)} %get-tuple-element.153) | copy-start | bytes 3538948
  300.0 20.1 %collective-permute-start.17 = (bf16[768,768]{1,0:T(8,128)(2,1)}, bf16[768,768]{1,0:T(8,128)(2,1)S(1)}, u32[]{:S(2)}, u32[]{:S(2)}) collective-permute-start(bf16[768,768]{1,0:T(8,128)(2,1)} %get-tuple-element.153), channel_id=1, source_target_pairs={{0,16},{4,12},{8,24},{12,4},{16,0},{20,28},{24,8},{28,20},{1,17},{... | collective-permute-start | bytes 3538952 | tf_op jit(solution)/shard_map/ppermute | solution.py:38
  301.3 18.8 %collective-permute-start.19 = (bf16[256,768]{1,0:T(8,128)(2,1)}, bf16[256,768]{1,0:T(8,128)(2,1)S(1)}, u32[]{:S(2)}, u32[]{:S(2)}) collective-permute-start(bf16[256,768]{1,0:T(8,128)(2,1)} %get-tuple-element.155), channel_id=1, source_target_pairs={{0,2},{1,3},{2,0},{3,1},{4,6},{5,7},{6,4},{7,5},{8,10},{9,11},{10,... | collective-permute-start | bytes 1179656 | tf_op jit(solution)/shard_map/ppermute | solution.py:38
  302.1 14.0 %collective-permute-start.18 = (bf16[208,768]{1,0:T(8,128)(2,1)}, bf16[208,768]{1,0:T(8,128)(2,1)S(1)}, u32[]{:S(2)}, u32[]{:S(2)}) collective-permute-start(bf16[208,768]{1,0:T(8,128)(2,1)} %get-tuple-element.154), channel_id=1, source_target_pairs={{0,1},{1,0},{2,3},{3,2},{4,5},{5,4},{6,7},{7,6},{8,9},{9,8},{10,11... | collective-permute-start | bytes 958472 | tf_op jit(solution)/shard_map/ppermute | solution.py:38
  326.9 46.4 %collective-permute-start.24 = (bf16[1536,768]{1,0:T(8,128)(2,1)}, bf16[1536,768]{1,0:T(8,128)(2,1)S(1)}, u32[]{:S(2)}, u32[]{:S(2)}) collective-permute-start(bf16[1536,768]{1,0:T(8,128)(2,1)} %get-tuple-element.162), channel_id=1, source_target_pairs={{0,8},{4,20},{8,0},{12,28},{16,24},{20,4},{24,16},{28,12},{1,9},{5... | collective-permute-start | bytes 7077896 | tf_op jit(solution)/shard_map/ppermute | solution.py:38
  327.3 18.8 %collective-permute-start.20 = (bf16[104,768]{1,0:T(8,128)(2,1)}, bf16[104,768]{1,0:T(8,128)(2,1)S(1)}, u32[]{:S(2)}, u32[]{:S(2)}) collective-permute-start(bf16[104,768]{1,0:T(8,128)(2,1)} %get-tuple-element.159), channel_id=1, source_target_pairs={{0,2},{1,3},{2,0},{3,1},{4,6},{5,7},{6,4},{7,5},{8,10},{9,11},{10,... | collective-permute-start | bytes 479240 | tf_op jit(solution)/shard_map/ppermute | solution.py:38
  327.3 34.0 %collective-permute-start.22 = (bf16[256,768]{1,0:T(8,128)(2,1)}, bf16[256,768]{1,0:T(8,128)(2,1)S(1)}, u32[]{:S(2)}, u32[]{:S(2)}) collective-permute-start(bf16[256,768]{1,0:T(8,128)(2,1)} %get-tuple-element.160), channel_id=1, source_target_pairs={{0,2},{1,3},{2,0},{3,1},{4,6},{5,7},{6,4},{7,5},{8,10},{9,11},{10,... | collective-permute-start | bytes 1179656 | tf_op jit(solution)/shard_map/ppermute | solution.py:38
  347.5 13.9 %collective-permute-start.21 = (bf16[104,768]{1,0:T(8,128)(2,1)S(1)}, bf16[104,768]{1,0:T(8,128)(2,1)S(1)}, u32[]{:S(2)}, u32[]{:S(2)}) collective-permute-start(bf16[104,768]{1,0:T(8,128)(2,1)S(1)} %add_convert_fusion.8), channel_id=1, source_target_pairs={{0,2},{1,3},{2,0},{3,1},{4,6},{5,7},{6,4},{7,5},{8,10},{9,11},{10,... | collective-permute-start | bytes 479240 | tf_op jit(solution)/shard_map/ppermute | solution.py:38
  363.8 9.6 %collective-permute-start.23 = (bf16[208,768]{1,0:T(8,128)(2,1)S(1)}, bf16[208,768]{1,0:T(8,128)(2,1)S(1)}, u32[]{:S(2)}, u32[]{:S(2)}) collective-permute-start(bf16[208,768]{1,0:T(8,128)(2,1)S(1)} %maximum_select_fusion.7), channel_id=1, source_target_pairs={{0,1},{1,0},{2,3},{3,2},{4,5},{5,4},{6,7},{7,6},{8,9},{9,8},{10,11... | collective-permute-start | bytes 958472 | tf_op jit(solution)/shard_map/ppermute | solution.py:38
  381.0 11.8 %collective-permute-start.27 = (bf16[3072,768]{1,0:T(8,128)(2,1)S(1)}, bf16[3072,768]{1,0:T(8,128)(2,1)}, u32[]{:S(2)}, u32[]{:S(2)}) collective-permute-start(bf16[3072,768]{1,0:T(8,128)(2,1)S(1)} %maximum_select_fusion.mine_ref), channel_id=1, source_target_pairs={{0,4},{4,0},{8,12},{12,8},{16,20},{20,16},{24,28},{28,24},{1,5},{5... | collective-permute-start | bytes 14155784 | tf_op jit(solution)/shard_map/ppermute | solution.py:38
  381.3 10.5 %collective-permute-start.25 = (bf16[416,768]{1,0:T(8,128)(2,1)S(1)}, bf16[416,768]{1,0:T(8,128)(2,1)S(1)}, u32[]{:S(2)}, u32[]{:S(2)}) collective-permute-start(bf16[416,768]{1,0:T(8,128)(2,1)S(1)} %maximum_select_fusion.5), channel_id=1, source_target_pairs={{0,16},{4,12},{8,24},{12,4},{16,0},{20,28},{24,8},{28,20},{1,17},{... | collective-permute-start | bytes 1916936 | tf_op jit(solution)/shard_map/ppermute | solution.py:38
  392.3 17.3 %collective-permute-start.26 = (bf16[832,768]{1,0:T(8,128)(2,1)S(1)}, bf16[832,768]{1,0:T(8,128)(2,1)S(1)}, u32[]{:S(2)}, u32[]{:S(2)}) collective-permute-start(bf16[832,768]{1,0:T(8,128)(2,1)S(1)} %maximum_select_fusion.3), channel_id=1, source_target_pairs={{0,8},{4,20},{8,0},{12,28},{16,24},{20,4},{24,16},{28,12},{1,9},{5... | collective-permute-start | bytes 3833864 | tf_op jit(solution)/shard_map/ppermute | solution.py:38
  413.5 5.0 %collective-permute-start.28 = (bf16[1664,768]{1,0:T(8,128)(2,1)S(1)}, bf16[1664,768]{1,0:T(8,128)(2,1)}, u32[]{:S(2)}, u32[]{:S(2)}) collective-permute-start(bf16[1664,768]{1,0:T(8,128)(2,1)S(1)} %maximum_select_fusion.1.mine_ref.half_mine.low_mine), channel_id=1, source_target_pairs={{0,4},{4,0},{8,12},{12,8},{16,20},{20,16},{24,28},{28,24},{1,5},{5... | collective-permute-start | bytes 7667720 | tf_op jit(solution)/shard_map/ppermute | solution.py:38
  (42 other events, 204.6 us)

commit v2 on v1

--- a/solution.py
+++ b/solution.py
@@ -71,11 +71,6 @@
     return [lax.dynamic_slice_in_dim(t, mine * rows, rows, 0) for t in terms] + [came]
 
 
-def split(value):
-    half = value.shape[0] // 2
-    return value[:half], value[half:]
-
-
 def total_of(terms):
     total = terms[0].astype(F32)
     for term in terms[1:]:
@@ -91,19 +86,25 @@
     )
 
 
-def sum_everywhere(terms):
+def sum_everywhere(terms, merge=False):
     core, chips = stages_of("batch")[0], stages_of("batch")[1:]
     plane = [(axis, one, two) for (axis, one), (_, two) in zip(chips, chips[::-1])]
-    order = plane + stages_of("seq")
+    line = stages_of("seq")
+    order = plane + (line[:-1] if merge else line)
     for stage in order:
         came, _ = yield part_of(terms, 1 - bit_of(stage), 2), stage
         terms = rest_of(terms, stage, came)
     value = total_of(terms)
-    for stage in order[::-1]:
+    if merge:
+        came, value = yield value, line[-1]
+        value = total_of([value, came])
+    for stage in order[:0:-1]:
         came, value = yield value, stage
         value = joined(value, came, stage)
-    came, value = yield value, core
-    return value, came
+    came, value = yield value, order[0]
+    other = swap(value, core)
+    other_came, came = yield came, core
+    return value, came, other, other_came
 
 
 def line_scatter(sent):
@@ -117,15 +118,17 @@
         kept = lax.dynamic_index_in_dim(pairs, mine, 1, keepdims=False)
         if bit + 1 < len(stages):
             came, _ = yield sent, (axis, bit)
-    parts = []
-    for part in split(sent[0]):
-        parts.append((yield part, stages[-1])[0])
-    return kept[0] + jnp.concatenate(parts, axis=0).astype(F32)
+    rows = sent.shape[1]
+    came = []
+    for begin, end in ((0, rows // 4), (rows // 4, rows // 2), (rows // 2, rows)):
+        came.append((yield sent[0, begin:end], stages[-1])[0])
+    return kept[0], came
 
 
 class Exchanges:
     def __init__(self):
         self.chains, self.came, self.sent, self.results = {}, {}, {}, {}
+        self.latest = []
 
     def add(self, name, chain):
         self.chains[name] = chain
@@ -135,6 +138,7 @@
         waiting = [n for n in names if n in self.came]
         landing = waiting + list(land)
         if landing:
+            late = list(late) or self.latest
             self.came.update(zip(landing, together([self.came[n] for n in landing], late)))
         next_sent, stages = {}, {}
         for name in names:
@@ -151,7 +155,8 @@
         next_sent = dict(zip(next_sent, together(list(next_sent.values()))))
         for name, value in next_sent.items():
             self.sent[name], self.came[name] = value, swap(value, stages[name])
-        return list(next_sent.values())
+        self.latest = list(next_sent.values())
+        return self.latest
 
 
 def line_steps(block):
@@ -642,7 +647,7 @@
 def ffn_kernel(
     chunks, core_ref, o_ref, x_ref, g_ref, wo_ref, up_ref, down_ref, bup_ref, vec_ref,
     out_ref, keep_ref, give_ref, dh2_ref, du_ref, n1_ref, r1_ref, sums_ref,
-    y1, low, act, slope, h2, dh2_low,
+    y1, low, ahead, act, slope, h2, dh2_low,
 ):
     step = pl.program_id(0)
     b_out, gain1, bias1, b_down, gain2, bias2 = (vec_ref[i : i + 1] for i in range(6))
@@ -657,23 +662,29 @@
         y1[...] = value
         low[...] = value.astype(BF)
 
-    @pl.when(step < chunks)
-    def _():
-        value, rate = gelu_both(dot(low[...], up_ref[...]) + bup_ref[0])
-        act[step] = value.astype(BF)
-        slope[step] = rate
-        product = dot(act[step], down_ref[...])
-
-        @pl.when(step == 0)
-        def _():
-            h2[...] = y1[...] + b_down + product
-
-        @pl.when(step > 0)
-        def _():
-            h2[...] += product
-
-    @pl.when(step == chunks - 1)
-    def _():
+    def up_product():
+        ahead[step % 2] = dot(low[...], up_ref[...]) + bup_ref[0]
+
+    def down_product():
+        value, rate = gelu_both(ahead[(step - 1) % 2])
+        value = value.astype(BF)
+        act[step - 1] = value
+        slope[step - 1] = rate
+        h2[...] += dot(value, down_ref[...])
+
+    @pl.when(step == 0)
+    def _():
+        h2[...] = y1[...] + b_down
+        up_product()
+
+    @pl.when(jnp.logical_and(step > 0, step < chunks))
+    def _():
+        up_product()
+        down_product()
+
+    @pl.when(step == chunks)
+    def _():
+        down_product()
         normed, rstd = normalise(h2[...])
         out_ref[...] = (normed * gain2 + bias2).astype(BF)
         grad = g_ref[...].astype(F32)
@@ -685,9 +696,9 @@
         sums_ref[1:2] = column_sum(grad * normed)
         sums_ref[2:3] = column_sum(grad)
 
-    @pl.when(step >= chunks)
-    def _():
-        chunk = 2 * chunks - 1 - step
+    @pl.when(step > chunks)
+    def _():
+        chunk = 2 * chunks - step
         d_u = dot(dh2_low[...], down_ref[...], ((1,), (1,))) * slope[chunk]
         sums_ref[pl.ds(8 + chunk, 1)] = column_sum(d_u)
         d_u = d_u.astype(BF)
@@ -714,10 +725,10 @@
         return jnp.minimum(i, chunks - 1)
 
     def both(i):
-        return jnp.where(i < chunks, i, 2 * chunks - 1 - i)
+        return jnp.where(i <= chunks, jnp.maximum(i - 1, 0), 2 * chunks - i)
 
     def back(i):
-        return jnp.minimum(2 * chunks - 1 - i, chunks - 1)
+        return jnp.minimum(2 * chunks - i, chunks - 1)
 
     rows_spec = full((rows, width))
     share = pl.BlockSpec((width, width), lambda i, _: (back(i), 0))
@@ -726,7 +737,7 @@
         functools.partial(ffn_kernel, chunks),
         grid_spec=pltpu.PrefetchScalarGridSpec(
             num_scalar_prefetch=1,
-            grid=(2 * chunks,),
+            grid=(2 * chunks + 1,),
             in_specs=[
                 rows_spec,
                 rows_spec,
@@ -750,6 +761,7 @@
             scratch_shapes=[
                 pltpu.VMEM((rows, width), F32),
                 pltpu.VMEM((rows, width), BF),
+                pltpu.VMEM((2, rows, width), F32),
                 pltpu.VMEM((chunks, rows, width), BF),
                 pltpu.VMEM((chunks, rows, width), F32),
                 pltpu.VMEM((rows, width), F32),
@@ -834,25 +846,39 @@
     )(o_low, dh2, du, n1, r1, w_up, w_out, gain, sums_two)
 
 
-def place_ffn_kernel(core_ref, mine_ref, other_ref, down_ref, up_ref):
-    for core in range(2):
-
-        @pl.when(core_ref[0] == core)
-        def _():
-            down_ref[...] = (mine_ref, other_ref)[core][...].astype(F32)
-            up_ref[...] = (other_ref, mine_ref)[core][...].astype(F32)
-
-
-def place_ffn(core, wide, mine, other):
-    width = mine.shape[1]
-    block = pl.BlockSpec((width, width), lambda i, _: (i, 0))
+def place_ffn_kernel(at_ref, *refs):
+    mine, other, (down_ref, up_ref) = refs[0:2], refs[2:4], refs[4:]
+    for late in range(2):
+        for core in range(2):
+
+            @pl.when(
+                jnp.logical_and(at_ref[0] == core, (pl.program_id(0) >= 2) == bool(late))
+            )
+            def _():
+                down_ref[...] = (mine, other)[core][late][...].astype(F32)
+                up_ref[...] = (other, mine)[core][late][...].astype(F32)
+
+
+def place_ffn(wide, pieces):
+    width = pieces[0].shape[1]
+    chips = stages_of("batch")[1:]
+    bits = [bit_of(stage) for stage in (stages_of("batch")[0], chips[0], chips[-1])]
+    early = pl.BlockSpec((width, width), lambda i, _: (jnp.minimum(i, 1), 0))
+    late = pl.BlockSpec((width, width), lambda i, _: (jnp.maximum(i - 2, 0), 0))
+
+    def block(i, bit):
+        return 2 * jnp.where(i < 2, bit, 1 - bit) + i % 2
+
     return pl.pallas_call(
         place_ffn_kernel,
         grid_spec=pltpu.PrefetchScalarGridSpec(
             num_scalar_prefetch=1,
-            grid=(wide // width,),
-            in_specs=[block, block],
-            out_specs=[block, pl.BlockSpec((width, width), lambda i, _: (0, i))],
+            grid=(4,),
+            in_specs=[early, late, early, late],
+            out_specs=[
+                pl.BlockSpec((width, width), lambda i, at: (block(i, at[1]), 0)),
+                pl.BlockSpec((width, width), lambda i, at: (0, block(i, at[2]))),
+            ],
         ),
         out_shape=[
             jax.ShapeDtypeStruct((wide, width), F32),
@@ -860,62 +886,80 @@
         ],
         name="place_ffn",
         **params(0, 16 * wide * width),
-    )(core, mine, other)
+    )(jnp.stack(bits).astype(jnp.int32), *pieces)
 
 
 def place_attn_kernel(
-    core_ref, mine_ref, other_ref, half_mine, half_other, low_mine, low_other,
-    out_ref, dwo_ref, small_ref,
+    at_ref, mine, mine_came, other, other_came, kept_ref, *refs
 ):
-    half = half_mine.shape[0]
+    came, (out_ref, dwo_ref, small_ref, dx_ref) = refs[:-4], refs[-4:]
+    width = dwo_ref.shape[0]
+    half = width // 2
+    rows = mine.shape[0]
     step = pl.program_id(0)
-    for core in range(2):
-        mine = core_ref[0] == core
-
-        for at, ref in ((0, out_ref), (1, dwo_ref)):
-
-            @pl.when(jnp.logical_and(mine, step == at))
-            def _():
-                ref[:half] = (half_mine, half_other)[core][...].astype(F32)
-                ref[half:] = (half_other, half_mine)[core][...].astype(F32)
-
-        @pl.when(jnp.logical_and(mine, step == 0))
-        def _():
-            small_ref[...] = (low_mine, low_other)[core][...].astype(F32)
-
-        for which in range(2):
-
-            @pl.when(jnp.logical_and(mine, step == 1 + which))
-            def _():
-                out_ref[...] = (mine_ref, other_ref)[(core + which) % 2][...].astype(F32)
-
-
-def place_attn(core, mine, other):
-    width = mine.shape[1]
-    half = width // 2
-    block = whole_spec((width, width))
-    halves = pl.BlockSpec((half, width), lambda i, _: (2 + jnp.minimum(i, 1), 0))
-    low = pl.BlockSpec((EXTRA, width), lambda i, _: (2 * width // EXTRA, 0))
+
+    def part(core, begin, end):
+        h = begin // rows
+        at = slice(begin - h * rows, end - h * rows)
+        own = jnp.where(at_ref[1] == h, mine[at], mine_came[at])
+        far = jnp.where(at_ref[2] == h, other[at], other_came[at])
+        return jnp.where(at_ref[0] == core, own, far).astype(F32)
+
+    def write(ref, at, core, begin, end):
+        cuts = sorted({begin, end} | ({rows} if begin < rows < end else set()))
+        for low, high in zip(cuts, cuts[1:]):
+            ref[at + low - begin : at + high - begin] = part(core, low, high)
+
+    @pl.when(step == 0)
+    def _():
+        write(out_ref, 0, 0, width, width + half)
+        write(out_ref, half, 1, width, width + half)
+        write(small_ref, 0, 0, 2 * width, 2 * width + EXTRA)
+
+    @pl.when(step == 1)
+    def _():
+        write(out_ref, 0, 0, 0, width)
+        write(dwo_ref, 0, 0, width + half, 2 * width)
+        write(dwo_ref, half, 1, width + half, 2 * width)
+
+    @pl.when(step == 2)
+    def _():
+        write(out_ref, 0, 1, 0, width)
+        begin = 0
+        for ref in came:
+            at = slice(begin, begin + ref.shape[0])
+            dx_ref[at] = kept_ref[at] + ref[...].astype(F32)
+            begin = at.stop
+
+
+def place_attn(pieces, kept, came):
+    width = kept.shape[1]
+    chips = stages_of("batch")[1:]
+    core, one, two = (bit_of(stage) for stage in (stages_of("batch")[0], chips[0], chips[-1]))
+    at = jnp.stack([core, jnp.where(core == 0, one, two), jnp.where(core == 0, two, one)])
+    operands = [*pieces, kept, *came]
     return pl.pallas_call(
         place_attn_kernel,
         grid_spec=pltpu.PrefetchScalarGridSpec(
             num_scalar_prefetch=1,
             grid=(3,),
-            in_specs=[block, block, halves, halves, low, low],
+            in_specs=[whole_spec(v.shape) for v in operands],
             out_specs=[
                 pl.BlockSpec((width, width), lambda i, _: (0, i)),
                 whole_spec((width, width)),
                 whole_spec((EXTRA, width)),
+                whole_spec(kept.shape),
             ],
         ),
         out_shape=[
             jax.ShapeDtypeStruct((width, 3 * width), F32),
             jax.ShapeDtypeStruct((width, width), F32),
             jax.ShapeDtypeStruct((EXTRA, width), F32),
+            jax.ShapeDtypeStruct(kept.shape, F32),
         ],
         name="place_attn",
         **params(0, 24 * width * width),
-    )(core, mine, other, mine, other, mine, other)
+    )(at.astype(jnp.int32), *operands)
 
 
 def per_device(
@@ -1013,25 +1057,26 @@
     attn_came = swap(*together([attn_give], sent), core)
     d_x_kept = input_grad(True, here_at, d_key, d_value, w_qkv, [d_query, d_first], sent)
     attn_came = together([attn_came], [d_x_kept])
-    exchanges.add("attn", sum_everywhere([attn_kept, *attn_came]))
+    exchanges.add("attn", sum_everywhere([attn_kept, *attn_came], merge=True))
     both = ["ffn", "attn"]
     exchanges.go(both, [d_x_kept])
     exchanges.go(both)
-    exchanges.go(both + ["input"], kept=d_x_kept)
-    exchanges.go(both + ["input"])
     exchanges.go(["attn"])
-    exchanges.go(["attn"], land=["input"])
-    exchanges.go(["attn"], land=["ffn"])
-    exchanges.go(["ffn", "input"])
+    exchanges.go(["ffn", "input"], kept=d_x_kept)
+    exchanges.go(both, land=["input"])
     exchanges.go(["attn"])
+    exchanges.go(["attn", "input"], land=["ffn"])
+    exchanges.go(["ffn"])
+    exchanges.go(["attn", "input"])
     while "ffn" not in exchanges.results:
         exchanges.go(["ffn"])
-    d_w_down, d_w_up = place_ffn(core_bit, w_up.shape[1], *exchanges.results["ffn"])
-    exchanges.go(["attn"], [d_w_down])
+    d_w_down, d_w_up = place_ffn(w_up.shape[1], exchanges.results["ffn"])
+    exchanges.go(["attn"], [d_w_down], land=["input"])
     while len(exchanges.results) < 3:
         exchanges.go(["attn", "input"])
-    d_input = exchanges.results["input"]
-    d_w_qkv, d_w_out, small = place_attn(core_bit, *exchanges.results["attn"])
+    d_w_qkv, d_w_out, small, d_input = place_attn(
+        exchanges.results["attn"], *exchanges.results["input"]
+    )
     chunks = w_up.shape[1] // width
     d_b_down, d_ln2_gain, d_ln2_bias = (small[i] for i in range(3))
     d_b_up = small[8 : 8 + chunks].reshape(-1)

time: 435 us -> 417 us (0.959)
  waiting for transfers between devices: 143 us -> 122 us
  other arithmetic: 52.9 us -> 46.3 us
  local copies, waits for them, and re-layouts: 25.1 us -> 31 us
    ppermute x23 -> x25, waiting for transfers between devices: 118 us -> 97 us  [swap(): lax.ppermute(value, stage[0], [(i, i ^ 1 << bits[i % 2]) for i in range(c...]
    squeeze x0 -> x3, local copies, waits for them, and re-layouts: none -> 5.19 us  [the longest x1 2.64 us: line_scatter(): return (kept[0], came)]
    select_n x8 -> x5, other arithmetic: 16.4 us -> 12 us  [joined(): jnp.where(bit_of(stage) == 0, jnp.concatenate([mine, other], axis=0), jnp...]
    convert_element_type x8 -> x7, other arithmetic: 22 us -> 20.2 us  [part_of(): return total.astype(BF)]
    unnamed x90 -> x102, local copies, waits for them, and re-layouts: 19.9 us -> 21.4 us
    ppermute x23 -> x25, starting transfers between devices: 16.6 us -> 17.1 us  [swap(): lax.ppermute(value, stage[0], [(i, i ^ 1 << bits[i % 2]) for i in range(c...]
  transfers between devices with their start and end apart: 29 -> 31, of which waited for: 16 -> 17; matrix products, arithmetic and copies ran while one was open for 4% -> 5% of each run, Pallas kernels for 27% -> 29%
where the time goes in v2:
time: 417 us; the launch traced here: 410 us
  Pallas kernels  179 us (43%)
  waiting for transfers between devices  122 us (29%)
  other arithmetic  46.3 us (11%)
  local copies, waits for them, and re-layouts  31 us (7%)
  starting transfers between devices  30.2 us (7%)
    ppermute x25, waiting for transfers between devices, swap(): lax.ppermute(value, stage[0], [(i, i ^ 1 << bits[i % 2]) for i in range(c...  97 us
    pallas_call x2, Pallas kernels, attend_back(): pl.pallas_call(functools.partial(attend_back_kernel, final, scale, pairs,...  46 us
    pallas_call x1, Pallas kernels, ffn(): pl.pallas_call(functools.partial(ffn_kernel, chunks), grid_spec=pltpu.Pre...  27.5 us
    pallas_call x4, Pallas kernels, project(): pl.pallas_call(functools.partial(project_kernel, first, rows), grid_spec=...  27.2 us
    ppermute x3, waiting for transfers between devices, line_steps(): lax.ppermute(two, 'seq', pairs[0])  24.5 us
    unnamed x102, local copies, waits for them, and re-layouts  21.4 us
    convert_element_type x7, other arithmetic, part_of(): return total.astype(BF)  20.2 us
    pallas_call x1, Pallas kernels, attend(): pl.pallas_call(functools.partial(attend_kernel, scale, 256), grid=(pairs,...  19.3 us
  transfers between devices with their start and end apart: 31, of which 17 were waited for; matrix products, arithmetic and copies ran while one was open for 5% of the time, Pallas kernels for 29%

profile of v2, /device:TPU:0, one launch (start us, length us, event | category | flops | bytes accessed | tf_op | source)
XLA Modules:
  0.0 409.9 jit_solution(16012360496001922872)
XLA Ops:
  2.6 3.1 collective-permute-start
  8.3 7.4 %project.4 = (bf16[2048,768]{1,0:T(8,128)(2,1)}, bf16[2048,1664]{1,0:T(8,128)(2,1)}, bf16[512,768]{1,0:T(8,128)(2,1)}, bf16[512,128]{1,0:T(8,128)(2,1)}, f32[8,128]{1,0:T(8,128)}) custom-call(s32[4]{0:T(128)} %pad_add_fusion.place_ref, bf16[528,768]{1,0:T(8,128)(2,1)} %copy-done.18, bf16[768,2304]{1,0:T(8,128)(2,1)} %w_ref.3, bf16[768,2304]{1,0:T(8,128)(2,1)} %w_ref.3, ...), custom_call_target="tpu_custom_call" | custom-call | flops 603979776 | bytes 3145728 | tf_op jit(solution)/shard_map/project/pallas_call | solution.py:299
  15.7 8.0 %collective-permute-done.refs_0_ = bf16[528,768]{1,0:T(8,128)(2,1)S(1)} collective-permute-done((bf16[528,768]{1,0:T(8,128)(2,1)S(1)}, bf16[528,768]{1,0:T(8,128)(2,1)S(1)}, u32[]{:S(2)}, u32[]{:S(2)}) %collective-permute-start) | collective-permute-done | bytes 811040 | tf_op jit(solution)/shard_map/ppermute | solution.py:170
  24.9 4.5 %collective-permute-start.2 = (bf16[528,768]{1,0:T(8,128)(2,1)}, bf16[528,768]{1,0:T(8,128)(2,1)S(1)}, u32[]{:S(2)}, u32[]{:S(2)}) collective-permute-start(bf16[528,768]{1,0:T(8,128)(2,1)} %get-tuple-element.101.refs_1_), channel_id=1, source_target_pairs={{0,1},{1,0},{2,3},{3,2},{4,5},{5,4},{6,7},{7,6},{8,9},{9,8},{10,11... | collective-permute-start | bytes 2433032 | tf_op jit(solution)/shard_map/ppermute | solution.py:170
  30.7 6.7 %project.5 = (bf16[2048,768]{1,0:T(8,128)(2,1)}, bf16[2048,1664]{1,0:T(8,128)(2,1)}, f32[8,128]{1,0:T(8,128)}) custom-call(s32[4]{0:T(128)} %pad_add_fusion.2.place_ref, bf16[528,768]{1,0:T(8,128)(2,1)} %get-tuple-element.102.refs_0_, bf16[528,768]{1,0:T(8,128)(2,1)} %get-tuple-element.101.refs_1_, ...), custom_call_target="tpu_custom_call", output_to_operand_aliasing={{0}: (7, {}), {1}: (8, {})} | custom-call | flops 1207959552 | bytes 3145728 | tf_op jit(solution)/shard_map/project/pallas_call | solution.py:299
  37.4 9.3 %collective-permute-done.2.refs_0_ = bf16[528,768]{1,0:T(8,128)(2,1)S(1)} collective-permute-done((bf16[528,768]{1,0:T(8,128)(2,1)}, bf16[528,768]{1,0:T(8,128)(2,1)S(1)}, u32[]{:S(2)}, u32[]{:S(2)}) %collective-permute-start.2) | collective-permute-done | bytes 811040 | tf_op jit(solution)/shard_map/ppermute | solution.py:170
  47.9 3.4 collective-permute-start.4
  54.0 6.6 %project.6 = (bf16[2048,768]{1,0:T(8,128)(2,1)}, bf16[2048,1664]{1,0:T(8,128)(2,1)}, f32[8,128]{1,0:T(8,128)}) custom-call(s32[4]{0:T(128)} %pad_add_fusion.3.place_ref, bf16[528,768]{1,0:T(8,128)(2,1)} %get-tuple-element.107.refs_0_, bf16[528,768]{1,0:T(8,128)(2,1)} %get-tuple-element.106.refs_1_, ...), custom_call_target="tpu_custom_call", output_to_operand_aliasing={{0}: (7, {}), {1}: (8, {})} | custom-call | flops 1207959552 | bytes 3145728 | tf_op jit(solution)/shard_map/project/pallas_call | solution.py:299
  60.6 7.2 %collective-permute-done.4.refs_0_ = bf16[528,768]{1,0:T(8,128)(2,1)S(1)} collective-permute-done((bf16[528,768]{1,0:T(8,128)(2,1)}, bf16[528,768]{1,0:T(8,128)(2,1)S(1)}, u32[]{:S(2)}, u32[]{:S(2)}) %collective-permute-start.4) | collective-permute-done | bytes 811040 | tf_op jit(solution)/shard_map/ppermute | solution.py:170
  68.9 6.6 %project.7 = (bf16[2048,768]{1,0:T(8,128)(2,1)}, bf16[2048,1664]{1,0:T(8,128)(2,1)}, f32[8,128]{1,0:T(8,128)}) custom-call(s32[4]{0:T(128)} %pad_add_fusion.1.place_ref, bf16[528,768]{1,0:T(8,128)(2,1)} %get-tuple-element.111.refs_0_, bf16[528,768]{1,0:T(8,128)(2,1)} %get-tuple-element.112.refs_1_, ...), custom_call_target="tpu_custom_call", output_to_operand_aliasing={{0}: (7, {}), {1}: (8, {})} | custom-call | flops 1207959552 | bytes 3145728 | tf_op jit(solution)/shard_map/project/pallas_call | solution.py:299
  75.5 19.3 %attend.1 = (f32[512,768]{1,0:T(8,128)}, bf16[512,768]{1,0:T(8,128)(2,1)}, f32[6,8,512]{2,1,0:T(8,128)}) custom-call(bf16[512,768]{1,0:T(8,128)(2,1)} %get-tuple-element.99.q_ref, bf16[2048,1664]{1,0:T(8,128)(2,1)} %get-tuple-element.115.k_ref.v_ref.kh_ref, bf16[2048,1664]{1,0:T(8,128)(2,1)} %get-tuple-element.115.k_ref.v_ref.kh_ref, ...), custom_call_target="tpu_custom_call" | custom-call | flops 3221225472 | bytes 12582912 | tf_op jit(solution)/shard_map/attend/pallas_call | solution.py:361
  94.8 27.5 %ffn.1 = (bf16[512,768]{1,0:T(8,128)(2,1)}, bf16[3072,768]{1,0:T(8,128)(2,1)}, bf16[3072,768]{1,0:T(8,128)(2,1)}, f32[512,768]{1,0:T(8,128)}, bf16[512,3072]{1,0...) custom-call(s32[1]{0:T(128)} %bitcast.core_ref, ...), custom_call_target="tpu_custom_call" | custom-call | flops 13287555072 | bytes 28311552 | tf_op jit(solution)/shard_map/ffn/pallas_call | solution.py:736
  122.4 11.9 %norm_one.1 = (f32[512,768]{1,0:T(8,128)}, bf16[512,768]{1,0:T(8,128)(2,1)}, bf16[768,768]{1,0:T(8,128)(2,1)}, f32[24,768]{1,0:T(8,128)}) custom-call(bf16[512,768]{1,0:T(8,128)(2,1)} %get-tuple-element.117.o_ref, f32[512,768]{1,0:T(8,128)} %get-tuple-element.121.dh2_ref, bf16[512,3072]{1,0:T(8,128)(2,1)} %get-tuple-element.122.du_ref, ...), custom_call_target="tpu_custom_call" | custom-call | flops 3623878656 | bytes 4718592 | tf_op jit(solution)/shard_map/norm_one/pallas_call | solution.py:822
  134.3 4.4 %add_convert_fusion.refs_0_ = bf16[1536,768]{1,0:T(8,128)(2,1)} fusion(bf16[3072,768]{1,0:T(8,128)(2,1)} %together.31, s32[]{:T(128)S(6)} %select_n.208, bf16[3072,768]{1,0:T(8,128)(2,1)} %get-tuple-element.119), kind=kLoop, calls=%fused_computation | loop fusion | flops 4718592 | bytes 7077892 | tf_op jit(solution)/shard_map/convert_element_type | solution.py:65
  140.8 22.7 %attend_back.2 = (f32[512,768]{1,0:T(8,128)}, f32[8,768]{1,0:T(8,128)}, bf16[2048,768]{1,0:T(8,128)(2,1)}, bf16[2048,768]{1,0:T(8,128)(2,1)}, f32[8,128]{1,0:T(8,128)}) custom-call(s32[2]{0:T(128)} %pad_add_fusion.5.at_ref, bf16[512,768]{1,0:T(8,128)(2,1)} %get-tuple-element.99.q_ref, bf16[2048,1664]{1,0:T(8,128)(2,1)} %get-tuple-element.115.k_ref.v_ref.kh_ref, ...), custom_call_target="tpu_custom_call" | custom-call | flops 8053063680 | bytes 12582912 | tf_op jit(solution)/shard_map/attend_back/pallas_call | solution.py:475
  163.5 6.9 %input_grad.2.refs_1_ = bf16[2,512,768]{2,1,0:T(8,128)(2,1)} custom-call(s32[2]{0:T(128)} %pad_add_fusion.5.at_ref, bf16[2048,768]{1,0:T(8,128)(2,1)} %get-tuple-element.130.dk_ref.refs_2_, bf16[2048,768]{1,0:T(8,128)(2,1)} %get-tuple-element.131.dv_ref.refs_3_, bf16[768,2304]{1,0:T(8,128)(2,1)} %w_ref.3, f32[8,128]{1,0:T(8,128)} %get-tuple-element.132.refs_0_), custom_call_target="tpu_custom_call" | custom-call | flops 2415919104 | bytes 6291456 | tf_op jit(solution)/shard_map/input_grad/pallas_call | solution.py:604
  171.8 3.7 add_convert_fusion.2.refs_0_
  178.2 23.3 %attend_back.3 = (bf16[512,768]{1,0:T(8,128)(2,1)}, f32[8,768]{1,0:T(8,128)}, bf16[2048,768]{1,0:T(8,128)(2,1)}, bf16[2048,768]{1,0:T(8,128)(2,1)}, f32[8,128]{1,0:T(8,128)}) custom-call(s32[2]{0:T(128)} %pad_add_fusion.5.at_ref, bf16[512,768]{1,0:T(8,128)(2,1)} %get-tuple-element.99.q_ref, ...), custom_call_target="tpu_custom_call", output_to_operand_aliasing={{2}: (11, {}), {3}: (12, {})} | custom-call | flops 8053063680 | bytes 12582912 | tf_op jit(solution)/shard_map/attend_back/pallas_call | solution.py:475
  205.6 11.4 %projection.1 = (bf16[1664,768]{1,0:T(8,128)(2,1)}, bf16[1664,768]{1,0:T(8,128)(2,1)}) custom-call(s32[1]{0:T(128)} %bitcast.core_ref, bf16[512,768]{1,0:T(8,128)(2,1)} %bitcast.36, bf16[2048,768]{1,0:T(8,128)(2,1)} %get-tuple-element.138.whole_ref, bf16[512,768]{1,0:T(8,128)(2,1)} %get-tuple-element.139.dq_ref.refs_0_, ...), custom_call_target="tpu_custom_call" | custom-call | flops 4831838208 | bytes 12582912 | tf_op jit(solution)/shard_map/projection/pallas_call | solution.py:557
  217.0 9.1 %collective-permute-done.9.refs_0_ = bf16[384,768]{1,0:T(8,128)(2,1)S(1)} collective-permute-done((bf16[384,768]{1,0:T(8,128)(2,1)S(1)}, bf16[384,768]{1,0:T(8,128)(2,1)S(1)}, u32[]{:S(2)}, u32[]{:S(2)}) %collective-permute-start.9) | collective-permute-done | bytes 589856 | tf_op jit(solution)/shard_map/ppermute | solution.py:38
  233.1 9.0 %input_grad.3.refs_1_ = f32[2,512,768]{2,1,0:T(8,128)} custom-call(s32[2]{0:T(128)} %pad_add_fusion.5.at_ref, bf16[2048,768]{1,0:T(8,128)(2,1)} %get-tuple-element.140.dk_ref, bf16[2048,768]{1,0:T(8,128)(2,1)} %get-tuple-element.141.dv_ref, bf16[768,2304]{1,0:T(8,128)(2,1)} %w_ref.3, bf16[512,768]{1,0:T(8,128)(2,1)} %get-tuple-element.139.dq_ref.refs_0_, ...), custom_call_target="tpu_custom_call" | custom-call | flops 2415919104 | bytes 6291456 | tf_op jit(solution)/shard_map/input_grad/pallas_call | solution.py:604
  242.1 5.0 %collective-permute-done.11.refs_0_ = bf16[192,768]{1,0:T(8,128)(2,1)S(1)} collective-permute-done((bf16[192,768]{1,0:T(8,128)(2,1)S(1)}, bf16[192,768]{1,0:T(8,128)(2,1)S(1)}, u32[]{:S(2)}, u32[]{:S(2)}) %collective-permute-start.11) | collective-permute-done | bytes 294944 | tf_op jit(solution)/shard_map/ppermute | solution.py:38
  255.1 14.8 %collective-permute-done.13.refs_0_ = bf16[192,768]{1,0:T(8,128)(2,1)S(1)} collective-permute-done((bf16[192,768]{1,0:T(8,128)(2,1)}, bf16[192,768]{1,0:T(8,128)(2,1)S(1)}, u32[]{:S(2)}, u32[]{:S(2)}) %collective-permute-start.13) | collective-permute-done | bytes 294944 | tf_op jit(solution)/shard_map/ppermute | solution.py:38
  276.2 10.1 %collective-permute-done.16.refs_0_ = bf16[416,768]{1,0:T(8,128)(2,1)S(1)} collective-permute-done((bf16[416,768]{1,0:T(8,128)(2,1)}, bf16[416,768]{1,0:T(8,128)(2,1)S(1)}, u32[]{:S(2)}, u32[]{:S(2)}) %collective-permute-start.16) | collective-permute-done | bytes 639008 | tf_op jit(solution)/shard_map/ppermute | solution.py:38
  300.2 7.5 %collective-permute-done.19.refs_2_ = bf16[128,768]{1,0:T(8,128)(2,1)S(1)} collective-permute-done((bf16[128,768]{1,0:T(8,128)(2,1)}, bf16[128,768]{1,0:T(8,128)(2,1)S(1)}, u32[]{:S(2)}, u32[]{:S(2)}) %collective-permute-start.19) | collective-permute-done | bytes 196640 | tf_op jit(solution)/shard_map/ppermute | solution.py:38
  309.5 3.2 collective-permute-done.17.refs_0_
  321.3 13.4 %collective-permute-done.20.refs_0_ = bf16[208,768]{1,0:T(8,128)(2,1)S(1)} collective-permute-done((bf16[208,768]{1,0:T(8,128)(2,1)}, bf16[208,768]{1,0:T(8,128)(2,1)S(1)}, u32[]{:S(2)}, u32[]{:S(2)}) %collective-permute-start.20) | collective-permute-done | bytes 319520 | tf_op jit(solution)/shard_map/ppermute | solution.py:38
  336.6 9.1 %collective-permute-done.21.refs_0_ = bf16[208,768]{1,0:T(8,128)(2,1)S(1)} collective-permute-done((bf16[208,768]{1,0:T(8,128)(2,1)S(1)}, bf16[208,768]{1,0:T(8,128)(2,1)S(1)}, u32[]{:S(2)}, u32[]{:S(2)}) %collective-permute-start.21) | collective-permute-done | bytes 319520 | tf_op jit(solution)/shard_map/ppermute | solution.py:38
  357.5 9.3 %collective-permute-done.24.refs_1_ = bf16[128,768]{1,0:T(8,128)(2,1)S(1)} collective-permute-done((bf16[128,768]{1,0:T(8,128)(2,1)S(1)}, bf16[128,768]{1,0:T(8,128)(2,1)S(1)}, u32[]{:S(2)}, u32[]{:S(2)}) %collective-permute-start.24) | collective-permute-done | bytes 196640 | tf_op jit(solution)/shard_map/ppermute | solution.py:38
  371.5 11.3 %place_ffn.1 = (f32[3072,768]{1,0:T(8,128)}, f32[768,3072]{1,0:T(8,128)}) custom-call(s32[3]{0:T(128)} %pad_add_fusion.6.at_ref, bf16[1536,768]{1,0:T(8,128)(2,1)} %get-tuple-element.162.refs_1_.refs_0_, bf16[1536,768]{1,0:T(8,128)(2,1)} %together.50.refs_2_.refs_1_, bf16[1536,768]{1,0:T(8,128)(2,1)} %collective-permute-done.27.refs_2_, ...), custom_call_target="tpu_custom_call" | custom-call | bytes 37748736 | tf_op jit(solution)/shard_map/place_ffn/pallas_call | solution.py:872
  382.8 8.5 %collective-permute-done.26.refs_1_ = bf16[256,768]{1,0:T(8,128)(2,1)S(1)} collective-permute-done((bf16[256,768]{1,0:T(8,128)(2,1)}, bf16[256,768]{1,0:T(8,128)(2,1)S(1)}, u32[]{:S(2)}, u32[]{:S(2)}) %collective-permute-start.26) | collective-permute-done | bytes 393248 | tf_op jit(solution)/shard_map/ppermute | solution.py:38
  397.7 8.7 %place_attn.1 = (f32[768,2304]{1,0:T(8,128)}, f32[768,768]{1,0:T(8,128)}, f32[128,768]{1,0:T(8,128)}, f32[512,768]{1,0:T(8,128)}) custom-call(s32[3]{0:T(128)} %pad_add_fusion.4.at_ref, bf16[832,768]{1,0:T(8,128)(2,1)} %get-tuple-element.169.refs_1_.mine, bf16[832,768]{1,0:T(8,128)(2,1)} %get-tuple-element.172.refs_2_.mine_came, ...), custom_call_target="tpu_custom_call" | custom-call | bytes 14155776 | tf_op jit(solution)/shard_map/place_attn/pallas_call | solution.py:941
  (218 shorter events, 95.4 us)
Async XLA Ops:
  2.6 21.2 %collective-permute-start = (bf16[528,768]{1,0:T(8,128)(2,1)S(1)}, bf16[528,768]{1,0:T(8,128)(2,1)S(1)}, u32[]{:S(2)}, u32[]{:S(2)}) collective-permute-start(bf16[528,768]{1,0:T(8,128)(2,1)S(1)} %fusion.1.refs_0_), channel_id=1, source_target_pairs={{0,1},{1,0},{2,3},{3,2},{4,5},{5,4},{6,7},{7,6},{8,9},{9,8},{10,11... | collective-permute-start | bytes 2433032 | tf_op jit(solution)/shard_map/ppermute | solution.py:170
  5.7 18.1 %collective-permute-start.1 = (bf16[528,768]{1,0:T(8,128)(2,1)S(1)}, bf16[528,768]{1,0:T(8,128)(2,1)S(1)}, u32[]{:S(2)}, u32[]{:S(2)}) collective-permute-start(bf16[528,768]{1,0:T(8,128)(2,1)S(1)} %fusion.1.refs_0_), channel_id=1, source_target_pairs={{1,2},{2,1},{5,6},{6,5},{9,10},{10,9},{13,14},{14,13},{17,18},{18,... | collective-permute-start | bytes 2433032 | tf_op jit(solution)/shard_map/ppermute | solution.py:170
  24.9 21.9 %collective-permute-start.2 = (bf16[528,768]{1,0:T(8,128)(2,1)}, bf16[528,768]{1,0:T(8,128)(2,1)S(1)}, u32[]{:S(2)}, u32[]{:S(2)}) collective-permute-start(bf16[528,768]{1,0:T(8,128)(2,1)} %get-tuple-element.101.refs_1_), channel_id=1, source_target_pairs={{0,1},{1,0},{2,3},{3,2},{4,5},{5,4},{6,7},{7,6},{8,9},{9,8},{10,11... | collective-permute-start | bytes 2433032 | tf_op jit(solution)/shard_map/ppermute | solution.py:170
  29.4 17.4 %collective-permute-start.3 = (bf16[528,768]{1,0:T(8,128)(2,1)}, bf16[528,768]{1,0:T(8,128)(2,1)S(1)}, u32[]{:S(2)}, u32[]{:S(2)}) collective-permute-start(bf16[528,768]{1,0:T(8,128)(2,1)} %get-tuple-element.102.refs_0_), channel_id=1, source_target_pairs={{1,2},{2,1},{5,6},{6,5},{9,10},{10,9},{13,14},{14,13},{17,18},{18,... | collective-permute-start | bytes 2433032 | tf_op jit(solution)/shard_map/ppermute | solution.py:170
  30.7 21.5 %copy-start.50 = (f32[768]{0:T(1024)S(1)}, f32[768]{0:T(1024)}, u32[]{:S(2)}) copy-start(f32[768]{0:T(1024)} %param.30) | copy-start | bytes 9220
  47.9 19.8 %collective-permute-start.4 = (bf16[528,768]{1,0:T(8,128)(2,1)}, bf16[528,768]{1,0:T(8,128)(2,1)S(1)}, u32[]{:S(2)}, u32[]{:S(2)}) collective-permute-start(bf16[528,768]{1,0:T(8,128)(2,1)} %get-tuple-element.106.refs_1_), channel_id=1, source_target_pairs={{0,1},{1,0},{2,3},{3,2},{4,5},{5,4},{6,7},{7,6},{8,9},{9,8},{10,11... | collective-permute-start | bytes 2433032 | tf_op jit(solution)/shard_map/ppermute | solution.py:170
  51.3 16.5 %collective-permute-start.5 = (bf16[528,768]{1,0:T(8,128)(2,1)}, bf16[528,768]{1,0:T(8,128)(2,1)S(1)}, u32[]{:S(2)}, u32[]{:S(2)}) collective-permute-start(bf16[528,768]{1,0:T(8,128)(2,1)} %get-tuple-element.107.refs_0_), channel_id=1, source_target_pairs={{1,2},{2,1},{5,6},{6,5},{9,10},{10,9},{13,14},{14,13},{17,18},{18,... | collective-permute-start | bytes 2433032 | tf_op jit(solution)/shard_map/ppermute | solution.py:170
  122.3 12.0 %collective-permute-start.6 = (bf16[3072,768]{1,0:T(8,128)(2,1)}, bf16[3072,768]{1,0:T(8,128)(2,1)}, u32[]{:S(2)}, u32[]{:S(2)}) collective-permute-start(bf16[3072,768]{1,0:T(8,128)(2,1)} %get-tuple-element.120), channel_id=1, source_target_pairs={{0,4},{4,0},{8,12},{12,8},{16,20},{20,16},{24,28},{28,24},{1,5},{5... | collective-permute-start | bytes 14155784 | tf_op jit(solution)/shard_map/ppermute | solution.py:38
  138.7 31.7 %collective-permute-start.7 = (bf16[1536,768]{1,0:T(8,128)(2,1)}, bf16[1536,768]{1,0:T(8,128)(2,1)S(1)}, u32[]{:S(2)}, u32[]{:S(2)}) collective-permute-start(bf16[1536,768]{1,0:T(8,128)(2,1)} %add_convert_fusion.refs_0_), channel_id=1, source_target_pairs={{0,8},{4,20},{8,0},{12,28},{16,24},{20,4},{24,16},{28,12},{1,9},{5... | collective-permute-start | bytes 7077896 | tf_op jit(solution)/shard_map/ppermute | solution.py:38
  175.5 25.9 %collective-permute-start.8 = (bf16[768,768]{1,0:T(8,128)(2,1)}, bf16[768,768]{1,0:T(8,128)(2,1)S(1)}, u32[]{:S(2)}, u32[]{:S(2)}) collective-permute-start(bf16[768,768]{1,0:T(8,128)(2,1)} %get-tuple-element.133.refs_4_), channel_id=1, source_target_pairs={{0,16},{4,12},{8,24},{12,4},{16,0},{20,28},{24,8},{28,20},{1,17},{... | collective-permute-start | bytes 3538952 | tf_op jit(solution)/shard_map/ppermute | solution.py:38
  177.1 39.9 %collective-permute-start.10 = (bf16[2,512,768]{2,1,0:T(8,128)(2,1)}, bf16[2,512,768]{2,1,0:T(8,128)(2,1)S(1)}, u32[]{:S(2)}, u32[]{:S(2)}) collective-permute-start(bf16[2,512,768]{2,1,0:T(8,128)(2,1)} %get-tuple-element.136.refs_5_), channel_id=1, source_target_pairs={{0,1},{1,0},{2,3},{3,2},{4,5},{5,4},{6,7},{7,6},{8,9},{9,8},{10,11... | collective-permute-start | bytes 4718600 | tf_op jit(solution)/shard_map/ppermute | solution.py:38
  204.6 21.5 %collective-permute-start.9 = (bf16[384,768]{1,0:T(8,128)(2,1)S(1)}, bf16[384,768]{1,0:T(8,128)(2,1)S(1)}, u32[]{:S(2)}, u32[]{:S(2)}) collective-permute-start(bf16[384,768]{1,0:T(8,128)(2,1)S(1)} %add_convert_fusion.4.refs_0_), channel_id=1, source_target_pairs={{0,1},{1,0},{2,3},{3,2},{4,5},{5,4},{6,7},{7,6},{8,9},{9,8},{10,11... | collective-permute-start | bytes 1769480 | tf_op jit(solution)/shard_map/ppermute | solution.py:38
  230.5 19.7 %collective-permute-start.12 = (bf16[1664,768]{1,0:T(8,128)(2,1)}, bf16[1664,768]{1,0:T(8,128)(2,1)}, u32[]{:S(2)}, u32[]{:S(2)}) collective-permute-start(bf16[1664,768]{1,0:T(8,128)(2,1)} %together.37), channel_id=1, source_target_pairs={{0,4},{4,0},{8,12},{12,8},{16,20},{20,16},{24,28},{28,24},{1,5},{5... | collective-permute-start | bytes 7667720 | tf_op jit(solution)/shard_map/ppermute | solution.py:38
  231.4 15.7 %collective-permute-start.11 = (bf16[192,768]{1,0:T(8,128)(2,1)S(1)}, bf16[192,768]{1,0:T(8,128)(2,1)S(1)}, u32[]{:S(2)}, u32[]{:S(2)}) collective-permute-start(bf16[192,768]{1,0:T(8,128)(2,1)S(1)} %copy-done.27), channel_id=1, source_target_pairs={{0,2},{1,3},{2,0},{3,1},{4,6},{5,7},{6,4},{7,5},{8,10},{9,11},{10,... | collective-permute-start | bytes 884744 | tf_op jit(solution)/shard_map/ppermute | solution.py:38
  254.5 17.6 %collective-permute-start.14 = (bf16[832,768]{1,0:T(8,128)(2,1)}, bf16[832,768]{1,0:T(8,128)(2,1)}, u32[]{:S(2)}, u32[]{:S(2)}) collective-permute-start(bf16[832,768]{1,0:T(8,128)(2,1)} %get-tuple-element.149.refs_3_), channel_id=1, source_target_pairs={{0,8},{4,20},{8,0},{12,28},{16,24},{20,4},{24,16},{28,12},{1,9},{5... | collective-permute-start | bytes 3833864 | tf_op jit(solution)/shard_map/ppermute | solution.py:38
  255.1 14.8 %collective-permute-start.13 = (bf16[192,768]{1,0:T(8,128)(2,1)}, bf16[192,768]{1,0:T(8,128)(2,1)S(1)}, u32[]{:S(2)}, u32[]{:S(2)}) collective-permute-start(bf16[192,768]{1,0:T(8,128)(2,1)} %get-tuple-element.148.refs_2_), channel_id=1, source_target_pairs={{0,2},{1,3},{2,0},{3,1},{4,6},{5,7},{6,4},{7,5},{8,10},{9,11},{10,... | collective-permute-start | bytes 884744 | tf_op jit(solution)/shard_map/ppermute | solution.py:38
  275.7 10.6 %collective-permute-start.16 = (bf16[416,768]{1,0:T(8,128)(2,1)}, bf16[416,768]{1,0:T(8,128)(2,1)S(1)}, u32[]{:S(2)}, u32[]{:S(2)}) collective-permute-start(bf16[416,768]{1,0:T(8,128)(2,1)} %get-tuple-element.154.refs_2_), channel_id=1, source_target_pairs={{0,16},{4,12},{8,24},{12,4},{16,0},{20,28},{24,8},{28,20},{1,17},{... | collective-permute-start | bytes 1916936 | tf_op jit(solution)/shard_map/ppermute | solution.py:38
  276.2 13.9 %collective-permute-start.15 = (bf16[384,768]{1,0:T(8,128)(2,1)}, bf16[384,768]{1,0:T(8,128)(2,1)}, u32[]{:S(2)}, u32[]{:S(2)}) collective-permute-start(bf16[384,768]{1,0:T(8,128)(2,1)} %get-tuple-element.152.refs_1_), channel_id=1, source_target_pairs={{0,1},{1,0},{2,3},{3,2},{4,5},{5,4},{6,7},{7,6},{8,9},{9,8},{10,11... | collective-permute-start | bytes 1769480 | tf_op jit(solution)/shard_map/ppermute | solution.py:38
  296.3 16.5 %collective-permute-start.17 = (bf16[768,768]{1,0:T(8,128)(2,1)}, bf16[768,768]{1,0:T(8,128)(2,1)S(1)}, u32[]{:S(2)}, u32[]{:S(2)}) collective-permute-start(bf16[768,768]{1,0:T(8,128)(2,1)} %get-tuple-element.157.refs_3_), channel_id=1, source_target_pairs={{0,16},{4,12},{8,24},{12,4},{16,0},{20,28},{24,8},{28,20},{1,17},{... | collective-permute-start | bytes 3538952 | tf_op jit(solution)/shard_map/ppermute | solution.py:38
  297.8 11.7 %collective-permute-start.18 = (bf16[208,768]{1,0:T(8,128)(2,1)S(1)}, bf16[208,768]{1,0:T(8,128)(2,1)S(1)}, u32[]{:S(2)}, u32[]{:S(2)}) collective-permute-start(bf16[208,768]{1,0:T(8,128)(2,1)S(1)} %copy-done.34), channel_id=1, source_target_pairs={{0,1},{1,0},{2,3},{3,2},{4,5},{5,4},{6,7},{7,6},{8,9},{9,8},{10,11... | collective-permute-start | bytes 958472 | tf_op jit(solution)/shard_map/ppermute | solution.py:38
  298.1 9.6 %collective-permute-start.19 = (bf16[128,768]{1,0:T(8,128)(2,1)}, bf16[128,768]{1,0:T(8,128)(2,1)S(1)}, u32[]{:S(2)}, u32[]{:S(2)}) collective-permute-start(bf16[128,768]{1,0:T(8,128)(2,1)} %get-tuple-element.158.refs_4_), channel_id=1, source_target_pairs={{0,2},{1,3},{2,0},{3,1},{4,6},{5,7},{6,4},{7,5},{8,10},{9,11},{10,... | collective-permute-start | bytes 589832 | tf_op jit(solution)/shard_map/ppermute | solution.py:38
  319.0 29.1 %collective-permute-start.22 = (bf16[1536,768]{1,0:T(8,128)(2,1)}, bf16[1536,768]{1,0:T(8,128)(2,1)S(1)}, u32[]{:S(2)}, u32[]{:S(2)}) collective-permute-start(bf16[1536,768]{1,0:T(8,128)(2,1)} %get-tuple-element.162.refs_1_.refs_0_), channel_id=1, source_target_pairs={{0,8},{4,20},{8,0},{12,28},{16,24},{20,4},{24,16},{28,12},{1,9},{5... | collective-permute-start | bytes 7077896 | tf_op jit(solution)/shard_map/ppermute | solution.py:38
  320.5 14.2 %collective-permute-start.20 = (bf16[208,768]{1,0:T(8,128)(2,1)}, bf16[208,768]{1,0:T(8,128)(2,1)S(1)}, u32[]{:S(2)}, u32[]{:S(2)}) collective-permute-start(bf16[208,768]{1,0:T(8,128)(2,1)} %get-tuple-element.161.refs_2_), channel_id=1, source_target_pairs={{0,2},{1,3},{2,0},{3,1},{4,6},{5,7},{6,4},{7,5},{8,10},{9,11},{10,... | collective-permute-start | bytes 958472 | tf_op jit(solution)/shard_map/ppermute | solution.py:38
  336.5 9.1 %collective-permute-start.21 = (bf16[208,768]{1,0:T(8,128)(2,1)S(1)}, bf16[208,768]{1,0:T(8,128)(2,1)S(1)}, u32[]{:S(2)}, u32[]{:S(2)}) collective-permute-start(bf16[208,768]{1,0:T(8,128)(2,1)S(1)} %add_convert_fusion.5.refs_3_), channel_id=1, source_target_pairs={{0,1},{1,0},{2,3},{3,2},{4,5},{5,4},{6,7},{7,6},{8,9},{9,8},{10,11... | collective-permute-start | bytes 958472 | tf_op jit(solution)/shard_map/ppermute | solution.py:38
  351.8 19.6 %collective-permute-start.28 = (bf16[1536,768]{1,0:T(8,128)(2,1)}, bf16[1536,768]{1,0:T(8,128)(2,1)}, u32[]{:S(2)}, u32[]{:S(2)}) collective-permute-start(bf16[1536,768]{1,0:T(8,128)(2,1)} %together.50.refs_2_.refs_1_), channel_id=1, source_target_pairs={{0,4},{4,0},{8,12},{12,8},{16,20},{20,16},{24,28},{28,24},{1,5},{5... | collective-permute-start | bytes 7077896 | tf_op jit(solution)/shard_map/ppermute | solution.py:38
  353.5 18.0 %collective-permute-start.27 = (bf16[1536,768]{1,0:T(8,128)(2,1)S(1)}, bf16[1536,768]{1,0:T(8,128)(2,1)}, u32[]{:S(2)}, u32[]{:S(2)}) collective-permute-start(bf16[1536,768]{1,0:T(8,128)(2,1)S(1)} %copy-done.1), channel_id=1, source_target_pairs={{0,4},{4,0},{8,12},{12,8},{16,20},{20,16},{24,28},{28,24},{1,5},{5... | collective-permute-start | bytes 7077896 | tf_op jit(solution)/shard_map/ppermute | solution.py:38
  353.6 13.2 %collective-permute-start.23 = (bf16[416,768]{1,0:T(8,128)(2,1)S(1)}, bf16[416,768]{1,0:T(8,128)(2,1)}, u32[]{:S(2)}, u32[]{:S(2)}) collective-permute-start(bf16[416,768]{1,0:T(8,128)(2,1)S(1)} %copy-done.7), channel_id=1, source_target_pairs={{0,16},{4,12},{8,24},{12,4},{16,0},{20,28},{24,8},{28,20},{1,17},{... | collective-permute-start | bytes 1916936 | tf_op jit(solution)/shard_map/ppermute | solution.py:38
  355.1 11.7 %collective-permute-start.24 = (bf16[128,768]{1,0:T(8,128)(2,1)S(1)}, bf16[128,768]{1,0:T(8,128)(2,1)S(1)}, u32[]{:S(2)}, u32[]{:S(2)}) collective-permute-start(bf16[128,768]{1,0:T(8,128)(2,1)S(1)} %copy-done.32), channel_id=1, source_target_pairs={{0,2},{1,3},{2,0},{3,1},{4,6},{5,7},{6,4},{7,5},{8,10},{9,11},{10,... | collective-permute-start | bytes 589832 | tf_op jit(solution)/shard_map/ppermute | solution.py:38
  370.3 21.0 %collective-permute-start.25 = (bf16[832,768]{1,0:T(8,128)(2,1)}, bf16[832,768]{1,0:T(8,128)(2,1)}, u32[]{:S(2)}, u32[]{:S(2)}) collective-permute-start(bf16[832,768]{1,0:T(8,128)(2,1)} %get-tuple-element.169.refs_1_.mine), channel_id=1, source_target_pairs={{0,8},{4,20},{8,0},{12,28},{16,24},{20,4},{24,16},{28,12},{1,9},{5... | collective-permute-start | bytes 3833864 | tf_op jit(solution)/shard_map/ppermute | solution.py:38
  370.9 20.4 %collective-permute-start.26 = (bf16[256,768]{1,0:T(8,128)(2,1)}, bf16[256,768]{1,0:T(8,128)(2,1)S(1)}, u32[]{:S(2)}, u32[]{:S(2)}) collective-permute-start(bf16[256,768]{1,0:T(8,128)(2,1)} %get-tuple-element.170.refs_2_), channel_id=1, source_target_pairs={{0,2},{1,3},{2,0},{3,1},{4,6},{5,7},{6,4},{7,5},{8,10},{9,11},{10,... | collective-permute-start | bytes 1179656 | tf_op jit(solution)/shard_map/ppermute | solution.py:38
  392.1 4.6 %collective-permute-start.30 = (bf16[832,768]{1,0:T(8,128)(2,1)}, bf16[832,768]{1,0:T(8,128)(2,1)S(1)}, u32[]{:S(2)}, u32[]{:S(2)}) collective-permute-start(bf16[832,768]{1,0:T(8,128)(2,1)} %get-tuple-element.172.refs_2_.mine_came), channel_id=1, source_target_pairs={{0,4},{4,0},{8,12},{12,8},{16,20},{20,16},{24,28},{28,24},{1,5},{5... | collective-permute-start | bytes 3833864 | tf_op jit(solution)/shard_map/ppermute | solution.py:38
  393.4 4.4 %collective-permute-start.29 = (bf16[832,768]{1,0:T(8,128)(2,1)S(1)}, bf16[832,768]{1,0:T(8,128)(2,1)}, u32[]{:S(2)}, u32[]{:S(2)}) collective-permute-start(bf16[832,768]{1,0:T(8,128)(2,1)S(1)} %copy-done.3), channel_id=1, source_target_pairs={{0,4},{4,0},{8,12},{12,8},{16,20},{20,16},{24,28},{28,24},{1,5},{5... | collective-permute-start | bytes 3833864 | tf_op jit(solution)/shard_map/ppermute | solution.py:38
  (50 other events, 271.3 us)

commit v3 on v2

--- a/solution.py
+++ b/solution.py
@@ -120,8 +120,9 @@
             came, _ = yield sent, (axis, bit)
     rows = sent.shape[1]
     came = []
-    for begin, end in ((0, rows // 4), (rows // 4, rows // 2), (rows // 2, rows)):
-        came.append((yield sent[0, begin:end], stages[-1])[0])
+    for begin, end in ((0, 12), (12, 21), (21, 32)):
+        part = sent[0, begin * rows // 32 : end * rows // 32]
+        came.append((yield part, stages[-1])[0])
     return kept[0], came
 
 

time: 417 us -> 416 us (level)
    unnamed x102 -> x96, local copies, waits for them, and re-layouts: 21.4 us -> 23.1 us
where the time goes in v3:
time: 416 us; the launch traced here: 408 us
  Pallas kernels  179 us (43%)
  waiting for transfers between devices  119 us (29%)
  other arithmetic  45.9 us (11%)
  local copies, waits for them, and re-layouts  33.2 us (8%)
  starting transfers between devices  30 us (7%)
    ppermute x25, waiting for transfers between devices, swap(): lax.ppermute(value, stage[0], [(i, i ^ 1 << bits[i % 2]) for i in range(c...  94.2 us
    pallas_call x2, Pallas kernels, attend_back(): pl.pallas_call(functools.partial(attend_back_kernel, final, scale, pairs,...  45.9 us
    pallas_call x1, Pallas kernels, ffn(): pl.pallas_call(functools.partial(ffn_kernel, chunks), grid_spec=pltpu.Pre...  27.5 us
    pallas_call x4, Pallas kernels, project(): pl.pallas_call(functools.partial(project_kernel, first, rows), grid_spec=...  27.2 us
    ppermute x3, waiting for transfers between devices, line_steps(): lax.ppermute(two, 'seq', pairs[0])  24.5 us
    unnamed x96, local copies, waits for them, and re-layouts  23.1 us
    convert_element_type x7, other arithmetic, part_of(): return total.astype(BF)  20.2 us
    pallas_call x1, Pallas kernels, attend(): pl.pallas_call(functools.partial(attend_kernel, scale, 256), grid=(pairs,...  19.3 us
  transfers between devices with their start and end apart: 31, of which 17 were waited for; matrix products, arithmetic and copies ran while one was open for 5% of the time, Pallas kernels for 29%

profile of v3, /device:TPU:0, one launch (start us, length us, event | category | flops | bytes accessed | tf_op | source)
XLA Modules:
  0.0 408.5 jit_solution(17230937299545208501)
XLA Ops:
  2.6 3.1 collective-permute-start
  8.3 7.4 %project.4 = (bf16[2048,768]{1,0:T(8,128)(2,1)}, bf16[2048,1664]{1,0:T(8,128)(2,1)}, bf16[512,768]{1,0:T(8,128)(2,1)}, bf16[512,128]{1,0:T(8,128)(2,1)}, f32[8,128]{1,0:T(8,128)}) custom-call(s32[4]{0:T(128)} %pad_add_fusion.place_ref, bf16[528,768]{1,0:T(8,128)(2,1)} %copy-done.17, bf16[768,2304]{1,0:T(8,128)(2,1)} %w_ref.3, bf16[768,2304]{1,0:T(8,128)(2,1)} %w_ref.3, ...), custom_call_target="tpu_custom_call" | custom-call | flops 603979776 | bytes 3145728 | tf_op jit(solution)/shard_map/project/pallas_call | solution.py:300
  15.7 8.0 %collective-permute-done.refs_0_ = bf16[528,768]{1,0:T(8,128)(2,1)S(1)} collective-permute-done((bf16[528,768]{1,0:T(8,128)(2,1)S(1)}, bf16[528,768]{1,0:T(8,128)(2,1)S(1)}, u32[]{:S(2)}, u32[]{:S(2)}) %collective-permute-start) | collective-permute-done | bytes 811040 | tf_op jit(solution)/shard_map/ppermute | solution.py:171
  24.9 4.5 %collective-permute-start.2 = (bf16[528,768]{1,0:T(8,128)(2,1)}, bf16[528,768]{1,0:T(8,128)(2,1)S(1)}, u32[]{:S(2)}, u32[]{:S(2)}) collective-permute-start(bf16[528,768]{1,0:T(8,128)(2,1)} %get-tuple-element.101.refs_1_), channel_id=1, source_target_pairs={{0,1},{1,0},{2,3},{3,2},{4,5},{5,4},{6,7},{7,6},{8,9},{9,8},{10,11... | collective-permute-start | bytes 2433032 | tf_op jit(solution)/shard_map/ppermute | solution.py:171
  30.7 6.7 %project.5 = (bf16[2048,768]{1,0:T(8,128)(2,1)}, bf16[2048,1664]{1,0:T(8,128)(2,1)}, f32[8,128]{1,0:T(8,128)}) custom-call(s32[4]{0:T(128)} %pad_add_fusion.2.place_ref, bf16[528,768]{1,0:T(8,128)(2,1)} %get-tuple-element.102.refs_0_, bf16[528,768]{1,0:T(8,128)(2,1)} %get-tuple-element.101.refs_1_, ...), custom_call_target="tpu_custom_call", output_to_operand_aliasing={{0}: (7, {}), {1}: (8, {})} | custom-call | flops 1207959552 | bytes 3145728 | tf_op jit(solution)/shard_map/project/pallas_call | solution.py:300
  37.4 9.3 %collective-permute-done.2.refs_0_ = bf16[528,768]{1,0:T(8,128)(2,1)S(1)} collective-permute-done((bf16[528,768]{1,0:T(8,128)(2,1)}, bf16[528,768]{1,0:T(8,128)(2,1)S(1)}, u32[]{:S(2)}, u32[]{:S(2)}) %collective-permute-start.2) | collective-permute-done | bytes 811040 | tf_op jit(solution)/shard_map/ppermute | solution.py:171
  47.9 3.4 collective-permute-start.4
  54.0 6.6 %project.6 = (bf16[2048,768]{1,0:T(8,128)(2,1)}, bf16[2048,1664]{1,0:T(8,128)(2,1)}, f32[8,128]{1,0:T(8,128)}) custom-call(s32[4]{0:T(128)} %pad_add_fusion.3.place_ref, bf16[528,768]{1,0:T(8,128)(2,1)} %get-tuple-element.107.refs_0_, bf16[528,768]{1,0:T(8,128)(2,1)} %get-tuple-element.106.refs_1_, ...), custom_call_target="tpu_custom_call", output_to_operand_aliasing={{0}: (7, {}), {1}: (8, {})} | custom-call | flops 1207959552 | bytes 3145728 | tf_op jit(solution)/shard_map/project/pallas_call | solution.py:300
  60.6 7.2 %collective-permute-done.4.refs_0_ = bf16[528,768]{1,0:T(8,128)(2,1)S(1)} collective-permute-done((bf16[528,768]{1,0:T(8,128)(2,1)}, bf16[528,768]{1,0:T(8,128)(2,1)S(1)}, u32[]{:S(2)}, u32[]{:S(2)}) %collective-permute-start.4) | collective-permute-done | bytes 811040 | tf_op jit(solution)/shard_map/ppermute | solution.py:171
  68.9 6.6 %project.7 = (bf16[2048,768]{1,0:T(8,128)(2,1)}, bf16[2048,1664]{1,0:T(8,128)(2,1)}, f32[8,128]{1,0:T(8,128)}) custom-call(s32[4]{0:T(128)} %pad_add_fusion.1.place_ref, bf16[528,768]{1,0:T(8,128)(2,1)} %get-tuple-element.111.refs_0_, bf16[528,768]{1,0:T(8,128)(2,1)} %get-tuple-element.112.refs_1_, ...), custom_call_target="tpu_custom_call", output_to_operand_aliasing={{0}: (7, {}), {1}: (8, {})} | custom-call | flops 1207959552 | bytes 3145728 | tf_op jit(solution)/shard_map/project/pallas_call | solution.py:300
  75.5 19.3 %attend.1 = (f32[512,768]{1,0:T(8,128)}, bf16[512,768]{1,0:T(8,128)(2,1)}, f32[6,8,512]{2,1,0:T(8,128)}) custom-call(bf16[512,768]{1,0:T(8,128)(2,1)} %get-tuple-element.99.q_ref, bf16[2048,1664]{1,0:T(8,128)(2,1)} %get-tuple-element.115.k_ref.v_ref.kh_ref, bf16[2048,1664]{1,0:T(8,128)(2,1)} %get-tuple-element.115.k_ref.v_ref.kh_ref, ...), custom_call_target="tpu_custom_call" | custom-call | flops 3221225472 | bytes 12582912 | tf_op jit(solution)/shard_map/attend/pallas_call | solution.py:362
  94.8 27.5 %ffn.1 = (bf16[512,768]{1,0:T(8,128)(2,1)}, bf16[3072,768]{1,0:T(8,128)(2,1)}, bf16[3072,768]{1,0:T(8,128)(2,1)}, f32[512,768]{1,0:T(8,128)}, bf16[512,3072]{1,0...) custom-call(s32[1]{0:T(128)} %bitcast.core_ref, ...), custom_call_target="tpu_custom_call" | custom-call | flops 13287555072 | bytes 28311552 | tf_op jit(solution)/shard_map/ffn/pallas_call | solution.py:737
  122.4 11.9 %norm_one.1 = (f32[512,768]{1,0:T(8,128)}, bf16[512,768]{1,0:T(8,128)(2,1)}, bf16[768,768]{1,0:T(8,128)(2,1)}, f32[24,768]{1,0:T(8,128)}) custom-call(bf16[512,768]{1,0:T(8,128)(2,1)} %get-tuple-element.117.o_ref, f32[512,768]{1,0:T(8,128)} %get-tuple-element.121.dh2_ref, bf16[512,3072]{1,0:T(8,128)(2,1)} %get-tuple-element.122.du_ref, ...), custom_call_target="tpu_custom_call" | custom-call | flops 3623878656 | bytes 4718592 | tf_op jit(solution)/shard_map/norm_one/pallas_call | solution.py:823
  134.3 4.4 %add_convert_fusion.refs_0_ = bf16[1536,768]{1,0:T(8,128)(2,1)} fusion(bf16[3072,768]{1,0:T(8,128)(2,1)} %together.31, s32[]{:T(128)S(6)} %select_n.208, bf16[3072,768]{1,0:T(8,128)(2,1)} %get-tuple-element.119), kind=kLoop, calls=%fused_computation | loop fusion | flops 4718592 | bytes 7077892 | tf_op jit(solution)/shard_map/convert_element_type | solution.py:65
  140.7 22.7 %attend_back.2 = (f32[512,768]{1,0:T(8,128)}, f32[8,768]{1,0:T(8,128)}, bf16[2048,768]{1,0:T(8,128)(2,1)}, bf16[2048,768]{1,0:T(8,128)(2,1)}, f32[8,128]{1,0:T(8,128)}) custom-call(s32[2]{0:T(128)} %pad_add_fusion.5.at_ref, bf16[512,768]{1,0:T(8,128)(2,1)} %get-tuple-element.99.q_ref, bf16[2048,1664]{1,0:T(8,128)(2,1)} %get-tuple-element.115.k_ref.v_ref.kh_ref, ...), custom_call_target="tpu_custom_call" | custom-call | flops 8053063680 | bytes 12582912 | tf_op jit(solution)/shard_map/attend_back/pallas_call | solution.py:476
  163.4 6.9 %input_grad.2.refs_1_ = bf16[2,512,768]{2,1,0:T(8,128)(2,1)} custom-call(s32[2]{0:T(128)} %pad_add_fusion.5.at_ref, bf16[2048,768]{1,0:T(8,128)(2,1)} %get-tuple-element.130.dk_ref.refs_2_, bf16[2048,768]{1,0:T(8,128)(2,1)} %get-tuple-element.131.dv_ref.refs_3_, bf16[768,2304]{1,0:T(8,128)(2,1)} %w_ref.3, f32[8,128]{1,0:T(8,128)} %get-tuple-element.132.refs_0_), custom_call_target="tpu_custom_call" | custom-call | flops 2415919104 | bytes 6291456 | tf_op jit(solution)/shard_map/input_grad/pallas_call | solution.py:605
  171.7 3.7 add_convert_fusion.2.refs_0_
  178.1 23.2 %attend_back.3 = (bf16[512,768]{1,0:T(8,128)(2,1)}, f32[8,768]{1,0:T(8,128)}, bf16[2048,768]{1,0:T(8,128)(2,1)}, bf16[2048,768]{1,0:T(8,128)(2,1)}, f32[8,128]{1,0:T(8,128)}) custom-call(s32[2]{0:T(128)} %pad_add_fusion.5.at_ref, bf16[512,768]{1,0:T(8,128)(2,1)} %get-tuple-element.99.q_ref, ...), custom_call_target="tpu_custom_call", output_to_operand_aliasing={{2}: (11, {}), {3}: (12, {})} | custom-call | flops 8053063680 | bytes 12582912 | tf_op jit(solution)/shard_map/attend_back/pallas_call | solution.py:476
  205.5 11.3 %projection.1 = (bf16[1664,768]{1,0:T(8,128)(2,1)}, bf16[1664,768]{1,0:T(8,128)(2,1)}) custom-call(s32[1]{0:T(128)} %bitcast.core_ref, bf16[512,768]{1,0:T(8,128)(2,1)} %bitcast.36, bf16[2048,768]{1,0:T(8,128)(2,1)} %get-tuple-element.138.whole_ref, bf16[512,768]{1,0:T(8,128)(2,1)} %get-tuple-element.139.dq_ref.refs_0_, ...), custom_call_target="tpu_custom_call" | custom-call | flops 4831838208 | bytes 12582912 | tf_op jit(solution)/shard_map/projection/pallas_call | solution.py:558
  216.8 9.2 %collective-permute-done.9.refs_0_ = bf16[384,768]{1,0:T(8,128)(2,1)S(1)} collective-permute-done((bf16[384,768]{1,0:T(8,128)(2,1)S(1)}, bf16[384,768]{1,0:T(8,128)(2,1)S(1)}, u32[]{:S(2)}, u32[]{:S(2)}) %collective-permute-start.9) | collective-permute-done | bytes 589856 | tf_op jit(solution)/shard_map/ppermute | solution.py:38
  233.0 9.0 %input_grad.3.refs_1_ = f32[2,512,768]{2,1,0:T(8,128)} custom-call(s32[2]{0:T(128)} %pad_add_fusion.5.at_ref, bf16[2048,768]{1,0:T(8,128)(2,1)} %get-tuple-element.140.dk_ref, bf16[2048,768]{1,0:T(8,128)(2,1)} %get-tuple-element.141.dv_ref, bf16[768,2304]{1,0:T(8,128)(2,1)} %w_ref.3, bf16[512,768]{1,0:T(8,128)(2,1)} %get-tuple-element.139.dq_ref.refs_0_, ...), custom_call_target="tpu_custom_call" | custom-call | flops 2415919104 | bytes 6291456 | tf_op jit(solution)/shard_map/input_grad/pallas_call | solution.py:605
  242.0 5.1 %collective-permute-done.11.refs_0_ = bf16[192,768]{1,0:T(8,128)(2,1)S(1)} collective-permute-done((bf16[192,768]{1,0:T(8,128)(2,1)S(1)}, bf16[192,768]{1,0:T(8,128)(2,1)S(1)}, u32[]{:S(2)}, u32[]{:S(2)}) %collective-permute-start.11) | collective-permute-done | bytes 294944 | tf_op jit(solution)/shard_map/ppermute | solution.py:38
  255.0 14.8 %collective-permute-done.13.refs_0_ = bf16[192,768]{1,0:T(8,128)(2,1)S(1)} collective-permute-done((bf16[192,768]{1,0:T(8,128)(2,1)}, bf16[192,768]{1,0:T(8,128)(2,1)S(1)}, u32[]{:S(2)}, u32[]{:S(2)}) %collective-permute-start.13) | collective-permute-done | bytes 294944 | tf_op jit(solution)/shard_map/ppermute | solution.py:38
  276.2 10.1 %collective-permute-done.16.refs_0_ = bf16[416,768]{1,0:T(8,128)(2,1)S(1)} collective-permute-done((bf16[416,768]{1,0:T(8,128)(2,1)}, bf16[416,768]{1,0:T(8,128)(2,1)S(1)}, u32[]{:S(2)}, u32[]{:S(2)}) %collective-permute-start.16) | collective-permute-done | bytes 639008 | tf_op jit(solution)/shard_map/ppermute | solution.py:38
  301.1 12.4 %collective-permute-done.19.refs_2_ = bf16[192,768]{1,0:T(8,128)(2,1)S(1)} collective-permute-done((bf16[192,768]{1,0:T(8,128)(2,1)}, bf16[192,768]{1,0:T(8,128)(2,1)S(1)}, u32[]{:S(2)}, u32[]{:S(2)}) %collective-permute-start.19) | collective-permute-done | bytes 294944 | tf_op jit(solution)/shard_map/ppermute | solution.py:38
  315.3 3.0 maximum_select_fusion.refs_0_
  322.3 14.0 %collective-permute-done.20.refs_0_ = bf16[208,768]{1,0:T(8,128)(2,1)} collective-permute-done((bf16[208,768]{1,0:T(8,128)(2,1)}, bf16[208,768]{1,0:T(8,128)(2,1)}, u32[]{:S(2)}, u32[]{:S(2)}) %collective-permute-start.20) | collective-permute-done | bytes 319520 | tf_op jit(solution)/shard_map/ppermute | solution.py:38
  338.2 8.0 %collective-permute-done.21.refs_0_ = bf16[208,768]{1,0:T(8,128)(2,1)S(1)} collective-permute-done((bf16[208,768]{1,0:T(8,128)(2,1)S(1)}, bf16[208,768]{1,0:T(8,128)(2,1)S(1)}, u32[]{:S(2)}, u32[]{:S(2)}) %collective-permute-start.21) | collective-permute-done | bytes 319520 | tf_op jit(solution)/shard_map/ppermute | solution.py:38
  346.3 3.4 collective-permute-done.22.refs_2_
  359.9 9.9 %collective-permute-done.24.refs_1_ = bf16[144,768]{1,0:T(8,128)(2,1)S(1)} collective-permute-done((bf16[144,768]{1,0:T(8,128)(2,1)S(1)}, bf16[144,768]{1,0:T(8,128)(2,1)S(1)}, u32[]{:S(2)}, u32[]{:S(2)}) %collective-permute-start.24) | collective-permute-done | bytes 221216 | tf_op jit(solution)/shard_map/ppermute | solution.py:38
  375.1 11.3 %place_ffn.1 = (f32[3072,768]{1,0:T(8,128)}, f32[768,3072]{1,0:T(8,128)}) custom-call(s32[3]{0:T(128)} %pad_add_fusion.6.at_ref, bf16[1536,768]{1,0:T(8,128)(2,1)} %get-tuple-element.162.refs_1_.refs_0_, bf16[1536,768]{1,0:T(8,128)(2,1)} %together.50.refs_2_.refs_1_, bf16[1536,768]{1,0:T(8,128)(2,1)} %collective-permute-done.27.refs_2_, ...), custom_call_target="tpu_custom_call" | custom-call | bytes 37748736 | tf_op jit(solution)/shard_map/place_ffn/pallas_call | solution.py:873
  396.4 8.7 %place_attn.1 = (f32[768,2304]{1,0:T(8,128)}, f32[768,768]{1,0:T(8,128)}, f32[128,768]{1,0:T(8,128)}, f32[512,768]{1,0:T(8,128)}) custom-call(s32[3]{0:T(128)} %pad_add_fusion.4.at_ref, bf16[832,768]{1,0:T(8,128)(2,1)} %get-tuple-element.169.refs_1_.mine, bf16[832,768]{1,0:T(8,128)(2,1)} %get-tuple-element.172.refs_2_.mine_came, ...), custom_call_target="tpu_custom_call" | custom-call | bytes 14155776 | tf_op jit(solution)/shard_map/place_attn/pallas_call | solution.py:942
  (213 shorter events, 94.3 us)
Async XLA Ops:
  2.6 21.2 %collective-permute-start = (bf16[528,768]{1,0:T(8,128)(2,1)S(1)}, bf16[528,768]{1,0:T(8,128)(2,1)S(1)}, u32[]{:S(2)}, u32[]{:S(2)}) collective-permute-start(bf16[528,768]{1,0:T(8,128)(2,1)S(1)} %fusion.1.refs_0_), channel_id=1, source_target_pairs={{0,1},{1,0},{2,3},{3,2},{4,5},{5,4},{6,7},{7,6},{8,9},{9,8},{10,11... | collective-permute-start | bytes 2433032 | tf_op jit(solution)/shard_map/ppermute | solution.py:171
  5.7 18.1 %collective-permute-start.1 = (bf16[528,768]{1,0:T(8,128)(2,1)S(1)}, bf16[528,768]{1,0:T(8,128)(2,1)S(1)}, u32[]{:S(2)}, u32[]{:S(2)}) collective-permute-start(bf16[528,768]{1,0:T(8,128)(2,1)S(1)} %fusion.1.refs_0_), channel_id=1, source_target_pairs={{1,2},{2,1},{5,6},{6,5},{9,10},{10,9},{13,14},{14,13},{17,18},{18,... | collective-permute-start | bytes 2433032 | tf_op jit(solution)/shard_map/ppermute | solution.py:171
  24.9 21.9 %collective-permute-start.2 = (bf16[528,768]{1,0:T(8,128)(2,1)}, bf16[528,768]{1,0:T(8,128)(2,1)S(1)}, u32[]{:S(2)}, u32[]{:S(2)}) collective-permute-start(bf16[528,768]{1,0:T(8,128)(2,1)} %get-tuple-element.101.refs_1_), channel_id=1, source_target_pairs={{0,1},{1,0},{2,3},{3,2},{4,5},{5,4},{6,7},{7,6},{8,9},{9,8},{10,11... | collective-permute-start | bytes 2433032 | tf_op jit(solution)/shard_map/ppermute | solution.py:171
  29.4 17.4 %collective-permute-start.3 = (bf16[528,768]{1,0:T(8,128)(2,1)}, bf16[528,768]{1,0:T(8,128)(2,1)S(1)}, u32[]{:S(2)}, u32[]{:S(2)}) collective-permute-start(bf16[528,768]{1,0:T(8,128)(2,1)} %get-tuple-element.102.refs_0_), channel_id=1, source_target_pairs={{1,2},{2,1},{5,6},{6,5},{9,10},{10,9},{13,14},{14,13},{17,18},{18,... | collective-permute-start | bytes 2433032 | tf_op jit(solution)/shard_map/ppermute | solution.py:171
  47.9 19.8 %collective-permute-start.4 = (bf16[528,768]{1,0:T(8,128)(2,1)}, bf16[528,768]{1,0:T(8,128)(2,1)S(1)}, u32[]{:S(2)}, u32[]{:S(2)}) collective-permute-start(bf16[528,768]{1,0:T(8,128)(2,1)} %get-tuple-element.106.refs_1_), channel_id=1, source_target_pairs={{0,1},{1,0},{2,3},{3,2},{4,5},{5,4},{6,7},{7,6},{8,9},{9,8},{10,11... | collective-permute-start | bytes 2433032 | tf_op jit(solution)/shard_map/ppermute | solution.py:171
  51.3 16.5 %collective-permute-start.5 = (bf16[528,768]{1,0:T(8,128)(2,1)}, bf16[528,768]{1,0:T(8,128)(2,1)S(1)}, u32[]{:S(2)}, u32[]{:S(2)}) collective-permute-start(bf16[528,768]{1,0:T(8,128)(2,1)} %get-tuple-element.107.refs_0_), channel_id=1, source_target_pairs={{1,2},{2,1},{5,6},{6,5},{9,10},{10,9},{13,14},{14,13},{17,18},{18,... | collective-permute-start | bytes 2433032 | tf_op jit(solution)/shard_map/ppermute | solution.py:171
  122.3 12.0 %collective-permute-start.6 = (bf16[3072,768]{1,0:T(8,128)(2,1)}, bf16[3072,768]{1,0:T(8,128)(2,1)}, u32[]{:S(2)}, u32[]{:S(2)}) collective-permute-start(bf16[3072,768]{1,0:T(8,128)(2,1)} %get-tuple-element.120), channel_id=1, source_target_pairs={{0,4},{4,0},{8,12},{12,8},{16,20},{20,16},{24,28},{28,24},{1,5},{5... | collective-permute-start | bytes 14155784 | tf_op jit(solution)/shard_map/ppermute | solution.py:38
  138.6 31.7 %collective-permute-start.7 = (bf16[1536,768]{1,0:T(8,128)(2,1)}, bf16[1536,768]{1,0:T(8,128)(2,1)S(1)}, u32[]{:S(2)}, u32[]{:S(2)}) collective-permute-start(bf16[1536,768]{1,0:T(8,128)(2,1)} %add_convert_fusion.refs_0_), channel_id=1, source_target_pairs={{0,8},{4,20},{8,0},{12,28},{16,24},{20,4},{24,16},{28,12},{1,9},{5... | collective-permute-start | bytes 7077896 | tf_op jit(solution)/shard_map/ppermute | solution.py:38
  175.5 25.8 %collective-permute-start.8 = (bf16[768,768]{1,0:T(8,128)(2,1)}, bf16[768,768]{1,0:T(8,128)(2,1)S(1)}, u32[]{:S(2)}, u32[]{:S(2)}) collective-permute-start(bf16[768,768]{1,0:T(8,128)(2,1)} %get-tuple-element.133.refs_4_), channel_id=1, source_target_pairs={{0,16},{4,12},{8,24},{12,4},{16,0},{20,28},{24,8},{28,20},{1,17},{... | collective-permute-start | bytes 3538952 | tf_op jit(solution)/shard_map/ppermute | solution.py:38
  177.0 39.8 %collective-permute-start.10 = (bf16[2,512,768]{2,1,0:T(8,128)(2,1)}, bf16[2,512,768]{2,1,0:T(8,128)(2,1)S(1)}, u32[]{:S(2)}, u32[]{:S(2)}) collective-permute-start(bf16[2,512,768]{2,1,0:T(8,128)(2,1)} %get-tuple-element.136.refs_5_), channel_id=1, source_target_pairs={{0,1},{1,0},{2,3},{3,2},{4,5},{5,4},{6,7},{7,6},{8,9},{9,8},{10,11... | collective-permute-start | bytes 4718600 | tf_op jit(solution)/shard_map/ppermute | solution.py:38
  204.5 21.5 %collective-permute-start.9 = (bf16[384,768]{1,0:T(8,128)(2,1)S(1)}, bf16[384,768]{1,0:T(8,128)(2,1)S(1)}, u32[]{:S(2)}, u32[]{:S(2)}) collective-permute-start(bf16[384,768]{1,0:T(8,128)(2,1)S(1)} %add_convert_fusion.4.refs_0_), channel_id=1, source_target_pairs={{0,1},{1,0},{2,3},{3,2},{4,5},{5,4},{6,7},{7,6},{8,9},{9,8},{10,11... | collective-permute-start | bytes 1769480 | tf_op jit(solution)/shard_map/ppermute | solution.py:38
  230.4 19.7 %collective-permute-start.12 = (bf16[1664,768]{1,0:T(8,128)(2,1)}, bf16[1664,768]{1,0:T(8,128)(2,1)}, u32[]{:S(2)}, u32[]{:S(2)}) collective-permute-start(bf16[1664,768]{1,0:T(8,128)(2,1)} %together.37), channel_id=1, source_target_pairs={{0,4},{4,0},{8,12},{12,8},{16,20},{20,16},{24,28},{28,24},{1,5},{5... | collective-permute-start | bytes 7667720 | tf_op jit(solution)/shard_map/ppermute | solution.py:38
  231.4 15.7 %collective-permute-start.11 = (bf16[192,768]{1,0:T(8,128)(2,1)S(1)}, bf16[192,768]{1,0:T(8,128)(2,1)S(1)}, u32[]{:S(2)}, u32[]{:S(2)}) collective-permute-start(bf16[192,768]{1,0:T(8,128)(2,1)S(1)} %copy-done.28), channel_id=1, source_target_pairs={{0,2},{1,3},{2,0},{3,1},{4,6},{5,7},{6,4},{7,5},{8,10},{9,11},{10,... | collective-permute-start | bytes 884744 | tf_op jit(solution)/shard_map/ppermute | solution.py:38
  254.5 17.6 %collective-permute-start.14 = (bf16[832,768]{1,0:T(8,128)(2,1)}, bf16[832,768]{1,0:T(8,128)(2,1)}, u32[]{:S(2)}, u32[]{:S(2)}) collective-permute-start(bf16[832,768]{1,0:T(8,128)(2,1)} %get-tuple-element.149.refs_3_), channel_id=1, source_target_pairs={{0,8},{4,20},{8,0},{12,28},{16,24},{20,4},{24,16},{28,12},{1,9},{5... | collective-permute-start | bytes 3833864 | tf_op jit(solution)/shard_map/ppermute | solution.py:38
  255.0 14.8 %collective-permute-start.13 = (bf16[192,768]{1,0:T(8,128)(2,1)}, bf16[192,768]{1,0:T(8,128)(2,1)S(1)}, u32[]{:S(2)}, u32[]{:S(2)}) collective-permute-start(bf16[192,768]{1,0:T(8,128)(2,1)} %get-tuple-element.148.refs_2_), channel_id=1, source_target_pairs={{0,2},{1,3},{2,0},{3,1},{4,6},{5,7},{6,4},{7,5},{8,10},{9,11},{10,... | collective-permute-start | bytes 884744 | tf_op jit(solution)/shard_map/ppermute | solution.py:38
  275.6 10.6 %collective-permute-start.16 = (bf16[416,768]{1,0:T(8,128)(2,1)}, bf16[416,768]{1,0:T(8,128)(2,1)S(1)}, u32[]{:S(2)}, u32[]{:S(2)}) collective-permute-start(bf16[416,768]{1,0:T(8,128)(2,1)} %get-tuple-element.154.refs_2_), channel_id=1, source_target_pairs={{0,16},{4,12},{8,24},{12,4},{16,0},{20,28},{24,8},{28,20},{1,17},{... | collective-permute-start | bytes 1916936 | tf_op jit(solution)/shard_map/ppermute | solution.py:38
  276.2 13.9 %collective-permute-start.15 = (bf16[384,768]{1,0:T(8,128)(2,1)}, bf16[384,768]{1,0:T(8,128)(2,1)}, u32[]{:S(2)}, u32[]{:S(2)}) collective-permute-start(bf16[384,768]{1,0:T(8,128)(2,1)} %get-tuple-element.152.refs_1_), channel_id=1, source_target_pairs={{0,1},{1,0},{2,3},{3,2},{4,5},{5,4},{6,7},{7,6},{8,9},{9,8},{10,11... | collective-permute-start | bytes 1769480 | tf_op jit(solution)/shard_map/ppermute | solution.py:38
  293.5 44.0 %copy-start.24 = (bf16[1,512,768]{2,1,0:T(8,128)(2,1)}, bf16[1,512,768]{2,1,0:T(8,128)(2,1)S(1)}, u32[]{:S(2)}) copy-start(bf16[1,512,768]{2,1,0:T(8,128)(2,1)S(1)} %dynamic-slice_convert_fusion) | copy-start | bytes 2359300
  297.3 16.4 %collective-permute-start.17 = (bf16[768,768]{1,0:T(8,128)(2,1)}, bf16[768,768]{1,0:T(8,128)(2,1)S(1)}, u32[]{:S(2)}, u32[]{:S(2)}) collective-permute-start(bf16[768,768]{1,0:T(8,128)(2,1)} %get-tuple-element.157.refs_3_), channel_id=1, source_target_pairs={{0,16},{4,12},{8,24},{12,4},{16,0},{20,28},{24,8},{28,20},{1,17},{... | collective-permute-start | bytes 3538952 | tf_op jit(solution)/shard_map/ppermute | solution.py:38
  298.7 14.9 %collective-permute-start.18 = (bf16[208,768]{1,0:T(8,128)(2,1)}, bf16[208,768]{1,0:T(8,128)(2,1)}, u32[]{:S(2)}, u32[]{:S(2)}) collective-permute-start(bf16[208,768]{1,0:T(8,128)(2,1)} %add_convert_fusion.7.refs_2_), channel_id=1, source_target_pairs={{0,1},{1,0},{2,3},{3,2},{4,5},{5,4},{6,7},{7,6},{8,9},{9,8},{10,11... | collective-permute-start | bytes 958472 | tf_op jit(solution)/shard_map/ppermute | solution.py:38
  299.0 14.6 %collective-permute-start.19 = (bf16[192,768]{1,0:T(8,128)(2,1)}, bf16[192,768]{1,0:T(8,128)(2,1)S(1)}, u32[]{:S(2)}, u32[]{:S(2)}) collective-permute-start(bf16[192,768]{1,0:T(8,128)(2,1)} %get-tuple-element.158.refs_4_), channel_id=1, source_target_pairs={{0,2},{1,3},{2,0},{3,1},{4,6},{5,7},{6,4},{7,5},{8,10},{9,11},{10,... | collective-permute-start | bytes 884744 | tf_op jit(solution)/shard_map/ppermute | solution.py:38
  320.6 29.1 %collective-permute-start.22 = (bf16[1536,768]{1,0:T(8,128)(2,1)}, bf16[1536,768]{1,0:T(8,128)(2,1)S(1)}, u32[]{:S(2)}, u32[]{:S(2)}) collective-permute-start(bf16[1536,768]{1,0:T(8,128)(2,1)} %get-tuple-element.162.refs_1_.refs_0_), channel_id=1, source_target_pairs={{0,8},{4,20},{8,0},{12,28},{16,24},{20,4},{24,16},{28,12},{1,9},{5... | collective-permute-start | bytes 7077896 | tf_op jit(solution)/shard_map/ppermute | solution.py:38
  321.6 14.8 %collective-permute-start.20 = (bf16[208,768]{1,0:T(8,128)(2,1)}, bf16[208,768]{1,0:T(8,128)(2,1)}, u32[]{:S(2)}, u32[]{:S(2)}) collective-permute-start(bf16[208,768]{1,0:T(8,128)(2,1)} %get-tuple-element.161.refs_2_), channel_id=1, source_target_pairs={{0,2},{1,3},{2,0},{3,1},{4,6},{5,7},{6,4},{7,5},{8,10},{9,11},{10,... | collective-permute-start | bytes 958472 | tf_op jit(solution)/shard_map/ppermute | solution.py:38
  337.4 8.9 %collective-permute-start.21 = (bf16[208,768]{1,0:T(8,128)(2,1)S(1)}, bf16[208,768]{1,0:T(8,128)(2,1)S(1)}, u32[]{:S(2)}, u32[]{:S(2)}) collective-permute-start(bf16[208,768]{1,0:T(8,128)(2,1)S(1)} %add_convert_fusion.5.refs_3_), channel_id=1, source_target_pairs={{0,1},{1,0},{2,3},{3,2},{4,5},{5,4},{6,7},{7,6},{8,9},{9,8},{10,11... | collective-permute-start | bytes 958472 | tf_op jit(solution)/shard_map/ppermute | solution.py:38
  354.3 20.8 %collective-permute-start.28 = (bf16[1536,768]{1,0:T(8,128)(2,1)}, bf16[1536,768]{1,0:T(8,128)(2,1)}, u32[]{:S(2)}, u32[]{:S(2)}) collective-permute-start(bf16[1536,768]{1,0:T(8,128)(2,1)} %together.50.refs_2_.refs_1_), channel_id=1, source_target_pairs={{0,4},{4,0},{8,12},{12,8},{16,20},{20,16},{24,28},{28,24},{1,5},{5... | collective-permute-start | bytes 7077896 | tf_op jit(solution)/shard_map/ppermute | solution.py:38
  355.9 19.2 %collective-permute-start.27 = (bf16[1536,768]{1,0:T(8,128)(2,1)S(1)}, bf16[1536,768]{1,0:T(8,128)(2,1)}, u32[]{:S(2)}, u32[]{:S(2)}) collective-permute-start(bf16[1536,768]{1,0:T(8,128)(2,1)S(1)} %copy-done.2), channel_id=1, source_target_pairs={{0,4},{4,0},{8,12},{12,8},{16,20},{20,16},{24,28},{28,24},{1,5},{5... | collective-permute-start | bytes 7077896 | tf_op jit(solution)/shard_map/ppermute | solution.py:38
  356.0 13.7 %collective-permute-start.23 = (bf16[416,768]{1,0:T(8,128)(2,1)S(1)}, bf16[416,768]{1,0:T(8,128)(2,1)}, u32[]{:S(2)}, u32[]{:S(2)}) collective-permute-start(bf16[416,768]{1,0:T(8,128)(2,1)S(1)} %copy-done.7), channel_id=1, source_target_pairs={{0,16},{4,12},{8,24},{12,4},{16,0},{20,28},{24,8},{28,20},{1,17},{... | collective-permute-start | bytes 1916936 | tf_op jit(solution)/shard_map/ppermute | solution.py:38
  357.3 12.4 %collective-permute-start.24 = (bf16[144,768]{1,0:T(8,128)(2,1)S(1)}, bf16[144,768]{1,0:T(8,128)(2,1)S(1)}, u32[]{:S(2)}, u32[]{:S(2)}) collective-permute-start(bf16[144,768]{1,0:T(8,128)(2,1)S(1)} %copy-done.34), channel_id=1, source_target_pairs={{0,2},{1,3},{2,0},{3,1},{4,6},{5,7},{6,4},{7,5},{8,10},{9,11},{10,... | collective-permute-start | bytes 663560 | tf_op jit(solution)/shard_map/ppermute | solution.py:38
  373.3 17.6 %collective-permute-start.25 = (bf16[832,768]{1,0:T(8,128)(2,1)}, bf16[832,768]{1,0:T(8,128)(2,1)}, u32[]{:S(2)}, u32[]{:S(2)}) collective-permute-start(bf16[832,768]{1,0:T(8,128)(2,1)} %get-tuple-element.169.refs_1_.mine), channel_id=1, source_target_pairs={{0,8},{4,20},{8,0},{12,28},{16,24},{20,4},{24,16},{28,12},{1,9},{5... | collective-permute-start | bytes 3833864 | tf_op jit(solution)/shard_map/ppermute | solution.py:38
  374.5 14.5 %collective-permute-start.26 = (bf16[176,768]{1,0:T(8,128)(2,1)}, bf16[176,768]{1,0:T(8,128)(2,1)S(1)}, u32[]{:S(2)}, u32[]{:S(2)}) collective-permute-start(bf16[176,768]{1,0:T(8,128)(2,1)} %get-tuple-element.170.refs_2_), channel_id=1, source_target_pairs={{0,2},{1,3},{2,0},{3,1},{4,6},{5,7},{6,4},{7,5},{8,10},{9,11},{10,... | collective-permute-start | bytes 811016 | tf_op jit(solution)/shard_map/ppermute | solution.py:38
  390.8 4.6 %collective-permute-start.30 = (bf16[832,768]{1,0:T(8,128)(2,1)}, bf16[832,768]{1,0:T(8,128)(2,1)S(1)}, u32[]{:S(2)}, u32[]{:S(2)}) collective-permute-start(bf16[832,768]{1,0:T(8,128)(2,1)} %get-tuple-element.172.refs_2_.mine_came), channel_id=1, source_target_pairs={{0,4},{4,0},{8,12},{12,8},{16,20},{20,16},{24,28},{28,24},{1,5},{5... | collective-permute-start | bytes 3833864 | tf_op jit(solution)/shard_map/ppermute | solution.py:38
  392.1 4.3 %collective-permute-start.29 = (bf16[832,768]{1,0:T(8,128)(2,1)S(1)}, bf16[832,768]{1,0:T(8,128)(2,1)}, u32[]{:S(2)}, u32[]{:S(2)}) collective-permute-start(bf16[832,768]{1,0:T(8,128)(2,1)S(1)} %copy-done.3), channel_id=1, source_target_pairs={{0,4},{4,0},{8,12},{12,8},{16,20},{20,16},{24,28},{28,24},{1,5},{5... | collective-permute-start | bytes 3833864 | tf_op jit(solution)/shard_map/ppermute | solution.py:38
  (47 other events, 272.0 us)
